TPU v7x, 32 devices: a whole 2x2x4 slice. The times are simulated.
32 devices in a mesh: canvas: 4 (over y, x), height: 8 (over z, core).
Axes of the slice: x: 2, y: 2, z: 4, core: 2. Of those that a mesh axis runs over, the one named last changes fastest.
Arguments:
- latents: bfloat16 [8, 64, 64, 512], P('canvas', 'height'), may hold values from -13 to 13
- crop_ids: int32 [8, 64, 64], P('canvas', 'height'), may hold values from 0 to 15, as said below
- params: float32 [11264, 512], P(('canvas', 'height')), may hold values from -0.53033009 to 0.53033009
- vectors: float32 [11, 512], replicated, may hold values from -1 to 2
- first_moment: float32 [11264, 512], P(('canvas', 'height')), may hold values from -320 to 320
- second_moment: float32 [11264, 512], P(('canvas', 'height')), may hold values from 1638.4 to 16384
- vector_first: float32 [11, 512], replicated, may hold values from -320 to 320
- vector_second: float32 [11, 512], replicated, may hold values from 1638.4 to 16384
- cotangent: bfloat16 [8, 64, 64, 512], P('canvas', 'height'), may hold values from -6 to 6
Outputs:
- first_hidden: float32 [8, 64, 64, 512], P('canvas', 'height')
- first_output: float32 [8, 64, 64, 512], P('canvas', 'height')
- second_output: float32 [8, 64, 64, 512], P('canvas', 'height')
- input_grad: float32 [8, 64, 64, 512], P('canvas', 'height')
- new_params: float32 [11264, 512], P(('canvas', 'height'))
- new_first: float32 [11264, 512], P(('canvas', 'height'))
- new_second: float32 [11264, 512], P(('canvas', 'height'))
- new_vectors: float32 [11, 512], replicated
- new_vector_first: float32 [11, 512], replicated
- new_vector_second: float32 [11, 512], replicated
Inputs may be any that keep to these rules, and one draw needn't show every extreme that they name: `crop_ids`: in each canvas the pixels of one id form a rectangle whose columns are a run of aligned groups of 8 columns.
All inputs are finite; a program needn't handle non-finite values.
Results may differ from a plain program's by a relative error of at most 0.017.
The roundings to bfloat16 on the way count: a program that leaves them out, or rounds other values in their place, can miss the bound.
Values may be sent and summed in bfloat16 or wider, within the bound.
A program may use at most 256 MiB of HBM per device.

v0:
```python
import jax
import jax.numpy as jnp
from jax import lax
from jax.sharding import PartitionSpec as P

C = 512
GROUPS = 32
STEP = 5
CROPS = 16


norm_epsilon = 1e-06
adam_epsilon = 1e-08
matrix_rate = 0.015
vector_rate = 0.2
mask_fill = -1e30
highest = lax.Precision.HIGHEST


def with_halo(cells, sides, width):
    for axis, dim in sides:
        count = lax.axis_size(axis)
        ends = count - 1
        head = lax.slice_in_dim(cells, 0, width, axis=dim)
        tail = lax.slice_in_dim(cells, cells.shape[dim] - width, cells.shape[dim], axis=dim)
        cells = jnp.concatenate(
            [
                lax.ppermute(tail, axis, [(i, (i + 1) % count) for i in range(ends)]),
                cells,
                lax.ppermute(head, axis, [((i + 1) % count, i) for i in range(ends)]),
            ],
            axis=dim,
        )
    return cells


def build_layout(crop_ids):
    canvas_count, row_count, col_count = crop_ids.shape
    whole_ids = lax.all_gather(crop_ids, "height", axis=1, tiled=True)
    height_total = whole_ids.shape[1]
    padded = jnp.pad(whole_ids, ((0, 0), (1, 1), (1, 1)), constant_values=-1)
    first_row = lax.axis_index("height") * row_count
    beside_all = lax.dynamic_slice_in_dim(padded, first_row, row_count + 2, 1)
    tap_list = []
    for row_step in range(3):
        for col_step in range(3):
            tap_list.append(
                beside_all[:, row_step : row_step + row_count, col_step : col_step + col_count]
                == crop_ids
            )
    tap_masks = jnp.stack(tap_list, axis=-1).astype(jnp.bfloat16)
    crop_range = jnp.arange(CROPS, dtype=jnp.int32)
    onehot = (crop_ids.reshape(canvas_count, row_count * col_count, 1) == crop_range).astype(
        jnp.float32
    )
    counts = jnp.sum(
        (whole_ids.reshape(canvas_count, height_total * col_count, 1) == crop_range).astype(
            jnp.float32
        ),
        axis=1,
    )
    divisor = jnp.maximum(counts * (C // GROUPS), 1.0)
    query_crops = crop_ids.reshape(canvas_count, row_count * col_count)
    key_crops = whole_ids.reshape(canvas_count, height_total * col_count)
    return (tap_masks, onehot, divisor, query_crops, key_crops)


def norm_forward(hidden, norm_gain, norm_bias, layout):
    canvas_count, row_count, col_count, channels = hidden.shape
    onehot, divisor = (layout[1], layout[2])
    grouped = hidden.reshape(canvas_count, row_count * col_count, GROUPS, channels // GROUPS)
    local_sum = jnp.einsum("npc,npgk->ncg", onehot, grouped, precision=highest)
    centre = lax.psum(local_sum, "height") / divisor[:, :, None]
    centre_pix = jnp.einsum("npc,ncg->npg", onehot, centre, precision=highest)
    centered = grouped - centre_pix[..., None]
    local_square = jnp.einsum("npc,npgk->ncg", onehot, centered * centered, precision=highest)
    spread = lax.psum(local_square, "height") / divisor[:, :, None]
    inverse_pix = jnp.einsum(
        "npc,ncg->npg", onehot, lax.rsqrt(spread + norm_epsilon), precision=highest
    )
    normal_form = centered * inverse_pix[..., None]
    output = normal_form.reshape(hidden.shape) * norm_gain + norm_bias
    return (output, (normal_form, inverse_pix))


def norm_backward(grad_output, stored, norm_gain, layout):
    normal_form, inverse_pix = stored
    onehot, divisor = (layout[1], layout[2])
    full_shape = grad_output.shape
    gain_grad = jnp.sum(grad_output * normal_form.reshape(full_shape), axis=(0, 1, 2))
    bias_grad = jnp.sum(grad_output, axis=(0, 1, 2))
    grad_normal = (grad_output * norm_gain).reshape(normal_form.shape)
    local_plain = jnp.einsum("npc,npgk->ncg", onehot, grad_normal, precision=highest)
    local_cross = jnp.einsum("npc,npgk->ncg", onehot, grad_normal * normal_form, precision=highest)
    total_plain, total_cross = lax.psum((local_plain, local_cross), "height")
    plain_pix = jnp.einsum(
        "npc,ncg->npg", onehot, total_plain / divisor[:, :, None], precision=highest
    )
    cross_pix = jnp.einsum(
        "npc,ncg->npg", onehot, total_cross / divisor[:, :, None], precision=highest
    )
    grad_input = inverse_pix[..., None] * (
        grad_normal - plain_pix[..., None] - normal_form * cross_pix[..., None]
    )
    return (grad_input.reshape(full_shape), gain_grad, bias_grad)


def conv_forward(source, weight, conv_bias, tap_masks):
    canvas_count, row_count, col_count, channels = source.shape
    padded = with_halo(source, (("height", 1),), 1)
    padded = jnp.pad(padded, ((0, 0), (0, 0), (1, 1), (0, 0)))
    pieces = []
    for row_step in range(3):
        for col_step in range(3):
            tap_index = 3 * row_step + col_step
            window = padded[:, row_step : row_step + row_count, col_step : col_step + col_count]
            pieces.append(window * tap_masks[..., tap_index, None])
    columns = jnp.stack(pieces, axis=3).reshape(canvas_count * row_count * col_count, 9 * channels)
    output = jnp.dot(columns, weight, preferred_element_type=jnp.float32) + conv_bias
    return (output.reshape(source.shape), columns)


def conv_backward(grad_low, weight, columns, tap_masks):
    canvas_count, row_count, col_count, channels = grad_low.shape
    padded = with_halo(grad_low, (("height", 1),), 1)
    padded = jnp.pad(padded, ((0, 0), (0, 0), (1, 1), (0, 0)))
    pieces = []
    for row_step in range(3):
        for col_step in range(3):
            tap_index = 3 * row_step + col_step
            window = padded[
                :, 2 - row_step : 2 - row_step + row_count, 2 - col_step : 2 - col_step + col_count
            ]
            pieces.append(window * tap_masks[..., 8 - tap_index, None])
    flipped = jnp.stack(pieces, axis=3).reshape(canvas_count * row_count * col_count, 9, channels)
    grad_source = jnp.einsum(
        "pto,tio->pi",
        flipped,
        weight.reshape(9, channels, channels),
        preferred_element_type=jnp.float32,
    )
    grad_flat = grad_low.reshape(-1, channels)
    grad_weight = jnp.einsum("pk,po->ko", columns, grad_flat, preferred_element_type=jnp.float32)
    grad_bias = jnp.sum(grad_flat, axis=0, dtype=jnp.float32)
    return (grad_source.reshape(grad_low.shape), grad_weight, grad_bias)


def masked_scores(queries, keys_all, query_crops, key_crops):
    scores = jnp.einsum(
        "nqc,nkc->nqk", queries, keys_all, preferred_element_type=jnp.float32
    ) * queries.shape[-1] ** (-0.5)
    return jnp.where(query_crops[:, :, None] == key_crops[:, None, :], scores, mask_fill)


def attend_forward(normed, qkv_weight, proj_weight, vectors, layout):
    canvas_count, row_count, col_count, channels = normed.shape
    inputs_low = normed.reshape(canvas_count, row_count * col_count, channels).astype(jnp.bfloat16)
    projected = jnp.einsum(
        "nlc,jcd->jnld", inputs_low, qkv_weight, preferred_element_type=jnp.float32
    )
    queries = (projected[0] + vectors[8]).astype(jnp.bfloat16)
    keys_local = projected[1].astype(jnp.bfloat16)
    values_local = (projected[2] + vectors[9]).astype(jnp.bfloat16)
    keys_all, values_all = (
        lax.all_gather(keys_local, "height", axis=1, tiled=True),
        lax.all_gather(values_local, "height", axis=1, tiled=True),
    )
    scores = masked_scores(queries, keys_all, layout[3], layout[4])
    row_top = jnp.max(scores, axis=-1, keepdims=True)
    exponent = jnp.exp(scores - row_top)
    row_total = jnp.sum(exponent, axis=-1, keepdims=True)
    probabilities = exponent / row_total
    log_total = row_top + jnp.log(row_total)
    attended = jnp.einsum(
        "nqk,nkc->nqc",
        probabilities.astype(jnp.bfloat16),
        values_all,
        preferred_element_type=jnp.float32,
    ).astype(jnp.bfloat16)
    output = (
        jnp.einsum("nlc,cd->nld", attended, proj_weight, preferred_element_type=jnp.float32)
        + vectors[10]
    )
    stored = (
        inputs_low,
        queries,
        keys_local,
        values_local,
        keys_all,
        values_all,
        log_total,
        attended,
    )
    return (output.reshape(normed.shape), stored)


def attend_backward(grad_output, qkv_weight, proj_weight, layout, stored):
    inputs_low, queries, keys_local, values_local, keys_all, values_all, log_total, attended = (
        stored
    )
    canvas_count, row_count, col_count, channels = grad_output.shape
    score_scale = channels ** (-0.5)
    grad_out_low = grad_output.reshape(canvas_count, row_count * col_count, channels).astype(
        jnp.bfloat16
    )
    proj_grad = jnp.einsum(
        "nlc,nld->cd", attended, grad_out_low, preferred_element_type=jnp.float32
    )
    proj_bias_grad = jnp.sum(grad_out_low, axis=(0, 1), dtype=jnp.float32)
    grad_attended = jnp.einsum(
        "nld,cd->nlc", grad_out_low, proj_weight, preferred_element_type=jnp.float32
    ).astype(jnp.bfloat16)
    probabilities = jnp.exp(masked_scores(queries, keys_all, layout[3], layout[4]) - log_total)
    grad_probs = jnp.einsum(
        "nqc,nkc->nqk", grad_attended, values_all, preferred_element_type=jnp.float32
    )
    delta_sum = jnp.sum(probabilities * grad_probs, axis=-1, keepdims=True)
    grad_scores = (probabilities * (grad_probs - delta_sum)).astype(jnp.bfloat16)
    grad_queries = (
        jnp.einsum("nqk,nkc->nqc", grad_scores, keys_all, preferred_element_type=jnp.float32)
        * score_scale
    ).astype(jnp.bfloat16)
    partial_keys = (
        jnp.einsum("nqk,nqc->nkc", grad_scores, queries, preferred_element_type=jnp.float32)
        * score_scale
    )
    partial_values = jnp.einsum(
        "nqk,nqc->nkc",
        probabilities.astype(jnp.bfloat16),
        grad_attended,
        preferred_element_type=jnp.float32,
    )
    grad_keys, grad_values = (
        lax.psum_scatter(
            partial_keys.astype(jnp.bfloat16), "height", scatter_dimension=1, tiled=True
        ).astype(jnp.float32),
        lax.psum_scatter(
            partial_values.astype(jnp.bfloat16), "height", scatter_dimension=1, tiled=True
        ).astype(jnp.float32),
    )
    grad_qkv = jnp.stack(
        [grad_queries, grad_keys.astype(jnp.bfloat16), grad_values.astype(jnp.bfloat16)]
    )
    grad_inputs = jnp.einsum(
        "jnld,jcd->nlc", grad_qkv, qkv_weight, preferred_element_type=jnp.float32
    )
    qkv_grad = jnp.einsum("nlc,jnld->jcd", inputs_low, grad_qkv, preferred_element_type=jnp.float32)
    query_bias_grad = jnp.sum(grad_qkv[0], axis=(0, 1), dtype=jnp.float32)
    value_bias_grad = jnp.sum(grad_qkv[2], axis=(0, 1), dtype=jnp.float32)
    bias_grads = (query_bias_grad, value_bias_grad, proj_bias_grad)
    return (grad_inputs.reshape(grad_output.shape), proj_grad, qkv_grad, bias_grads)


def swish_slope(normed):
    logistic = jax.nn.sigmoid(normed)
    return logistic * (1.0 + normed * (1.0 - logistic))


def assemble(params, vectors):
    whole_rows = lax.all_gather(
        params.astype(jnp.bfloat16), ("canvas", "height"), axis=0, tiled=True
    )
    whole_vectors = vectors.astype(jnp.bfloat16)
    channels = whole_rows.shape[1]
    weights = (
        whole_rows[: 9 * channels],
        whole_rows[9 * channels : 18 * channels],
        whole_rows[18 * channels : 21 * channels].reshape(3, channels, channels),
        whole_rows[21 * channels :],
    )
    return (weights, whole_vectors)


def forward(hidden, weights, vectors, layout):
    conv_one, conv_two, qkv_weight, proj_weight = weights
    tap_masks = layout[0]
    normed_one, kept_one = norm_forward(hidden, vectors[0], vectors[1], layout)
    activated_one = jax.nn.silu(normed_one).astype(jnp.bfloat16)
    conv_out, columns_one = conv_forward(activated_one, conv_one, vectors[2], tap_masks)
    normed_two, kept_two = norm_forward(conv_out, vectors[3], vectors[4], layout)
    activated_two = jax.nn.silu(normed_two).astype(jnp.bfloat16)
    branch, columns_two = conv_forward(activated_two, conv_two, vectors[5], tap_masks)
    first_hidden = hidden + branch
    normed_three, kept_three = norm_forward(first_hidden, vectors[6], vectors[7], layout)
    attn_branch, kept_attn = attend_forward(normed_three, qkv_weight, proj_weight, vectors, layout)
    output = first_hidden + attn_branch
    stored = (
        normed_one,
        kept_one,
        columns_one,
        normed_two,
        kept_two,
        columns_two,
        kept_three,
        kept_attn,
    )
    return (first_hidden, output, stored)


def backward(grad_final, weights, vectors, layout, stored):
    conv_one, conv_two, qkv_weight, proj_weight = weights
    normed_one, kept_one, columns_one, normed_two, kept_two, columns_two, kept_three, kept_attn = (
        stored
    )
    tap_masks = layout[0]
    grad_normed, proj_grad, qkv_grad, bias_grads = attend_backward(
        grad_final, qkv_weight, proj_weight, layout, kept_attn
    )
    grad_through, gain_three, bias_three = norm_backward(
        grad_normed, kept_three, vectors[6], layout
    )
    grad_hidden = grad_final + grad_through
    grad_source, conv_two_grad, conv_two_bias = conv_backward(
        grad_hidden.astype(jnp.bfloat16), conv_two, columns_two, tap_masks
    )
    grad_pre, gain_two, bias_two = norm_backward(
        grad_source * swish_slope(normed_two), kept_two, vectors[3], layout
    )
    grad_source, conv_one_grad, conv_one_bias = conv_backward(
        grad_pre.astype(jnp.bfloat16), conv_one, columns_one, tap_masks
    )
    grad_back, gain_one, bias_one = norm_backward(
        grad_source * swish_slope(normed_one), kept_one, vectors[0], layout
    )
    input_grad = grad_hidden + grad_back
    matrix_grad = jnp.concatenate(
        [conv_one_grad, conv_two_grad, qkv_grad.reshape(-1, qkv_grad.shape[-1]), proj_grad], axis=0
    )
    vector_grad = jnp.stack(
        [
            gain_one,
            bias_one,
            conv_one_bias,
            gain_two,
            bias_two,
            conv_two_bias,
            gain_three,
            bias_three,
            bias_grads[0],
            bias_grads[1],
            bias_grads[2],
        ]
    )
    return (input_grad, matrix_grad, vector_grad)


def adam_update(current, gradient, moment_one, moment_two, learn_rate):
    first_new = 0.5 * moment_one + 0.5 * gradient
    second_new = 0.9 * moment_two + 0.1 * gradient * gradient
    first_hat = first_new / (1.0 - 0.5**STEP)
    second_hat = second_new / (1.0 - 0.9**STEP)
    return (
        current - learn_rate * first_hat / (jnp.sqrt(second_hat) + adam_epsilon),
        first_new,
        second_new,
    )


def body(
    latents,
    crop_ids,
    params,
    vectors,
    first_moment,
    second_moment,
    vector_first,
    vector_second,
    cotangent,
):
    layout = build_layout(crop_ids)
    hidden = latents.astype(jnp.float32)
    weights, vector_low = assemble(params, vectors)
    first_hidden, first_output, stored = forward(hidden, weights, vector_low, layout)
    input_grad, matrix_grad, vector_grad = backward(
        cotangent.astype(jnp.float32), weights, vector_low, layout, stored
    )
    matrix_share = lax.psum_scatter(
        matrix_grad, ("canvas", "height"), scatter_dimension=0, tiled=True
    )
    vector_total = lax.psum(vector_grad, ("canvas", "height"))
    new_params, new_first, new_second = adam_update(
        params, matrix_share, first_moment, second_moment, matrix_rate
    )
    new_vectors, new_vector_first, new_vector_second = adam_update(
        vectors, vector_total, vector_first, vector_second, vector_rate
    )
    new_weights, new_vector_low = assemble(new_params, new_vectors)
    second_pass = forward(hidden, new_weights, new_vector_low, layout)
    return (
        first_hidden,
        first_output,
        second_pass[1],
        input_grad,
        new_params,
        new_first,
        new_second,
        new_vectors,
        new_vector_first,
        new_vector_second,
    )


def solution(mesh):
    in_specs = (
        P("canvas", "height", None, None),
        P("canvas", "height", None),
        P(("canvas", "height"), None),
        P(),
        P(("canvas", "height"), None),
        P(("canvas", "height"), None),
        P(),
        P(),
        P("canvas", "height", None, None),
    )
    out_specs = (
        P("canvas", "height", None, None),
        P("canvas", "height", None, None),
        P("canvas", "height", None, None),
        P("canvas", "height", None, None),
        P(("canvas", "height"), None),
        P(("canvas", "height"), None),
        P(("canvas", "height"), None),
        P(),
        P(),
        P(),
    )
    return jax.shard_map(body, mesh=mesh, in_specs=in_specs, out_specs=out_specs, check_vma=False)
```

profile of v0, /device:TPU:0, one launch (start us, length us, event | category | flops | bytes accessed | tf_op | source)
XLA Modules:
  0.0 1836.9 jit_solution(3634141015965277373)
XLA Ops:
  10.8 15.9 all_gather.21
  34.0 29.7 %psum.125 = f32[2,16,32]{2,1,0:T(8,128)S(1)} all-reduce(f32[2,16,32]{2,1,0:T(8,128)S(1)} %fusion.178), channel_id=1, replica_groups=mesh['canvas'=4,'height'=8] {'height'}, use_global_device_ids=true, to_apply=%region_1.2 | all-reduce | flops 1024 | bytes 8192 | tf_op jit(solution)/shard_map/psum | solution.py:73
  64.9 26.8 %psum.126 = f32[2,16,32]{2,1,0:T(8,128)S(1)} all-reduce(f32[2,16,32]{2,1,0:T(8,128)S(1)} %fusion.176), channel_id=1, replica_groups=mesh['canvas'=4,'height'=8] {'height'}, use_global_device_ids=true, to_apply=%region_4.5 | all-reduce | flops 1024 | bytes 8192 | tf_op jit(solution)/shard_map/psum | solution.py:77
  121.5 31.7 %copy.250 = bf16[2,8,64,9,512]{4,3,2,1,0:T(8,128)(2,1)S(1)} copy(bf16[2,8,64,9,512]{4,2,0,1,3:T(8,128)(2,1)S(1)} %fusion.121) | data formatting | bytes 18874368 | tf_op jit(solution)/shard_map/stack | solution.py:118
  153.2 12.3 copy.378
  165.4 9.0 convolution_add_fusion.3
  182.0 27.8 %psum.127 = f32[2,16,32]{2,1,0:T(8,128)S(1)} all-reduce(f32[2,16,32]{2,1,0:T(8,128)S(1)} %fusion.150), channel_id=1, replica_groups=mesh['canvas'=4,'height'=8] {'height'}, use_global_device_ids=true, to_apply=%region_6.7 | all-reduce | flops 1024 | bytes 8192 | tf_op jit(solution)/shard_map/psum | solution.py:73
  211.7 25.9 %psum.128 = f32[2,16,32]{2,1,0:T(8,128)S(1)} all-reduce(f32[2,16,32]{2,1,0:T(8,128)S(1)} %fusion.148), channel_id=1, replica_groups=mesh['canvas'=4,'height'=8] {'height'}, use_global_device_ids=true, to_apply=%region_8.9 | all-reduce | flops 1024 | bytes 8192 | tf_op jit(solution)/shard_map/psum | solution.py:77
  247.8 5.3 reshape.480
  256.9 5.1 multiply_convert_fusion.8
  269.1 5.3 reshape.477
  289.9 31.7 %copy.267 = bf16[2,8,64,9,512]{4,3,2,1,0:T(8,128)(2,1)S(1)} copy(bf16[2,8,64,9,512]{4,2,0,1,3:T(8,128)(2,1)S(1)} %fusion.103) | data formatting | bytes 18874368 | tf_op jit(solution)/shard_map/stack | solution.py:118
  321.6 17.5 copy.379
  339.1 9.0 convolution_add_fusion.2
  351.3 5.0 reshape.419
  358.6 27.0 %psum.129 = f32[2,16,32]{2,1,0:T(8,128)S(1)} all-reduce(f32[2,16,32]{2,1,0:T(8,128)S(1)} %fusion.172), channel_id=1, replica_groups=mesh['canvas'=4,'height'=8] {'height'}, use_global_device_ids=true, to_apply=%region_10.11 | all-reduce | flops 1024 | bytes 8192 | tf_op jit(solution)/shard_map/psum | solution.py:73
  388.2 25.9 %psum.130 = f32[2,16,32]{2,1,0:T(8,128)S(1)} all-reduce(f32[2,16,32]{2,1,0:T(8,128)S(1)} %fusion.170), channel_id=1, replica_groups=mesh['canvas'=4,'height'=8] {'height'}, use_global_device_ids=true, to_apply=%region_12.13 | all-reduce | flops 1024 | bytes 8192 | tf_op jit(solution)/shard_map/psum | solution.py:77
  451.6 74.5 %all-gather.17.cloned.1.call-done = bf16[1,2,4096,512]{3,2,0,1:T(8,128)(2,1)} async-done(((bf16[1,2,512,512]{3,2,0,1:T(8,128)(2,1)}), bf16[1,2,4096,512]{3,2,0,1:T(8,128)(2,1)}) %all-gather.17.cloned.1.call-update) | async-done | bytes 8388624 | tf_op jit(solution)/shard_map/all_gather | solution.py:165
  526.1 13.3 fusion.294
  539.4 8.3 fusion.1
  547.7 11.0 fusion.18
  558.8 49.5 %all-gather.11.cloned.1.call-done = bf16[2,4096,512]{2,1,0:T(8,128)(2,1)} async-done(((bf16[2,512,512]{2,1,0:T(8,128)(2,1)}), bf16[2,4096,512]{2,1,0:T(8,128)(2,1)}) %all-gather.11.cloned.1.call-update) | async-done | bytes 8388624 | tf_op jit(solution)/shard_map/all_gather | solution.py:166
  608.4 17.4 multiply_reduce_fusion
  625.7 15.4 multiply_convert_fusion.1
  641.1 11.9 multiply_convert_fusion
  653.2 8.4 fusion.287
  661.5 11.1 fusion.54
  674.5 9.0 convert_reduce_fusion.2
  683.5 15.2 reduce-scatter.6.cloned.1.call-done
  698.7 90.1 %reduce-scatter.4.cloned.1.call-done = bf16[2,512,512]{2,1,0:T(8,128)(2,1)} async-done(((bf16[2,4096,512]{2,1,0:T(8,128)(2,1)}), bf16[2,512,512]{2,1,0:T(8,128)(2,1)}) %reduce-scatter.4.cloned.1.call-update) | async-done | bytes 1048592 | tf_op jit(solution)/shard_map/reduce_scatter | solution.py:234
  797.2 4.9 reshape.422
  805.3 26.0 %all-reduce.9 = (f32[2,16,32]{2,1,0:T(8,128)S(1)}, f32[2,16,32]{2,1,0:T(8,128)S(1)}) all-reduce(f32[2,16,32]{2,1,0:T(8,128)S(1)} %fusion.166, f32[2,16,32]{2,1,0:T(8,128)S(1)} %fusion.168), channel_id=1, replica_groups=mesh['canvas'=4,'height'=8] {'height'}, use_global_device_ids=true, to_apply=%region_21.22 | all-reduce | flops 2048 | bytes 16384 | tf_op jit(solution)/shard_map/psum | solution.py:95
  845.0 6.6 bitcast_reduce_fusion
  854.4 8.1 fusion.300
  872.4 5.0 fusion.297
  883.0 5.1 reshape.424
  888.1 6.7 fusion.41
  897.2 27.0 %all-reduce.8 = (f32[2,16,32]{2,1,0:T(8,128)S(1)}, f32[2,16,32]{2,1,0:T(8,128)S(1)}) all-reduce(f32[2,16,32]{2,1,0:T(8,128)S(1)} %fusion.146, f32[2,16,32]{2,1,0:T(8,128)S(1)} %fusion.164), channel_id=1, replica_groups=mesh['canvas'=4,'height'=8] {'height'}, use_global_device_ids=true, to_apply=%region_25.26 | all-reduce | flops 2048 | bytes 16384 | tf_op jit(solution)/shard_map/psum | solution.py:95
  938.2 4.7 convert_reduce_fusion.4
  943.0 11.4 fusion.299
  954.4 26.7 %pad_maximum_fusion = f32[11264,512]{1,0:T(8,128)} fusion(f32[512,512]{1,0:T(8,128)S(1)} %copy-done.40, f32[1536,512]{1,0:T(8,128)S(1)} %bitcast.544, f32[4608,512]{1,0:T(8,128)S(1)} %bitcast.515, f32[4608,512]{1,0:T(8,128)} %fusion.299), kind=kLoop, calls=%fused_computation.1 | loop fusion | flops 17301504 | bytes 46137344 | tf_op jit(solution)/shard_map/concatenate | solution.py:326
  981.2 250.3 %reduce-scatter.8.cloned.1.call-done = f32[352,512]{1,0:T(8,128)} async-done(((f32[11264,512]{1,0:T(8,128)}), f32[352,512]{1,0:T(8,128)}) %reduce-scatter.8.cloned.1.call-update) | async-done | bytes 720912 | tf_op jit(solution)/shard_map/reduce_scatter | solution.py:377
  1245.7 5.0 fusion.298
  1253.8 40.5 %psum.135 = f32[11,512]{1,0:T(8,128)S(1)} all-reduce(f32[11,512]{1,0:T(8,128)S(1)} %stack.318), channel_id=1, replica_groups=mesh['canvas'=4,'height'=8] {'canvas','height'}, use_global_device_ids=true, to_apply=%region_37.38 | all-reduce | flops 5632 | bytes 45056 | tf_op jit(solution)/shard_map/psum | solution.py:380
  1304.9 4.8 reshape.435
  1321.5 31.7 %copy.308 = bf16[2,8,64,9,512]{4,3,2,1,0:T(8,128)(2,1)S(1)} copy(bf16[2,8,64,9,512]{4,2,0,1,3:T(8,128)(2,1)S(1)} %fusion.81) | data formatting | bytes 18874368 | tf_op jit(solution)/shard_map/stack | solution.py:118
  1353.2 12.3 copy.380
  1365.5 10.7 fusion.48
  1385.9 28.9 %psum.136 = f32[2,16,32]{2,1,0:T(8,128)S(1)} all-reduce(f32[2,16,32]{2,1,0:T(8,128)S(1)} %fusion.144), channel_id=1, replica_groups=mesh['canvas'=4,'height'=8] {'height'}, use_global_device_ids=true, to_apply=%region_40.41 | all-reduce | flops 1024 | bytes 8192 | tf_op jit(solution)/shard_map/psum | solution.py:73
  1418.3 25.9 %psum.137 = f32[2,16,32]{2,1,0:T(8,128)S(1)} all-reduce(f32[2,16,32]{2,1,0:T(8,128)S(1)} %fusion.142), channel_id=1, replica_groups=mesh['canvas'=4,'height'=8] {'height'}, use_global_device_ids=true, to_apply=%region_42.43 | all-reduce | flops 1024 | bytes 8192 | tf_op jit(solution)/shard_map/psum | solution.py:77
  1446.5 5.3 reshape.478
  1472.6 5.5 reshape.479
  1496.8 31.7 %copy.325 = bf16[2,8,64,9,512]{4,3,2,1,0:T(8,128)(2,1)S(1)} copy(bf16[2,8,64,9,512]{4,2,0,1,3:T(8,128)(2,1)S(1)} %fusion.63) | data formatting | bytes 18874368 | tf_op jit(solution)/shard_map/stack | solution.py:118
  1528.5 17.5 copy.381
  1546.0 5.0 fusion.51
  1556.6 5.2 reshape.433
  1564.0 27.0 %psum.138 = f32[2,16,32]{2,1,0:T(8,128)S(1)} all-reduce(f32[2,16,32]{2,1,0:T(8,128)S(1)} %fusion.159), channel_id=1, replica_groups=mesh['canvas'=4,'height'=8] {'height'}, use_global_device_ids=true, to_apply=%region_44.45 | all-reduce | flops 1024 | bytes 8192 | tf_op jit(solution)/shard_map/psum | solution.py:73
  1593.6 26.4 %all-reduce.7 = (f32[2,16,32]{2,1,0:T(8,128)S(1)}, f32[2,16,32]{2,1,0:T(8,128)S(1)}, f32[2,16,32]{2,1,0:T(8,128)S(1)}) all-reduce(f32[2,16,32]{2,1,0:T(8,128)S(1)} %fusion.157, f32[2,16,32]{2,1,0:T(8,128)S(1)} %fusion.153, f32[2,16,32]{2,1,0:T(8,128)S(1)} %fusion.155), channel_id=1, replica_groups=mesh['canvas'=4,'height'=8] {'height'}, use_global_device_ids=true, to_apply=%region_46.47 | all-reduce | flops 3072 | bytes 24576 | tf_op jit(solution)/shard_map/psum | solution.py:77
  1681.3 5.7 multiply_add_fusion
  1688.6 43.6 %all-gather.19.cloned.1.call-done = bf16[1,2,4096,512]{2,3,1,0:T(8,128)(2,1)} async-done(((bf16[1,2,512,512]{2,3,1,0:T(8,128)(2,1)}), bf16[1,2,4096,512]{2,3,1,0:T(8,128)(2,1)}) %all-gather.19.cloned.1.call-update) | async-done | bytes 8388624 | tf_op jit(solution)/shard_map/all_gather | solution.py:165
  1732.2 14.8 fusion.6
  1747.0 21.8 %fusion.295 = (f32[2,512]{1,0:T(2,128)S(1)}, f32[2,512,4096]{2,1,0:T(8,128)}) fusion(f32[2,512,4096]{2,1,0:T(8,128)} %fusion.6, s32[2,4096]{1,0:T(2,128)S(1)} %copy-done.68, s32[2,512]{1,0:T(2,128)S(1)} %eq.40), kind=kOutput, calls=%fused_computation.501 | output fusion | flops 33558528 | bytes 33595392 | tf_op jit(solution)/shard_map/sub | solution.py:170
  1768.9 45.6 %all-gather.15.cloned.1.call-done = bf16[2,4096,512]{1,2,0:T(8,128)(2,1)} async-done(((bf16[2,512,512]{1,2,0:T(8,128)(2,1)}), bf16[2,4096,512]{1,2,0:T(8,128)(2,1)}) %all-gather.15.cloned.1.call-update) | async-done | bytes 8388624 | tf_op jit(solution)/shard_map/all_gather | solution.py:166
  1814.4 12.1 convolution_add_fusion
  (516 shorter events, 364.8 us)
Async XLA Ops:
  7.2 19.6 %copy-start.16 = (bf16[2,8,64,512]{3,2,1,0:T(8,128)(2,1)S(1)}, bf16[2,8,64,512]{3,2,1,0:T(8,128)(2,1)}, u32[]{:S(2)}) copy-start(bf16[2,8,64,512]{3,2,1,0:T(8,128)(2,1)} %param.9) | copy-start | bytes 3145732
  7.2 158.2 %all-gather.9.cloned.1.call-start = ((), (), s32[]{:S(2)}) async-start(), calls=%async_computation.3 | async-start | bytes 11894784 | tf_op jit(solution)/shard_map/all_gather | solution.py:260
  9.2 516.9 %all-gather.17.cloned.1.call-start = ((), (), s32[]{:S(2)}) async-start(), calls=%async_computation.10 | async-start | bytes 9437184 | tf_op jit(solution)/shard_map/all_gather | solution.py:165
  26.8 499.3 %copy-start.67 = (s32[2,4096]{1,0:T(2,128)}, s32[2,4096]{1,0:T(2,128)S(1)}, u32[]{:S(2)}) copy-start(s32[2,4096]{1,0:T(2,128)S(1)} %eq.88) | copy-start | bytes 98308
  33.3 31.4 %copy-start.4 = (f32[2,512,32,16]{1,3,2,0:T(8,128)}, f32[2,512,32,16]{1,3,2,0:T(8,128)S(1)}, u32[]{:S(2)}) copy-start(f32[2,512,32,16]{1,3,2,0:T(8,128)S(1)} %reshape.415) | copy-start | bytes 6291460
  64.1 33.8 %copy-start.29 = (f32[2,512,32]{1,2,0:T(8,128)}, f32[2,512,32]{1,2,0:T(8,128)S(1)}, u32[]{:S(2)}) copy-start(f32[2,512,32]{1,2,0:T(8,128)S(1)} %fusion.177) | copy-start | bytes 393220
  98.0 10.6 copy-start.8
  108.6 177.5 %copy-start.69 = (f32[1,512]{1,0:T(1,128)}, f32[1,512]{1,0:T(1,128)S(1)}, u32[]{:S(2)}) copy-start(f32[1,512]{1,0:T(1,128)S(1)} %get-tuple-element.132) | copy-start | bytes 6148
  108.6 177.5 %copy-start.73 = (f32[1,512]{1,0:T(1,128)}, f32[1,512]{1,0:T(1,128)S(1)}, u32[]{:S(2)}) copy-start(f32[1,512]{1,0:T(1,128)S(1)} %get-tuple-element.131) | copy-start | bytes 6148
  112.5 4.2 collective-permute-start
  113.8 3.2 collective-permute-start.1
  116.5 172.8 %copy-start.48 = (bf16[2,8,64]{2,0,1:T(2,128)(2,1)}, bf16[2,8,64]{2,0,1:T(2,128)(2,1)S(1)}, u32[]{:S(2)}) copy-start(bf16[2,8,64]{2,0,1:T(2,128)(2,1)S(1)} %copy.249) | copy-start | bytes 6148
  116.6 172.4 %copy-start.50 = (bf16[2,8,64]{2,0,1:T(2,128)(2,1)}, bf16[2,8,64]{2,0,1:T(2,128)(2,1)S(1)}, u32[]{:S(2)}) copy-start(bf16[2,8,64]{2,0,1:T(2,128)(2,1)S(1)} %copy.248) | copy-start | bytes 6148
  116.6 172.1 %copy-start.52 = (bf16[2,8,64]{2,0,1:T(2,128)(2,1)}, bf16[2,8,64]{2,0,1:T(2,128)(2,1)S(1)}, u32[]{:S(2)}) copy-start(bf16[2,8,64]{2,0,1:T(2,128)(2,1)S(1)} %copy.247) | copy-start | bytes 6148
  116.6 171.4 %copy-start.54 = (bf16[2,8,64]{2,0,1:T(2,128)(2,1)}, bf16[2,8,64]{2,0,1:T(2,128)(2,1)S(1)}, u32[]{:S(2)}) copy-start(bf16[2,8,64]{2,0,1:T(2,128)(2,1)S(1)} %copy.246) | copy-start | bytes 6148
  116.6 169.4 %copy-start.56 = (bf16[2,8,64]{2,0,1:T(2,128)(2,1)}, bf16[2,8,64]{2,0,1:T(2,128)(2,1)S(1)}, u32[]{:S(2)}) copy-start(bf16[2,8,64]{2,0,1:T(2,128)(2,1)S(1)} %copy.245) | copy-start | bytes 6148
  116.7 169.0 %copy-start.58 = (bf16[2,8,64]{2,0,1:T(2,128)(2,1)}, bf16[2,8,64]{2,0,1:T(2,128)(2,1)S(1)}, u32[]{:S(2)}) copy-start(bf16[2,8,64]{2,0,1:T(2,128)(2,1)S(1)} %copy.244) | copy-start | bytes 6148
  116.7 168.4 %copy-start.60 = (bf16[2,8,64]{2,0,1:T(2,128)(2,1)}, bf16[2,8,64]{2,0,1:T(2,128)(2,1)S(1)}, u32[]{:S(2)}) copy-start(bf16[2,8,64]{2,0,1:T(2,128)(2,1)S(1)} %copy.243) | copy-start | bytes 6148
  116.7 168.0 %copy-start.62 = (bf16[2,8,64]{2,0,1:T(2,128)(2,1)}, bf16[2,8,64]{2,0,1:T(2,128)(2,1)S(1)}, u32[]{:S(2)}) copy-start(bf16[2,8,64]{2,0,1:T(2,128)(2,1)S(1)} %copy.242) | copy-start | bytes 6148
  116.7 167.7 %copy-start.64 = (bf16[2,8,64]{2,0,1:T(2,128)(2,1)}, bf16[2,8,64]{2,0,1:T(2,128)(2,1)S(1)}, u32[]{:S(2)}) copy-start(bf16[2,8,64]{2,0,1:T(2,128)(2,1)S(1)} %copy.241) | copy-start | bytes 6148
  180.6 30.8 %copy-start.6 = (f32[2,512,32,16]{1,0,3,2:T(2,128)}, f32[2,512,32,16]{1,0,3,2:T(2,128)S(1)}, u32[]{:S(2)}) copy-start(f32[2,512,32,16]{1,0,3,2:T(2,128)S(1)} %reshape_reshape.15) | copy-start | bytes 6291460
  210.2 28.4 %copy-start.31 = (f32[2,512,32]{1,0,2:T(2,128)}, f32[2,512,32]{1,0,2:T(2,128)S(1)}, u32[]{:S(2)}) copy-start(f32[2,512,32]{1,0,2:T(2,128)S(1)} %copy.253) | copy-start | bytes 393220
  262.7 21.0 %collective-permute-start.2 = (bf16[2,1,64,512]{3,2,0,1:T(8,128)(2,1)}, bf16[2,1,64,512]{3,2,0,1:T(8,128)(2,1)S(1)}, u32[]{:S(2)}, u32[]{:S(2)}) collective-permute-start(bf16[2,1,64,512]{3,2,0,1:T(8,128)(2,1)} %get-tuple-element.100), channel_id=1, source_target_pairs={{0,1},{1,2},{2,3},{3,4},{4,5},{5,6},{6,7},{8,9},{9,10},{10,11},{11... | collective-permute-start | bytes 393224 | tf_op jit(solution)/shard_map/ppermute | solution.py:28
  264.0 19.7 %collective-permute-start.3 = (bf16[2,1,64,512]{3,2,0,1:T(8,128)(2,1)}, bf16[2,1,64,512]{3,2,0,1:T(8,128)(2,1)S(1)}, u32[]{:S(2)}, u32[]{:S(2)}) collective-permute-start(bf16[2,1,64,512]{3,2,0,1:T(8,128)(2,1)} %get-tuple-element.101), channel_id=1, source_target_pairs={{1,0},{2,1},{3,2},{4,3},{5,4},{6,5},{7,6},{9,8},{10,9},{11,10},{12... | collective-permute-start | bytes 393224 | tf_op jit(solution)/shard_map/ppermute | solution.py:30
  339.1 9.0 copy-start.19
  339.1 9.0 copy-start.17
  348.5 85.6 %copy-start.1 = (f32[2,8,64,512]{3,2,0,1:T(8,128)}, f32[2,8,64,512]{3,2,0,1:T(8,128)S(1)}, u32[]{:S(2)}) copy-start(f32[2,8,64,512]{3,2,0,1:T(8,128)S(1)} %copy_add_fusion.3) | copy-start | bytes 6291460
  445.8 162.6 %all-gather.11.cloned.1.call-start = ((), (), s32[]{:S(2)}) async-start(), calls=%async_computation.4 | async-start | bytes 9437184 | tf_op jit(solution)/shard_map/all_gather | solution.py:166
  448.8 249.9 %reduce-scatter.6.cloned.1.call-start = ((), (), s32[]{:S(2)}) async-start(), calls=%async_computation.6 | async-start | bytes 9437184 | tf_op jit(solution)/shard_map/reduce_scatter | solution.py:237
  539.4 8.3 copy-start.41
  558.8 230.1 %reduce-scatter.4.cloned.1.call-start = ((), (), s32[]{:S(2)}) async-start(), calls=%async_computation.5 | async-start | bytes 9437184 | tf_op jit(solution)/shard_map/reduce_scatter | solution.py:234
  653.1 578.4 %reduce-scatter.8.cloned.1.call-start = ((), (), s32[]{:S(2)}) async-start(), calls=%async_computation.7 | async-start | bytes 23789568 | tf_op jit(solution)/shard_map/reduce_scatter | solution.py:377
  653.2 21.3 %slice-start.6 = ((s8[8388608]{0:T(1024)(128)(4,1)}), s8[4194304]{0:T(1024)(128)(4,1)S(1)}, s32[]{:S(2)}) async-start(s8[8388608]{0:T(1024)(128)(4,1)} %bitcast.516), calls=%async_computation.18 | async-start | bytes 8388608
  661.5 12.9 slice-start.7
  845.0 9.3 slice-start
  845.0 9.3 slice-start.1
  845.0 9.3 slice-start.2
  851.7 14.4 collective-permute-start.4
  853.0 13.1 collective-permute-start.5
  938.2 16.2 slice-start.3
  943.0 11.4 slice-start.4
  943.0 11.4 slice-start.5
  943.0 11.4 copy-start.27
  943.0 11.4 copy-start.40
  981.1 250.4 %copy-start.28 = (f32[352,512]{1,0:T(8,128)S(1)}, f32[352,512]{1,0:T(8,128)}, u32[]{:S(2)}) copy-start(f32[352,512]{1,0:T(8,128)} %param.11) | copy-start | bytes 2162692
  981.2 256.8 %copy-start.26 = (bf16[2,512,512]{2,1,0:T(8,128)(2,1)S(1)}, bf16[2,512,512]{2,1,0:T(8,128)(2,1)}, u32[]{:S(2)}) copy-start(bf16[2,512,512]{2,1,0:T(8,128)(2,1)} %reduce-scatter.6.cloned.1.call-done) | copy-start | bytes 3145732
  981.2 384.3 %all-gather.13.cloned.1.call-start = ((), (), s32[]{:S(2)}) async-start(), calls=%async_computation.8 | async-start | bytes 11894784 | tf_op jit(solution)/shard_map/all_gather | solution.py:260
  1235.1 497.1 %all-gather.19.cloned.1.call-start = ((), (), s32[]{:S(2)}) async-start(), calls=%async_computation.11 | async-start | bytes 9437184 | tf_op jit(solution)/shard_map/all_gather | solution.py:165
  1235.2 3.0 collective-permute-start.6
  1236.5 3.2 collective-permute-start.7
  1253.1 41.1 %copy-start.66 = (f32[11,512]{1,0:T(8,128)S(1)}, f32[11,512]{1,0:T(8,128)}, u32[]{:S(2)}) copy-start(f32[11,512]{1,0:T(8,128)} %param.12) | copy-start | bytes 67588
  1253.1 41.1 %copy-start.71 = (f32[11,512]{1,0:T(8,128)S(1)}, f32[11,512]{1,0:T(8,128)}, u32[]{:S(2)}) copy-start(f32[11,512]{1,0:T(8,128)} %param.15) | copy-start | bytes 67588
  1253.1 41.2 %copy-start.72 = (f32[11,512]{1,0:T(8,128)S(1)}, f32[11,512]{1,0:T(8,128)}, u32[]{:S(2)}) copy-start(f32[11,512]{1,0:T(8,128)} %param.16) | copy-start | bytes 67588
  1296.8 17.2 collective-permute-start.8
  1299.3 14.8 collective-permute-start.9
  1469.8 20.4 %collective-permute-start.10 = (bf16[2,1,64,512]{3,2,0,1:T(8,128)(2,1)}, bf16[2,1,64,512]{3,2,0,1:T(8,128)(2,1)S(1)}, u32[]{:S(2)}, u32[]{:S(2)}) collective-permute-start(bf16[2,1,64,512]{3,2,0,1:T(8,128)(2,1)} %get-tuple-element.86), channel_id=1, source_target_pairs={{0,1},{1,2},{2,3},{3,4},{4,5},{5,6},{6,7},{8,9},{9,10},{10,11},{11... | collective-permute-start | bytes 393224 | tf_op jit(solution)/shard_map/ppermute | solution.py:28
  1471.1 19.1 %collective-permute-start.11 = (bf16[2,1,64,512]{3,2,0,1:T(8,128)(2,1)}, bf16[2,1,64,512]{3,2,0,1:T(8,128)(2,1)S(1)}, u32[]{:S(2)}, u32[]{:S(2)}) collective-permute-start(bf16[2,1,64,512]{3,2,0,1:T(8,128)(2,1)} %get-tuple-element.87), channel_id=1, source_target_pairs={{1,0},{2,1},{3,2},{4,3},{5,4},{6,5},{7,6},{9,8},{10,9},{11,10},{12... | collective-permute-start | bytes 393224 | tf_op jit(solution)/shard_map/ppermute | solution.py:30
  1496.7 49.2 %slice-start.12 = ((s8[11534336]{0:T(1024)(128)(4,1)}), s8[4194304]{0:T(1024)(128)(4,1)S(1)}, s32[]{:S(2)}) async-start(s8[11534336]{0:T(1024)(128)(4,1)} %bitcast.552), calls=%async_computation.24 | async-start | bytes 8388608
  1496.7 49.2 %slice-start.13 = ((s8[11534336]{0:T(1024)(128)(4,1)}), s8[4194304]{0:T(1024)(128)(4,1)S(1)}, s32[]{:S(2)}) async-start(s8[11534336]{0:T(1024)(128)(4,1)} %bitcast.552), calls=%async_computation.25 | async-start | bytes 8388608
  1528.5 17.5 slice-start.14
  1650.7 163.7 %all-gather.15.cloned.1.call-start = ((), (), s32[]{:S(2)}) async-start(), calls=%async_computation.9 | async-start | bytes 9437184 | tf_op jit(solution)/shard_map/all_gather | solution.py:166
  1732.2 14.8 copy-start.68
  1747.0 67.4 %copy-start.80 = (f32[1,512]{1,0:T(1,128)S(1)}, f32[1,512]{1,0:T(1,128)}, u32[]{:S(2)}) copy-start(f32[1,512]{1,0:T(1,128)} %get-tuple-element.114) | copy-start | bytes 6148
  1814.4 12.1 copy-start.3
  (56 other events, 200.2 us)
Sparse Core Ops, SparseCore 0:
  11.4 94.1 all-gather.8
  445.9 80.2 all-gather.16
  527.7 80.5 all-gather.10
  610.5 88.1 reduce-scatter.5
  700.8 87.9 reduce-scatter.3
  981.3 250.2 reduce-scatter.7
  1235.2 89.1 all-gather.12
  1650.8 81.2 all-gather.18
  1733.8 80.5 all-gather.14
where the time goes:
time: 1850 us; the launch traced here: 1840 us
  waiting for transfers between devices  571 us (31%)
  local copies, waits for them, and re-layouts  466 us (25%)
  blocking collectives  380 us (21%)
  other arithmetic  197 us (11%)
  matrix products  188 us (10%)
    reduce_scatter x1, waiting for transfers between devices, body(): lax.psum_scatter(matrix_grad, ('canvas', 'height'), scatter_dimension=0,...  250 us
    psum x5, blocking collectives, norm_forward(): centre = lax.psum(local_sum, 'height') / divisor[:, :, None]  140 us
    psum x5, blocking collectives, norm_forward(): spread = lax.psum(local_square, 'height') / divisor[:, :, None]  131 us
    another operation x4, local copies, waits for them, and re-layouts, conv_forward(): jnp.stack(pieces, axis=3)  127 us
    all_gather x2, waiting for transfers between devices, attend_forward(): lax.all_gather(keys_local, 'height', axis=1, tiled=True)  118 us
    all_gather x2, waiting for transfers between devices, attend_forward(): lax.all_gather(values_local, 'height', axis=1, tiled=True)  95.1 us
    reduce_scatter x1, waiting for transfers between devices, attend_backward(): lax.psum_scatter(partial_keys.astype(jnp.bfloat16), 'height', scatter_dim...  90.1 us
    unnamed x220, local copies, waits for them, and re-layouts  86.6 us
  transfers between devices with their start and end apart: 21, of which 9 were waited for; matrix products, arithmetic and copies ran while one was open for 21% of the time, Pallas kernels for 0%

commit v1 on v0

v1 whole, which is shorter than its diff:
```python
import functools

import jax
import jax.numpy as jnp
from jax import lax
from jax.experimental import pallas as pl
from jax.experimental.pallas import tpu as pltpu
from jax.sharding import PartitionSpec as P

C = 512
GROUPS = 32
STEP = 5
CROPS = 16
SPAN = C // GROUPS
LANES = 128
TILES = C // LANES
UNIT = 8

norm_epsilon = 1e-06
adam_epsilon = 1e-08
matrix_rate = 0.015
vector_rate = 0.2
mask_fill = -1e30

F32 = jnp.float32
B16 = jnp.bfloat16
MESH = pl.DeviceIdType.MESH
VMEM_LIMIT = 60 * 2**20

vmem = pl.BlockSpec(memory_space=pltpu.VMEM)
smem = pl.BlockSpec(memory_space=pltpu.SMEM)
anyw = pl.BlockSpec(memory_space=pl.ANY)


def params_of(cid=None):
    if cid is None:
        return pltpu.CompilerParams(vmem_limit_bytes=VMEM_LIMIT)
    return pltpu.CompilerParams(
        vmem_limit_bytes=VMEM_LIMIT, collective_id=cid, has_side_effects=True
    )


def sds(shape, dtype):
    return jax.ShapeDtypeStruct(shape, dtype)


def split_dot(pick, value):
    total = None
    rest = value
    for _ in range(3):
        part = rest.astype(B16)
        term = jnp.dot(pick, part, preferred_element_type=F32)
        total = term if total is None else total + term
        rest = rest - part.astype(F32)
    return total


def lane_group_sum(piece):
    lane = lax.broadcasted_iota(jnp.int32, piece.shape, 1)
    step = 1
    while step < SPAN:
        ahead = pltpu.roll(piece, LANES - step, 1)
        behind = pltpu.roll(piece, step, 1)
        piece = piece + jnp.where((lane & step) == 0, ahead, behind)
        step *= 2
    return piece


def tiles_of(value):
    return [value[:, j * LANES : (j + 1) * LANES] for j in range(TILES)]


def wide(piece, times=TILES):
    return jnp.concatenate([piece] * times, axis=1)


def pack(quantities):
    shape = quantities[0][0].shape
    sub = lax.broadcasted_iota(jnp.int32, shape, 1) & (SPAN - 1)
    out = jnp.zeros(shape, F32)
    for q, pieces in enumerate(quantities):
        for j, piece in enumerate(pieces):
            out = jnp.where(sub == TILES * q + j, piece, out)
    return out


def unpack(packed):
    sub = lax.broadcasted_iota(jnp.int32, packed.shape, 1) & (SPAN - 1)
    return jnp.concatenate(
        [lane_group_sum(jnp.where(sub == j, packed, 0.0)) for j in range(TILES)], axis=1
    )


def shift_down(packed, q):
    return pltpu.roll(packed, LANES - TILES * q, packed.ndim - 1)


def greet(n):
    me = lax.axis_index("height")
    barrier = pltpu.get_barrier_semaphore()
    for d in range(1, n):
        pl.semaphore_signal(
            barrier, inc=1, device_id={"height": lax.rem(me + d, n)}, device_id_type=MESH
        )
    pl.semaphore_wait(barrier, n - 1)


def spread_copies(n, buf, send, recv, rnd):
    me = lax.axis_index("height")
    return [
        pltpu.make_async_remote_copy(
            src_ref=buf.at[rnd, 0],
            dst_ref=buf.at[rnd, d],
            send_sem=send.at[rnd, d],
            recv_sem=recv.at[rnd, d],
            device_id={"height": lax.rem(me + d, n)},
            device_id_type=MESH,
        )
        for d in range(1, n)
    ]


def cell_totals(load, out_ref, cells):
    def body(i, _):
        out_ref[pl.ds(i * 16, 16), :] = jnp.sum(load(i).reshape(16, UNIT, C), axis=1)
        return 0

    lax.fori_loop(0, cells // 16, body, 0)


def over_cells(cell_ref, i):
    return jnp.broadcast_to(cell_ref[pl.ds(i * 16, 16), :][:, None, :], (16, UNIT, C)).reshape(
        16 * UNIT, C
    )


def group_totals(pick_ref, cell_value):
    return [lane_group_sum(t) for t in tiles_of(split_dot(pick_ref[...], cell_value))]


def stats_payload(load, pick_ref, spread_ref, count_ref, cells, tmp_a, tmp_b):
    cell_totals(load, tmp_a, cells)
    sums = group_totals(pick_ref, tmp_a[...])
    count = count_ref[...]
    inv_count = 1.0 / jnp.maximum(count, 1.0)
    mean = jnp.concatenate([s * inv_count for s in sums], axis=1)
    tmp_b[...] = split_dot(spread_ref[...], mean)

    def centred(i):
        delta = load(i) - over_cells(tmp_b, i)
        return delta * delta

    cell_totals(centred, tmp_a, cells)
    squares = group_totals(pick_ref, tmp_a[...])
    return pack([sums, squares, [count] * TILES])


def combine_stats(gathered):
    sums = gathered
    squares = shift_down(gathered, 1)
    counts = shift_down(gathered, 2)
    divisor = jnp.maximum(jnp.sum(counts, axis=0), 1.0)
    mean = jnp.sum(sums, axis=0) / divisor
    apart = sums / jnp.maximum(counts, 1.0) - mean[None]
    spread = jnp.sum(squares + counts * apart * apart, axis=0) / divisor
    return mean, lax.rsqrt(spread + norm_epsilon), divisor


def shift_columns(row, left_mask, right_mask):
    width = row.shape[0]
    left = pltpu.roll(row, 1, 0) * wide(left_mask)
    right = pltpu.roll(row, width - 1, 0) * wide(right_mask)
    return jnp.concatenate([left, row, right], axis=1).astype(B16)


def logistic(a):
    return 1.0 / (1.0 + jnp.exp(-a))


def silu(a):
    return a * logistic(a)


def silu_slope(a):
    s = logistic(a)
    return s * (1.0 + a * (1.0 - s))


def layout_kernel(n, dims, x, pick, spread, ids_px, ids_lane, ids_all, mean_c, inv_c, div, cnt,
                  col_l, col_r, row_u, row_d, buf, idbuf, halo, tmp_a, tmp_b, send, recv, isend, irecv,
                  hsend, hrecv):
    canvases, rows, width = dims
    cells = canvases * rows * width // UNIT
    me = lax.axis_index("height")
    greet(n)
    id_copies = []
    idbuf[0] = ids_lane[...]
    for d in range(1, n):
        cp = pltpu.make_async_remote_copy(
            src_ref=idbuf.at[0], dst_ref=idbuf.at[d], send_sem=isend.at[d], recv_sem=irecv.at[d],
            device_id={"height": lax.rem(me + d, n)}, device_id_type=MESH)
        cp.start()
        id_copies.append(cp)
    up, down = halo_copies(n, ids_px.at[:, 0], ids_px.at[:, rows - 1], halo, hsend, hrecv)
    start_halo(n, up, down)

    def load(i):
        return x[pl.ds(i * 16 * UNIT, 16 * UNIT), :].astype(F32)

    ones = jnp.sum(pick[...].astype(F32), axis=1, keepdims=True) * float(UNIT * SPAN)
    cnt[...] = jnp.broadcast_to(ones, cnt.shape)
    buf[0, 0] = stats_payload(load, pick, spread, cnt, cells, tmp_a, tmp_b)
    copies = spread_copies(n, buf, send, recv, 0)
    for cp in copies:
        cp.start()
    wait_halo(n, up, down, halo, -1.0)
    column = lax.broadcasted_iota(jnp.int32, (width, LANES), 0)
    first, last = column == 0, column == width - 1
    for v in range(canvases):
        for r in range(rows + 2):
            here = halo[0, v] if r == 0 else halo[1, v] if r == rows + 1 else ids_px[v, r - 1]
            same_l = (pltpu.roll(here, 1, 0) == here) & jnp.logical_not(first)
            same_r = (pltpu.roll(here, width - 1, 0) == here) & jnp.logical_not(last)
            col_l[v, r] = same_l.astype(F32)
            col_r[v, r] = same_r.astype(F32)
            if 1 <= r <= rows:
                above = halo[0, v] if r == 1 else ids_px[v, r - 2]
                below = halo[1, v] if r == rows else ids_px[v, r]
                at = pl.ds((v * rows + r - 1) * width, width)
                row_u[at, :] = (above == here).astype(F32)
                row_d[at, :] = (below == here).astype(F32)
    for cp in copies:
        cp.wait_recv()
    mean, inv, divisor = combine_stats(buf[0])
    mean_c[...] = split_dot(spread[...], unpack(mean))
    inv_c[...] = split_dot(spread[...], unpack(inv))
    div[...] = unpack(divisor)[:, :LANES]
    for cp in id_copies:
        cp.wait_recv()
    ids_all[me] = idbuf[0]
    for d in range(1, n):
        ids_all[lax.rem(me - d + n, n)] = idbuf[d]
    for cp in copies + id_copies:
        cp.wait_send()


def halo_copies(n, first_row, last_row, halo, hsend, hrecv):
    me = lax.axis_index("height")
    up = pltpu.make_async_remote_copy(
        src_ref=first_row, dst_ref=halo.at[1], send_sem=hsend.at[0], recv_sem=hrecv.at[1],
        device_id={"height": lax.rem(me + n - 1, n)}, device_id_type=MESH)
    down = pltpu.make_async_remote_copy(
        src_ref=last_row, dst_ref=halo.at[0], send_sem=hsend.at[1], recv_sem=hrecv.at[0],
        device_id={"height": lax.rem(me + 1, n)}, device_id_type=MESH)
    return up, down


def start_halo(n, up, down):
    me = lax.axis_index("height")

    @pl.when(me > 0)
    def _():
        up.start()

    @pl.when(me < n - 1)
    def _():
        down.start()


def wait_halo(n, up, down, halo, edge):
    me = lax.axis_index("height")

    @pl.when(me > 0)
    def _():
        up.wait_send()
        down.wait_recv()

    @pl.when(me < n - 1)
    def _():
        down.wait_send()
        up.wait_recv()

    @pl.when(me == 0)
    def _():
        halo[0] = jnp.full(halo.shape[1:], edge, halo.dtype)

    @pl.when(me == n - 1)
    def _():
        halo[1] = jnp.full(halo.shape[1:], edge, halo.dtype)


def layout_call(n, dims, x, pick, spread, ids_px, ids_lane):
    canvases, rows, width = dims
    px = canvases * rows * width
    cells = px // UNIT
    stats = canvases * CROPS
    return pl.pallas_call(
        functools.partial(layout_kernel, n, dims),
        out_shape=[
            sds((n,) + ids_lane.shape, F32),
            sds((cells, C), F32),
            sds((cells, C), F32),
            sds((stats, LANES), F32),
            sds((stats, LANES), F32),
            sds((canvases, rows + 2, width, LANES), F32),
            sds((canvases, rows + 2, width, LANES), F32),
            sds((px, LANES), F32),
            sds((px, LANES), F32),
        ],
        in_specs=[vmem] * 5,
        out_specs=[vmem] * 9,
        scratch_shapes=[
            pltpu.VMEM((1, n, stats, LANES), F32),
            pltpu.VMEM((n,) + ids_lane.shape, F32),
            pltpu.VMEM((2, canvases, width, LANES), F32),
            pltpu.VMEM((cells, C), F32),
            pltpu.VMEM((cells, C), F32),
            pltpu.SemaphoreType.DMA((1, n)),
            pltpu.SemaphoreType.DMA((1, n)),
            pltpu.SemaphoreType.DMA((n,)),
            pltpu.SemaphoreType.DMA((n,)),
            pltpu.SemaphoreType.DMA((2,)),
            pltpu.SemaphoreType.DMA((2,)),
        ],
        compiler_params=params_of(1),
        name="layout",
    )(x, pick, spread, ids_px, ids_lane)


def resnet_forward_kernel(n, dims, keep, x, pick, spread, cnt, mean1, inv1, col_l, col_r, row_u, row_d,
                          vec, whole, *refs):
    canvases, rows, width = dims
    px = canvases * rows * width
    cells = px // UNIT
    plane = rows * width
    if keep:
        hid, u, y1, s1, s2, mean2, inv2, mean3, inv3 = refs[:9]
        refs = refs[9:]
    else:
        hid, u = refs[:2]
        y1, s1, s2, mean2, inv2, mean3, inv3 = refs[2:9]
        refs = refs[9:]
    k1, k2, halo, buf, tmp_a, tmp_b, ksem, send, recv, hsend, hrecv = refs
    load1 = pltpu.make_async_copy(whole.at[pl.ds(0, 9 * C)], k1, ksem.at[0])
    load2 = pltpu.make_async_copy(whole.at[pl.ds(9 * C, 9 * C)], k2, ksem.at[1])
    load1.start()
    load2.start()
    greet(n)
    row_cells = width // UNIT

    def activate(source, mean, inv, gain, bias, dest, rnd):
        def one(v, r):
            at = pl.ds(pl.multiple_of((v * rows + r) * width, width), width)
            cell = pl.ds(pl.multiple_of((v * rows + r) * row_cells, row_cells), row_cells)
            value = source[at, :].astype(F32)
            m = jnp.broadcast_to(mean[cell, :][:, None, :], (row_cells, UNIT, C)).reshape(width, C)
            s = jnp.broadcast_to(inv[cell, :][:, None, :], (row_cells, UNIT, C)).reshape(width, C)
            a = (value - m) * s * gain + bias
            dest[v, r + 1] = shift_columns(silu(a), col_l[v, r + 1], col_r[v, r + 1])

        def edges(v, _):
            one(v, 0)
            if rows > 1:
                one(v, rows - 1)
            return 0

        lax.fori_loop(0, canvases, edges, 0)
        mid = pl.ds(C, C)
        up, down = halo_copies(n, dest.at[:, 1, :, mid], dest.at[:, rows, :, mid], halo.at[rnd],
                               hsend.at[rnd], hrecv.at[rnd])
        start_halo(n, up, down)

        def inner(i, _):
            one(i // (rows - 2), 1 + lax.rem(i, rows - 2))
            return 0

        if rows > 2:
            lax.fori_loop(0, canvases * (rows - 2), inner, 0)
        wait_halo(n, up, down, halo.at[rnd], 0.0)
        for v in range(canvases):
            for side, r in ((0, 0), (1, rows + 1)):
                dest[v, r] = shift_columns(halo[rnd, side, v].astype(F32), col_l[v, r], col_r[v, r])

    def convolve(source, weight, emit):
        def body(v, _):
            at = pl.ds(pl.multiple_of(v * plane, plane), plane)
            total = None
            for dr in (1, 0, 2):
                lhs = source[v, dr : dr + rows].reshape(plane, 3 * C)
                part = jnp.dot(lhs, weight[3 * C * dr : 3 * C * (dr + 1), :],
                               preferred_element_type=F32)
                if dr == 0:
                    part = part * wide(row_u[at, :])
                if dr == 2:
                    part = part * wide(row_d[at, :])
                total = part if total is None else total + part
            emit(at, total)
            return 0

        lax.fori_loop(0, canvases, body, 0)

    def statistics(source, mean, inv, rnd):
        def load(i):
            return source[pl.ds(i * 16 * UNIT, 16 * UNIT), :]

        buf[rnd, 0] = stats_payload(load, pick, spread, cnt, cells, tmp_a, tmp_b)
        copies = spread_copies(n, buf, send, recv, rnd)
        for cp in copies:
            cp.start()
        for cp in copies:
            cp.wait_recv()
        m, s, _ = combine_stats(buf[rnd])
        mean[...] = split_dot(spread[...], unpack(m))
        inv[...] = split_dot(spread[...], unpack(s))
        return copies

    activate(x, mean1, inv1, vec[0:1, :], vec[1:2, :], s1, 0)
    load1.wait()

    def emit_first(at, total):
        y1[at, :] = total + vec[2:3, :]

    convolve(s1, k1, emit_first)
    sent = statistics(y1, mean2, inv2, 0)
    activate(y1, mean2, inv2, vec[3:4, :], vec[4:5, :], s2, 1)
    load2.wait()

    def emit_second(at, total):
        hid[at, :] = total + vec[5:6, :] + x[at, :].astype(F32)

    convolve(s2, k2, emit_second)
    sent = sent + statistics(hid, mean3, inv3, 1)
    gain3, bias3 = vec[6:7, :], vec[7:8, :]

    def last(i, _):
        at = pl.ds(i * 16 * UNIT, 16 * UNIT)
        value = (hid[at, :] - over_cells(mean3, i)) * over_cells(inv3, i)
        u[at, :] = (value * gain3 + bias3).astype(B16)
        return 0

    lax.fori_loop(0, cells // 16, last, 0)
    for cp in sent:
        cp.wait_send()


def resnet_forward_call(n, dims, keep, x, pick, spread, cnt, mean1, inv1, masks, vec, whole):
    canvases, rows, width = dims
    px = canvases * rows * width
    cells = px // UNIT
    stats = canvases * CROPS
    saved = [
        ((px, C), F32),
        ((canvases, rows + 2, width, 3 * C), B16),
        ((canvases, rows + 2, width, 3 * C), B16),
        ((cells, C), F32),
        ((cells, C), F32),
        ((cells, C), F32),
        ((cells, C), F32),
    ]
    main = [((px, C), F32), ((px, C), B16)]
    outs = main + (saved if keep else [])
    scratch = [] if keep else [pltpu.VMEM(*s) for s in saved]
    return pl.pallas_call(
        functools.partial(resnet_forward_kernel, n, dims, keep),
        out_shape=[sds(*s) for s in outs],
        in_specs=[vmem] * 11 + [anyw],
        out_specs=[vmem] * len(outs),
        scratch_shapes=scratch
        + [
            pltpu.VMEM((9 * C, C), B16),
            pltpu.VMEM((9 * C, C), B16),
            pltpu.VMEM((2, 2, canvases, width, C), B16),
            pltpu.VMEM((2, n, stats, LANES), F32),
            pltpu.VMEM((cells, C), F32),
            pltpu.VMEM((cells, C), F32),
            pltpu.SemaphoreType.DMA((2,)),
            pltpu.SemaphoreType.DMA((2, n)),
            pltpu.SemaphoreType.DMA((2, n)),
            pltpu.SemaphoreType.DMA((2, 2)),
            pltpu.SemaphoreType.DMA((2, 2)),
        ],
        compiler_params=params_of(2 if keep else 3),
        name="resnet_forward" if keep else "resnet_again",
    )(x, pick, spread, cnt, mean1, inv1, *masks, vec, whole)


def attention_kernel(keep, chunk, block, ua, key_ids, query_ids, offsets, dz, vec, whole, *refs):
    total = ua.shape[0] * ua.shape[1]
    queries = query_ids.shape[0]
    segment = ua.shape[1]
    scale = C ** (-0.5)
    if keep:
        out, dup, dw, dvec = refs[:4]
        u, w, k, v, pbuf, sbuf, q, dout, dq, usem, wsem = refs[4:]
    else:
        out = refs[0]
        u, w, k, v, usem, wsem = refs[1:]
    load_w = pltpu.make_async_copy(whole.at[pl.ds(18 * C, 4 * C)], w, wsem.at[0])
    load_w.start()
    blocks = ua.shape[0]
    loads = [
        pltpu.make_async_copy(ua.at[i], u.at[pl.ds(i * segment, segment)], usem.at[i])
        for i in range(blocks)
    ]
    for cp in loads:
        cp.start()
    load_w.wait()
    for cp in loads:
        cp.wait()
    nt = (((1,), (1,)), ((), ()))
    tn = (((0,), (0,)), ((), ()))

    def project(i, _):
        at = pl.ds(pl.multiple_of(i * chunk, chunk), chunk)
        piece = u[at, :]
        k[at, :] = jnp.dot(piece, w[C : 2 * C, :], preferred_element_type=F32).astype(B16)
        v[at, :] = (
            jnp.dot(piece, w[2 * C : 3 * C, :], preferred_element_type=F32) + vec[9:10, :]
        ).astype(B16)
        return 0

    lax.fori_loop(0, total // chunk, project, 0)
    per = segment // block

    def place(i):
        return pl.multiple_of(offsets[i // per] + lax.rem(i, per) * block, block)

    def attend(i, _):
        at = pl.ds(pl.multiple_of(i * block, block), block)
        uq = u[pl.ds(place(i), block), :]
        qb = (
            jnp.dot(uq, w[0:C, :], preferred_element_type=F32) + vec[8:9, :]
        ).astype(B16)
        s = lax.dot_general(qb, k[...], nt, preferred_element_type=F32) * scale
        s = jnp.where(query_ids[at, :][:, :1] == key_ids[...], s, mask_fill)
        e = jnp.exp(s - jnp.max(s, axis=1, keepdims=True))
        p = e * (1.0 / jnp.sum(e, axis=1, keepdims=True))
        pb = p.astype(B16)
        ob = jnp.dot(pb, v[...], preferred_element_type=F32).astype(B16)
        out[at, :] = ob
        if keep:
            pbuf[at, :] = pb
            q[at, :] = qb
            do = lax.dot_general(
                dz[at, :], w[3 * C : 4 * C, :], nt, preferred_element_type=F32
            ).astype(B16)
            dout[at, :] = do
            dp = lax.dot_general(do, v[...], nt, preferred_element_type=F32)
            delta = jnp.sum(p * dp, axis=1, keepdims=True)
            ds = (p * (dp - delta)).astype(B16)
            sbuf[at, :] = ds
            dq[at, :] = (jnp.dot(ds, k[...], preferred_element_type=F32) * scale).astype(B16)
        return 0

    lax.fori_loop(0, queries // block, attend, 0)
    if not keep:
        return
    zero = jnp.zeros((C, C), F32)

    def back(i, carry):
        dwk, dwv, dbv = carry
        at = pl.ds(pl.multiple_of(i * chunk, chunk), chunk)
        dk = (
            lax.dot_general(sbuf[:, at], q[...], tn, preferred_element_type=F32) * scale
        ).astype(B16)
        dvf = lax.dot_general(pbuf[:, at], dout[...], tn, preferred_element_type=F32)
        dv = dvf.astype(B16)
        du = lax.dot_general(dk, w[C : 2 * C, :], nt, preferred_element_type=F32)
        du = du + lax.dot_general(dv, w[2 * C : 3 * C, :], nt, preferred_element_type=F32)
        dup[at, :] = du.astype(B16)
        piece = u[at, :]
        dwk = dwk + lax.dot_general(piece, dk, tn, preferred_element_type=F32)
        dwv = dwv + lax.dot_general(piece, dv, tn, preferred_element_type=F32)
        return dwk, dwv, dbv + jnp.sum(dvf, axis=0, keepdims=True)

    dwk, dwv, dbv = lax.fori_loop(0, total // chunk, back, (zero, zero, jnp.zeros((1, C), F32)))
    dw[C : 2 * C, :] = dwk.astype(B16)
    dw[2 * C : 3 * C, :] = dwv.astype(B16)
    dw[3 * C : 4 * C, :] = lax.dot_general(
        out[...], dz[...], tn, preferred_element_type=F32
    ).astype(B16)
    dwq = zero
    for s in range(2):
        where = pl.ds(pl.multiple_of(offsets[s], segment), segment)
        at = pl.ds(s * segment, segment)
        dwq = dwq + lax.dot_general(u[where, :], dq[at, :], tn, preferred_element_type=F32)
        du = lax.dot_general(dq[at, :], w[0:C, :], nt, preferred_element_type=F32)
        dup[where, :] = (dup[where, :].astype(F32) + du).astype(B16)
    dw[0:C, :] = dwq.astype(B16)
    dvec[...] = jnp.concatenate(
        [
            jnp.sum(dq[...].astype(F32), axis=0, keepdims=True),
            dbv,
            jnp.sum(dz[...].astype(F32), axis=0, keepdims=True),
            jnp.zeros((5, C), F32),
        ],
        axis=0,
    )


def attention_call(keep, ua, key_ids, query_ids, offsets, dz, vec, whole):
    blocks, segment, _ = ua.shape
    total = blocks * segment
    queries = query_ids.shape[0]
    block = min(256, segment)
    chunk = 512
    outs = [sds((queries, C), B16)]
    scratch = [
        pltpu.VMEM((total, C), B16),
        pltpu.VMEM((4 * C, C), B16),
        pltpu.VMEM((total, C), B16),
        pltpu.VMEM((total, C), B16),
    ]
    if keep:
        outs += [sds((total, C), B16), sds((4 * C, C), B16), sds((8, C), F32)]
        scratch += [
            pltpu.VMEM((queries, total), B16),
            pltpu.VMEM((queries, total), B16),
            pltpu.VMEM((queries, C), B16),
            pltpu.VMEM((queries, C), B16),
            pltpu.VMEM((queries, C), B16),
        ]
    return pl.pallas_call(
        functools.partial(attention_kernel, keep, chunk, block),
        out_shape=outs,
        in_specs=[anyw, vmem, vmem, smem, vmem, vmem, anyw],
        out_specs=[vmem] * len(outs),
        scratch_shapes=scratch
        + [pltpu.SemaphoreType.DMA((blocks,)), pltpu.SemaphoreType.DMA((1,))],
        compiler_params=params_of(),
        name="attention" if keep else "attention_again",
    )(ua, key_ids, query_ids, offsets, dz, vec, whole)


def other_core(h):
    return h + 1 - 2 * lax.rem(h, 2)


def gather_kernel(n, u, ua, lsem, send, recv):
    me = lax.axis_index("height")
    half = n // 2
    mine = me // half
    base = mine * half
    core = lax.rem(me, 2)
    partner = lax.rem(me + half, n)
    sibling = other_core(me)
    mates = half // 2
    seat = (me - base) // 2

    def mate(j):
        return base + core + 2 * lax.rem(seat + j, mates)

    barrier = pltpu.get_barrier_semaphore()
    peers = [partner, sibling] + [mate(j) for j in range(1, mates)]
    for p in peers:
        pl.semaphore_signal(barrier, inc=1, device_id={"height": p}, device_id_type=MESH)
    pl.semaphore_wait(barrier, len(peers))
    count = [0]
    started = []

    def push(src, slot, to):
        cp = pltpu.make_async_remote_copy(
            src_ref=src, dst_ref=ua.at[slot], send_sem=send.at[count[0]], recv_sem=recv.at[slot],
            device_id={"height": to}, device_id_type=MESH)
        count[0] += 1
        cp.start()
        started.append(cp)

    def arrived(slot):
        pltpu.make_async_remote_copy(
            src_ref=u.at[0], dst_ref=ua.at[slot], send_sem=send.at[0], recv_sem=recv.at[slot],
            device_id={"height": partner}, device_id_type=MESH).wait_recv()

    own = pltpu.make_async_copy(u.at[mine], ua.at[me], lsem.at[0])
    own.start()
    push(u.at[1 - mine], me, partner)
    for j in range(1, mates):
        push(u.at[mine], me, mate(j))
    push(u.at[mine], me, sibling)
    arrived(partner)
    for j in range(1, mates):
        push(ua.at[partner], partner, mate(j))
    push(ua.at[partner], partner, sibling)
    for j in range(1, mates):
        friend = base + core + 2 * lax.rem(seat + mates - j, mates)
        far = lax.rem(friend + half, n)
        arrived(friend)
        push(ua.at[friend], friend, sibling)
        arrived(far)
        push(ua.at[far], far, sibling)
    arrived(sibling)
    arrived(lax.rem(sibling + half, n))
    for j in range(1, mates):
        friend = base + (1 - core) + 2 * lax.rem(seat + mates - j, mates)
        arrived(friend)
        arrived(lax.rem(friend + half, n))
    own.wait()
    for cp in started:
        cp.wait_send()


def gather_call(n, cid, u):
    half = n // 2
    sends = 2 * (half // 2) + 1 + 2 * (half // 2 - 1) + 1
    return pl.pallas_call(
        functools.partial(gather_kernel, n),
        out_shape=sds((n,) + u.shape[1:], B16),
        in_specs=[anyw],
        out_specs=anyw,
        scratch_shapes=[
            pltpu.SemaphoreType.DMA((1,)),
            pltpu.SemaphoreType.DMA((sends,)),
            pltpu.SemaphoreType.DMA((n,)),
        ],
        compiler_params=params_of(cid),
        name="gather_u",
    )(u)


def scatter_kernel(n, dup, out, from_sib, from_mate, mine_sum, from_partner, lsem, send, recv):
    me = lax.axis_index("height")
    half = n // 2
    mine = me // half
    base = mine * half
    core = lax.rem(me, 2)
    partner = lax.rem(me + half, n)
    sibling = other_core(me)
    mates = half // 2
    seat = (me - base) // 2
    barrier = pltpu.get_barrier_semaphore()

    def mate(j, c=core):
        return base + c + 2 * lax.rem(seat + j, mates)

    peers = [partner, sibling] + [mate(j) for j in range(1, mates)]
    for p in peers:
        pl.semaphore_signal(barrier, inc=1, device_id={"height": p}, device_id_type=MESH)
    pl.semaphore_wait(barrier, len(peers))
    order = [(j, far) for j in range(1, mates) for far in (1, 0)] + [(0, 1), (0, 0)]

    def rows_of(j, far, c):
        owner = mate(j, c)
        return lax.rem(owner + half, n) if far else owner

    sib = []
    for t, (j, far) in enumerate(order):
        cp = pltpu.make_async_remote_copy(
            src_ref=dup.at[rows_of(j, far, 1 - core)], dst_ref=from_sib.at[t],
            send_sem=send.at[t], recv_sem=recv.at[t],
            device_id={"height": sibling}, device_id_type=MESH)
        cp.start()
        sib.append(cp)
    base_sem = len(order)
    out_copies = []
    for t, (j, far) in enumerate(order):
        sib[t].wait_recv()
        block = rows_of(j, far, core)
        if j > 0:
            mine_sum[t] = (dup[block].astype(F32) + from_sib[t].astype(F32)).astype(B16)
            at = (j - 1) * 2 + far
            cp = pltpu.make_async_remote_copy(
                src_ref=mine_sum.at[t], dst_ref=from_mate.at[at],
                send_sem=send.at[base_sem + at], recv_sem=recv.at[base_sem + at],
                device_id={"height": mate(j)}, device_id_type=MESH)
            cp.start()
            out_copies.append(cp)
    t_far, t_own = len(order) - 2, len(order) - 1
    total = dup[partner].astype(F32) + from_sib[t_far].astype(F32)
    for j in range(1, mates):
        at = (j - 1) * 2 + 1
        pltpu.make_async_remote_copy(
            src_ref=mine_sum.at[0], dst_ref=from_mate.at[at], send_sem=send.at[0],
            recv_sem=recv.at[base_sem + at], device_id={"height": sibling},
            device_id_type=MESH).wait_recv()
        total = total + from_mate[at].astype(F32)
    mine_sum[t_far] = total.astype(B16)
    last = base_sem + 2 * (mates - 1)
    home = pltpu.make_async_remote_copy(
        src_ref=mine_sum.at[t_far], dst_ref=from_partner, send_sem=send.at[last],
        recv_sem=recv.at[last], device_id={"height": partner}, device_id_type=MESH)
    home.start()
    total = dup[me].astype(F32) + from_sib[t_own].astype(F32)
    for j in range(1, mates):
        at = (j - 1) * 2
        pltpu.make_async_remote_copy(
            src_ref=mine_sum.at[0], dst_ref=from_mate.at[at], send_sem=send.at[0],
            recv_sem=recv.at[base_sem + at], device_id={"height": sibling},
            device_id_type=MESH).wait_recv()
        total = total + from_mate[at].astype(F32)
    out[mine] = total
    home.wait_recv()
    out[1 - mine] = from_partner[...].astype(F32)
    for cp in sib + out_copies + [home]:
        cp.wait_send()


def scatter_call(n, cid, dup):
    half = n // 2
    mates = half // 2
    copies = 2 * mates + 2 * (mates - 1) + 1
    seg = dup.shape[1:]
    return pl.pallas_call(
        functools.partial(scatter_kernel, n),
        out_shape=sds((2,) + seg, F32),
        in_specs=[vmem],
        out_specs=vmem,
        scratch_shapes=[
            pltpu.VMEM((2 * mates,) + seg, B16),
            pltpu.VMEM((max(2 * (mates - 1), 1),) + seg, B16),
            pltpu.VMEM((2 * mates,) + seg, B16),
            pltpu.VMEM(seg, B16),
            pltpu.SemaphoreType.DMA((1,)),
            pltpu.SemaphoreType.DMA((copies,)),
            pltpu.SemaphoreType.DMA((copies,)),
        ],
        compiler_params=params_of(cid),
        name="scatter_du",
    )(dup)


def resnet_backward_kernel(n, dims, cot, du, hid, y1, x, mean1, inv1, mean2, inv2, mean3, inv3, s1, s2, pick,
                           spread, div, col_l, col_r, row_u, row_d, vec, whole, datt, igrad, grads, dvec,
                           dw1, dw2, k, dh, d3, low, low_u, low_d, part, norm, halo, buf, tmp_a, tmp_b, ksem, send,
                           recv, hsend, hrecv):
    canvases, rows, width = dims
    px = canvases * rows * width
    cells = px // UNIT
    plane = rows * width
    nt = (((1,), (1,)), ((), ()))
    tn = (((0,), (0,)), ((), ()))
    load2 = pltpu.make_async_copy(whole.at[pl.ds(9 * C, 9 * C)], k, ksem.at[0])
    load1 = pltpu.make_async_copy(whole.at[pl.ds(0, 9 * C)], k, ksem.at[1])
    load2.start()
    out_att = pltpu.make_async_copy(datt, grads.at[pl.ds(18 * C, 4 * C)], ksem.at[2])
    out_two = pltpu.make_async_copy(dw2, grads.at[pl.ds(9 * C, 9 * C)], ksem.at[3])
    out_one = pltpu.make_async_copy(dw1, grads.at[pl.ds(0, 9 * C)], ksem.at[4])
    out_att.start()
    greet(n)
    zero_row = jnp.zeros((1, C), F32)

    def pixels(i):
        return pl.ds(i * 16 * UNIT, 16 * UNIT)

    def norm_sums(grad_of, source, mean, inv, gain):
        def body(i, carry):
            dg, db = carry
            at = pixels(i)
            unit = (source[at, :].astype(F32) - over_cells(mean, i)) * over_cells(inv, i)
            d = grad_of(i, unit)
            norm[at, :] = unit
            e = d * gain
            part[at, :] = e
            cross = d * unit
            here = pl.ds(i * 16, 16)
            tmp_a[here, :] = jnp.sum(e.reshape(16, UNIT, C), axis=1)
            tmp_b[here, :] = jnp.sum((cross * gain).reshape(16, UNIT, C), axis=1)
            return (dg + jnp.sum(cross, axis=0, keepdims=True), db + jnp.sum(d, axis=0, keepdims=True))

        dg, db = lax.fori_loop(0, cells // 16, body, (zero_row, zero_row))
        packed = pack([group_totals(pick, tmp_a[...]), group_totals(pick, tmp_b[...])])
        return packed, dg, db

    def send_sums(packed, rnd):
        buf[rnd, 0] = packed
        copies = spread_copies(n, buf, send, recv, rnd)
        for cp in copies:
            cp.start()
        return copies

    def norm_finish(copies, rnd, inv, emit):
        for cp in copies:
            cp.wait_recv()
        gathered = jnp.sum(buf[rnd], axis=0) / div[...]
        tmp_a[...] = split_dot(spread[...], unpack(gathered))
        tmp_b[...] = split_dot(spread[...], unpack(shift_down(gathered, 1)))

        def body(i, _):
            at = pixels(i)
            emit(i, over_cells(inv, i) * (part[at, :] - over_cells(tmp_a, i) - norm[at, :] * over_cells(tmp_b, i)))
            return 0

        lax.fori_loop(0, cells // 16, body, 0)

    def spread_rows(rnd):
        def row_at(v, r):
            return pl.ds(pl.multiple_of((v * rows + r) * width, width), width)

        def one(i, _):
            v, r = i // rows, lax.rem(i, rows)
            d3[v, r + 1] = shift_columns(low[row_at(v, r), :].astype(F32), col_l[v, r + 1], col_r[v, r + 1])
            return 0

        lax.fori_loop(0, canvases * rows, one, 0)
        mid = pl.ds(C, C)
        up, down = halo_copies(n, d3.at[:, 1, :, mid], d3.at[:, rows, :, mid], halo.at[rnd],
                               hsend.at[rnd], hrecv.at[rnd])
        start_halo(n, up, down)
        return up, down

    def finish_rows(up, down, rnd):
        wait_halo(n, up, down, halo.at[rnd], 0.0)
        for v in range(canvases):
            for side, r in ((0, 0), (1, rows + 1)):
                d3[v, r] = shift_columns(halo[rnd, side, v].astype(F32), col_l[v, r], col_r[v, r])

    def convolve_back(emit):
        def body(v, _):
            at = pl.ds(pl.multiple_of(v * plane, plane), plane)
            total = None
            for dr in (1, 0, 2):
                acc = None
                for dc in range(3):
                    tap = 3 * (2 - dr) + (2 - dc)
                    lhs = d3[v, dr : dr + rows, :, dc * C : (dc + 1) * C].reshape(plane, C)
                    term = lax.dot_general(lhs, k[tap * C : (tap + 1) * C, :], nt, preferred_element_type=F32)
                    acc = term if acc is None else acc + term
                if dr == 0:
                    acc = acc * wide(row_u[at, :])
                if dr == 2:
                    acc = acc * wide(row_d[at, :])
                total = acc if total is None else total + acc
            emit(at, total)
            return 0

        lax.fori_loop(0, canvases, body, 0)

    def mask_rows():
        def body(i, _):
            at = pixels(i)
            value = low[at, :].astype(F32)
            low_u[at, :] = (value * wide(row_u[at, :])).astype(B16)
            low_d[at, :] = (value * wide(row_d[at, :])).astype(B16)
            return 0

        lax.fori_loop(0, cells // 16, body, 0)

    def weight_grad(source, dest):
        for dr, grad in ((0, low_u), (1, low), (2, low_d)):
            def body(dc, _):
                acc = None
                for v in range(canvases):
                    lhs = source[v, dr : dr + rows, :, pl.ds(pl.multiple_of(dc * C, C), C)].reshape(plane, C)
                    term = lax.dot_general(
                        lhs, grad[v * plane : (v + 1) * plane, :], tn, preferred_element_type=F32)
                    acc = term if acc is None else acc + term
                dest[pl.ds(pl.multiple_of((3 * dr + dc) * C, C), C), :] = acc.astype(B16)
                return 0

            lax.fori_loop(0, 3, body, 0)

    packed, dg3, db3 = norm_sums(lambda i, unit: du[pixels(i), :], hid, mean3, inv3, vec[6:7, :])
    sent = send_sums(packed, 0)

    def emit_hidden(i, value):
        at = pixels(i)
        total = cot[at, :].astype(F32) + value
        dh[at, :] = total
        low[at, :] = total.astype(B16)

    norm_finish(sent, 0, inv3, emit_hidden)
    up, down = spread_rows(0)
    mask_rows()
    dc2 = jnp.sum(low[...].astype(F32), axis=0, keepdims=True)
    finish_rows(up, down, 0)
    load2.wait()

    def emit_part(at, total):
        part[at, :] = total

    convolve_back(emit_part)
    load1.start()
    gain2, bias2 = vec[3:4, :], vec[4:5, :]

    def grad_two(i, unit):
        return part[pixels(i), :] * silu_slope(unit * gain2 + bias2)

    packed, dg2, db2 = norm_sums(grad_two, y1, mean2, inv2, gain2)
    more = send_sums(packed, 1)
    weight_grad(s2, dw2)
    out_two.start()

    def emit_low(i, value):
        low[pixels(i), :] = value.astype(B16)

    norm_finish(more, 1, inv2, emit_low)
    sent = sent + more
    up, down = spread_rows(1)
    mask_rows()
    dc1 = jnp.sum(low[...].astype(F32), axis=0, keepdims=True)
    weight_grad(s1, dw1)
    out_one.start()
    finish_rows(up, down, 1)
    load1.wait()
    convolve_back(emit_part)
    gain1, bias1 = vec[0:1, :], vec[1:2, :]

    def grad_one(i, unit):
        return part[pixels(i), :] * silu_slope(unit * gain1 + bias1)

    packed, dg1, db1 = norm_sums(grad_one, x, mean1, inv1, gain1)
    more = send_sums(packed, 2)
    dvec[...] = jnp.concatenate([dg1, db1, dc1, dg2, db2, dc2, dg3, db3], axis=0)

    def emit_input(i, value):
        igrad[pixels(i), :] = dh[pixels(i), :] + value

    norm_finish(more, 2, inv1, emit_input)
    sent = sent + more
    out_att.wait()
    out_two.wait()
    out_one.wait()
    for cp in sent:
        cp.wait_send()


def resnet_backward_call(n, dims, cid, cot, du, hid, y1, x, norms, s1, s2, pick, spread, div, masks, vec, whole,
                         datt):
    canvases, rows, width = dims
    px = canvases * rows * width
    cells = px // UNIT
    stats = canvases * CROPS
    return pl.pallas_call(
        functools.partial(resnet_backward_kernel, n, dims),
        out_shape=[sds((px, C), F32), sds((22 * C, C), B16), sds((8, C), F32)],
        in_specs=[vmem] * 21 + [anyw, anyw],
        out_specs=[vmem, anyw, vmem],
        scratch_shapes=[
            pltpu.VMEM((9 * C, C), B16),
            pltpu.VMEM((9 * C, C), B16),
            pltpu.VMEM((9 * C, C), B16),
            pltpu.VMEM((px, C), F32),
            pltpu.VMEM((canvases, rows + 2, width, 3 * C), B16),
            pltpu.VMEM((px, C), B16),
            pltpu.VMEM((px, C), B16),
            pltpu.VMEM((px, C), B16),
            pltpu.VMEM((px, C), F32),
            pltpu.VMEM((px, C), F32),
            pltpu.VMEM((2, 2, canvases, width, C), B16),
            pltpu.VMEM((3, n, stats, LANES), F32),
            pltpu.VMEM((cells, C), F32),
            pltpu.VMEM((cells, C), F32),
            pltpu.SemaphoreType.DMA((5,)),
            pltpu.SemaphoreType.DMA((3, n)),
            pltpu.SemaphoreType.DMA((3, n)),
            pltpu.SemaphoreType.DMA((2, 2)),
            pltpu.SemaphoreType.DMA((2, 2)),
        ],
        compiler_params=params_of(cid),
        name="resnet_backward",
    )(cot, du, hid, y1, x, *norms, s1, s2, pick, spread, div, *masks, vec, whole, datt)


class Grid:
    def __init__(self, columns, n):
        self.columns, self.n, self.seats = columns, n, n // 2
        self.phases = columns.bit_length() - 1
        self.c = lax.axis_index("canvas")
        self.h = lax.axis_index("height")
        self.seat, self.core = self.h // 2, lax.rem(self.h, 2)
        flips = [
            (1 - 2 * lax.rem(self.c // 2**t, 2)) * 2**t for t in range(self.phases)
        ]
        last = self.phases - 1
        self.flips = [
            (1 - self.core) * flips[last - k] + self.core * flips[k] for k in range(self.phases)
        ]
        self.other_flips = [
            self.core * flips[last - k] + (1 - self.core) * flips[k] for k in range(self.phases)
        ]

    def column(self, e, flips=None):
        flips = self.flips if flips is None else flips
        col = self.c
        for k in range(self.phases):
            if (e >> k) & 1:
                col = col + flips[k]
        return col

    def mate(self, k):
        return {"canvas": self.c + self.flips[k], "height": self.h}

    def sibling(self):
        return {"canvas": self.c, "height": 2 * self.seat + 1 - self.core}

    def beside(self, step):
        return {"canvas": self.c, "height": self.h + 2 * step}

    def greet(self):
        barrier = pltpu.get_barrier_semaphore()
        for d in range(1, self.n):
            pl.semaphore_signal(
                barrier, inc=1, device_id={"canvas": self.c, "height": lax.rem(self.h + d, self.n)},
                device_id_type=MESH)
        for k in range(self.phases):
            pl.semaphore_signal(barrier, inc=1, device_id=self.mate(k), device_id_type=MESH)
        pl.semaphore_wait(barrier, self.n - 1 + self.phases)


def remote(src, dst, send, recv, to):
    return pltpu.make_async_remote_copy(
        src_ref=src, dst_ref=dst, send_sem=send, recv_sem=recv, device_id=to, device_id_type=MESH)


def lowest_bit(e):
    return (e & -e).bit_length() - 1


def spread_blocks(grid, fresh, whole, own_sem, zsend, msend, ssend, recv, srecv):
    g = grid
    seats, phases = g.seats, g.phases
    own = pltpu.make_async_copy(fresh, whole.at[g.c, g.seat, g.core], own_sem)
    own.start()

    def slot(e, seat):
        return whole.at[g.column(e), seat, g.core]

    def forward(e, seat, src, start):
        k_top = phases if e == 0 else lowest_bit(e)
        for k in range(k_top - 1, -1, -1):
            cp = remote(src, slot(e, seat), msend.at[k, e, seat], recv.at[e | (1 << k), seat], g.mate(k))
            cp.start() if start else cp.wait_send()
        cp = remote(src, slot(e, seat), ssend.at[e, seat], srecv.at[e, seat], g.sibling())
        cp.start() if start else cp.wait_send()

    def along(seat, step, src, start):
        cp = remote(src, slot(0, seat), zsend.at[(step + 1) // 2, seat], recv.at[0, seat], g.beside(step))
        cp.start() if start else cp.wait_send()

    def line(seat, src, start):
        @pl.when((seat <= g.seat) & (g.seat < seats - 1))
        def _():
            along(seat, 1, src, start)

        @pl.when((seat >= g.seat) & (g.seat > 0))
        def _():
            along(seat, -1, src, start)

    def arrive(e, seat):
        remote(fresh, slot(e, seat), ssend.at[0, 0], recv.at[e, seat], g.sibling()).wait_recv()

    early = [e for e in range(1, 2**phases) if lowest_bit(e) > 0]
    early.sort(key=lambda e: -lowest_bit(e))
    late = [e for e in range(1, 2**phases) if lowest_bit(e) == 0]

    def handle(e, seat):
        arrive(e, seat)
        if e == 0:
            line(seat, slot(0, seat), True)
        forward(e, seat, slot(e, seat), True)

    def both_sides(d, todo):
        for side in (-1, 1):
            seat = g.seat + side * d

            @pl.when((seat >= 0) & (seat < seats))
            def _():
                for e in todo:
                    handle(e, seat)

    line(g.seat, fresh, True)
    forward(0, g.seat, fresh, True)
    for e in early:
        handle(e, g.seat)

    def further(d, _):
        both_sides(d, [0] + early)
        return 0

    lax.fori_loop(1, seats, further, 0)
    for e in late:
        handle(e, g.seat)

    def finish(d, _):
        both_sides(d, late)
        return 0

    lax.fori_loop(1, seats, finish, 0)

    def drain(seat, _):
        for e in range(2**phases):
            remote(fresh, whole.at[g.column(e, g.other_flips), seat, 1 - g.core], ssend.at[0, 0],
                   srecv.at[e, seat], g.sibling()).wait_recv()
            forward(e, seat, slot(e, seat), False)
        line(seat, slot(0, seat), False)
        return 0

    lax.fori_loop(0, seats, drain, 0)
    own.wait()


def spread_scratch(columns, n):
    seats, phases = n // 2, columns.bit_length() - 1
    dma = pltpu.SemaphoreType.DMA
    return [
        dma((1,)),
        dma((2, seats)),
        dma((phases, columns, seats)),
        dma((columns, seats)),
        dma((columns, seats)),
        dma((columns, seats)),
    ]


def spread_kernel(columns, n, block, whole, fresh, own, zsend, msend, ssend, recv, srecv):
    grid = Grid(columns, n)
    fresh[...] = block[...].astype(B16)
    grid.greet()
    spread_blocks(grid, fresh, whole, own.at[0], zsend, msend, ssend, recv, srecv)


def spread_call(columns, n, cid, block):
    return pl.pallas_call(
        functools.partial(spread_kernel, columns, n),
        out_shape=sds((columns, n // 2, 2) + block.shape, B16),
        in_specs=[vmem],
        out_specs=anyw,
        scratch_shapes=[pltpu.VMEM(block.shape, B16)] + spread_scratch(columns, n),
        compiler_params=params_of(cid),
        name="spread_weights",
    )(block)


def adam_update(current, gradient, moment_one, moment_two, learn_rate):
    first_new = 0.5 * moment_one + 0.5 * gradient
    second_new = 0.9 * moment_two + 0.1 * gradient * gradient
    first_hat = first_new / (1.0 - 0.5**STEP)
    second_hat = second_new / (1.0 - 0.9**STEP)
    return (
        current - learn_rate * first_hat / (jnp.sqrt(second_hat) + adam_epsilon),
        first_new,
        second_new,
    )


def step_kernel(columns, n, grads, w, m, s, dvec, vw, vm, vs, new_w, new_m, new_s, new_vw, new_vm, new_vs, whole,
                acc, sib, got, up, down, fresh, vbuf, vtrade, lsem, gsend, grecv, psend, precv, usend, urecv,
                vsend, vrecv, tsend, trecv, own, zsend, msend, ssend, recv, srecv):
    g = Grid(columns, n)
    seats, phases = g.seats, g.phases
    slots = 2**phases
    order = sorted(range(slots), key=lambda e: (lowest_bit(e) if e else phases, e == (e & -e)))
    loads = []
    for e in order:
        cp = pltpu.make_async_copy(grads.at[g.column(e), :, g.core], acc.at[e], lsem.at[e])
        cp.start()
        loads.append(cp)

    @pl.when(g.seat == 0)
    def _():
        up[...] = jnp.zeros(up.shape, B16)

    @pl.when(g.seat == seats - 1)
    def _():
        down[...] = jnp.zeros(down.shape, B16)

    vbuf[g.h] = dvec[...]
    g.greet()
    sib_copies = []
    for e in order:
        cp = remote(grads.at[g.column(e, g.other_flips), :, 1 - g.core], sib.at[e], gsend.at[e], grecv.at[e],
                    g.sibling())
        cp.start()
        sib_copies.append(cp)

    def vector_copy(d):
        src = lax.rem(g.h + d, n)
        return remote(vbuf.at[g.h], vbuf.at[g.h], vsend.at[d], vrecv.at[g.h],
                      {"canvas": g.c, "height": src})

    def vector_arrival(d):
        src = lax.rem(g.h + d, n)
        return remote(vbuf.at[src], vbuf.at[src], vsend.at[d], vrecv.at[src],
                      {"canvas": g.c, "height": src})

    for d in range(1, n):
        vector_copy(d).start()

    def local(e, seat, below):
        total = acc[e, seat].astype(F32) + sib[e, seat].astype(F32)
        for k in range(below):
            total = total + got[k, e >> (k + 1), seat].astype(F32)
        return total

    def in_turn(i):
        even = 1 - lax.rem(i, 2)
        return (i // 2) * even + (1 - even) * (seats - 1 - i // 2)

    def phase_copy(k, e, seat):
        return remote(acc.at[e, seat], got.at[k, e >> (k + 1), seat], psend.at[k, e >> (k + 1), seat],
                      precv.at[k, e >> (k + 1), seat], g.mate(k))

    ready = 0
    for e in order:
        loads[ready].wait()
        sib_copies[ready].wait_recv()
        ready += 1
        if e == 0:
            break
        k = lowest_bit(e)

        def one(i, _):
            seat = in_turn(i)
            for q in range(k):
                phase_copy(q, e | (1 << q), seat).wait_recv()
            acc[e, seat] = local(e, seat, k).astype(B16)
            phase_copy(k, e, seat).start()
            return 0

        lax.fori_loop(0, seats, one, 0)

    for d in range(1, n):
        vector_arrival(d).wait_recv()
    vtrade[0, 0] = jnp.sum(vbuf[...], axis=0)
    for k in range(phases):
        cp = remote(vtrade.at[k, 0], vtrade.at[k, 1], tsend.at[k], trecv.at[k], g.mate(k))
        cp.start()
        cp.wait_recv()
        vtrade[k + 1, 0] = vtrade[k, 0] + vtrade[k, 1]
    new_vw[...], new_vm[...], new_vs[...] = adam_update(vw[...], vtrade[phases, 0], vm[...], vs[...], vector_rate)

    def line_copy(step, seat):
        box = up if step > 0 else down
        at = (step + 1) // 2
        return remote(acc.at[0, seat], box.at[seat], usend.at[at, seat], urecv.at[at, seat], g.beside(step))

    def own_column(i, _):
        seat = in_turn(i)
        for q in range(phases):
            phase_copy(q, 1 << q, seat).wait_recv()

        @pl.when(seat > g.seat)
        def _():
            @pl.when(g.seat > 0)
            def _():
                line_copy(1, seat).wait_recv()

            acc[0, seat] = (local(0, seat, phases) + up[seat].astype(F32)).astype(B16)
            line_copy(1, seat).start()

        @pl.when(seat < g.seat)
        def _():
            @pl.when(g.seat < seats - 1)
            def _():
                line_copy(-1, seat).wait_recv()

            acc[0, seat] = (local(0, seat, phases) + down[seat].astype(F32)).astype(B16)
            line_copy(-1, seat).start()

        return 0

    lax.fori_loop(0, seats, own_column, 0)

    @pl.when(g.seat > 0)
    def _():
        line_copy(1, g.seat).wait_recv()

    @pl.when(g.seat < seats - 1)
    def _():
        line_copy(-1, g.seat).wait_recv()

    total = local(0, g.seat, phases) + up[g.seat].astype(F32) + down[g.seat].astype(F32)
    next_w, new_m[...], new_s[...] = adam_update(w[...], total, m[...], s[...], matrix_rate)
    new_w[...] = next_w
    fresh[...] = next_w.astype(B16)
    spread_blocks(g, fresh, whole, own.at[0], zsend, msend, ssend, recv, srecv)
    for cp in sib_copies:
        cp.wait_send()
    for d in range(1, n):
        vector_copy(d).wait_send()
    for k in range(phases):
        remote(vtrade.at[k, 0], vtrade.at[k, 1], tsend.at[k], trecv.at[k], g.mate(k)).wait_send()

    def drain(seat, _):
        for e in range(1, slots):
            phase_copy(lowest_bit(e), e, seat).wait_send()

        @pl.when(seat > g.seat)
        def _():
            line_copy(1, seat).wait_send()

        @pl.when(seat < g.seat)
        def _():
            line_copy(-1, seat).wait_send()

        return 0

    lax.fori_loop(0, seats, drain, 0)


def step_call(columns, n, cid, grads, w, m, s, dvec, vw, vm, vs):
    seats, phases = n // 2, columns.bit_length() - 1
    block = w.shape
    half = max(columns // 2, 1)
    dma = pltpu.SemaphoreType.DMA
    return pl.pallas_call(
        functools.partial(step_kernel, columns, n),
        out_shape=[sds(block, F32)] * 3 + [sds(vw.shape, F32)] * 3 + [sds((columns, seats, 2) + block, B16)],
        in_specs=[anyw] + [vmem] * 7,
        out_specs=[vmem] * 6 + [anyw],
        scratch_shapes=[
            pltpu.VMEM((columns, seats) + block, B16),
            pltpu.VMEM((columns, seats) + block, B16),
            pltpu.VMEM((phases, half, seats) + block, B16),
            pltpu.VMEM((seats,) + block, B16),
            pltpu.VMEM((seats,) + block, B16),
            pltpu.VMEM(block, B16),
            pltpu.VMEM((n,) + vw.shape, F32),
            pltpu.VMEM((phases + 1, 2) + vw.shape, F32),
            dma((columns,)),
            dma((columns,)),
            dma((columns,)),
            dma((phases, half, seats)),
            dma((phases, half, seats)),
            dma((2, seats)),
            dma((2, seats)),
            dma((n,)),
            dma((n,)),
            dma((phases,)),
            dma((phases,)),
        ]
        + spread_scratch(columns, n),
        compiler_params=params_of(cid),
        name="step_weights",
    )(grads, w, m, s, dvec, vw, vm, vs)


def rounded_vectors(vectors):
    return lax.reduce_precision(vectors, exponent_bits=8, mantissa_bits=7)


def body(columns, n, latents, crop_ids, params, vectors, first_moment, second_moment, vector_first, vector_second,
         cotangent):
    canvases, rows, width, channels = latents.shape
    dims = (canvases, rows, width)
    px = canvases * rows * width
    plane = rows * width
    half = n // 2
    me = lax.axis_index("height")
    mine = me // half
    partner = lax.rem(me + half, n)
    swap = [(i, (i + half) % n) for i in range(n)]

    count = vectors.shape[0]

    def padded(value):
        return jnp.pad(value, ((0, 16 - count), (0, 0)))

    whole = spread_call(columns, n, 8, params).reshape(-1, channels)
    wide_vectors = padded(vectors)
    vec = rounded_vectors(wide_vectors)
    cell_ids = crop_ids[:, :, ::UNIT] + CROPS * jnp.arange(canvases, dtype=jnp.int32)[:, None, None]
    cell_ids = cell_ids.reshape(1, -1)
    stat = jnp.arange(canvases * CROPS, dtype=jnp.int32)[:, None]
    pick = (cell_ids == stat).astype(B16)
    spread = (cell_ids.reshape(-1, 1) == stat.reshape(1, -1)).astype(B16)
    ids = crop_ids.astype(F32)
    ids_px = jnp.broadcast_to(ids[..., None], (canvases, rows, width, LANES))
    ids_lane = jnp.pad(ids.reshape(canvases, plane), ((0, 8 - canvases), (0, 0)))
    x = latents.reshape(px, channels)
    cot = cotangent.reshape(px, channels)
    ids_all, mean1, inv1, div, cnt, *masks = layout_call(n, dims, x, pick, spread, ids_px, ids_lane)
    canvas_ids = lax.dynamic_index_in_dim(ids_all, mine, axis=1, keepdims=False)
    key_ids = canvas_ids.reshape(1, n * plane)
    query_ids = jnp.stack([canvas_ids[me], canvas_ids[partner]]).reshape(2 * plane, 1)
    query_ids = jnp.broadcast_to(query_ids, (2 * plane, LANES))
    offsets = jnp.stack([me, partner]) * plane
    cot3 = cotangent.reshape(canvases, plane, channels)
    own_cot = lax.dynamic_index_in_dim(cot3, mine, axis=0, keepdims=False)
    far_cot = lax.ppermute(
        lax.dynamic_index_in_dim(cot3, 1 - mine, axis=0, keepdims=False), "height", swap)
    dz = jnp.concatenate([own_cot, far_cot], axis=0)

    def attention_output(o, hid, weight, bias):
        o = o.reshape(2, plane, channels)
        back = lax.ppermute(o[1], "height", swap)
        ordered = jnp.where(mine == 0, jnp.stack([o[0], back]), jnp.stack([back, o[0]]))
        product = jnp.dot(ordered.reshape(px, channels), weight, preferred_element_type=F32)
        return hid + product + bias

    hid, u, y1, s1, s2, mean2, inv2, mean3, inv3 = resnet_forward_call(
        n, dims, True, x, pick, spread, cnt, mean1, inv1, masks, vec, whole)
    ua = gather_call(n, 4, u.reshape(canvases, plane, channels))
    o, dup, dw_att, dvec_att = attention_call(True, ua, key_ids, query_ids, offsets, dz, vec, whole)
    first_output = attention_output(o, hid, whole[21 * C :], vec[10])
    du = scatter_call(n, 6, dup.reshape(n, plane, channels)).reshape(px, channels)
    norms = (mean1, inv1, mean2, inv2, mean3, inv3)
    input_grad, matrix_grad, dvec = resnet_backward_call(
        n, dims, 7, cot, du, hid, y1, x, norms, s1, s2, pick, spread, div, masks, vec, whole, dw_att)
    vector_grad = jnp.concatenate([dvec, dvec_att], axis=0)
    new_params, new_first, new_second, *new_small, new_whole = step_call(
        columns, n, 9, matrix_grad.reshape((columns, half, 2) + params.shape), params, first_moment, second_moment,
        vector_grad, wide_vectors, padded(vector_first), padded(vector_second))
    new_vectors, new_vector_first, new_vector_second = [a[:count] for a in new_small]
    new_whole = new_whole.reshape(-1, channels)
    new_vec = rounded_vectors(new_small[0])
    hid2, u2 = resnet_forward_call(
        n, dims, False, x, pick, spread, cnt, mean1, inv1, masks, new_vec, new_whole)
    ua2 = gather_call(n, 5, u2.reshape(canvases, plane, channels))
    (o2,) = attention_call(False, ua2, key_ids, query_ids, offsets, dz, new_vec, new_whole)
    second_output = attention_output(o2, hid2, new_whole[21 * C :], new_vec[10])
    shape = latents.shape
    return (
        hid.reshape(shape),
        first_output.reshape(shape),
        second_output.reshape(shape),
        input_grad.reshape(shape),
        new_params,
        new_first,
        new_second,
        new_vectors,
        new_vector_first,
        new_vector_second,
    )


def solution(mesh):
    spatial = P("canvas", "height", None, None)
    owned = P(("canvas", "height"), None)
    return jax.shard_map(
        functools.partial(body, mesh.shape["canvas"], mesh.shape["height"]),
        mesh=mesh,
        in_specs=(spatial, P("canvas", "height", None), owned, P(), owned, owned, P(), P(), spatial),
        out_specs=(spatial, spatial, spatial, spatial, owned, owned, owned, P(), P(), P()),
        check_vma=False,
    )
```

time: 1850 us -> 710 us (0.38)
  Pallas kernels: 0 us -> 617 us
  waiting for transfers between devices: 571 us -> 45.2 us
  local copies, waits for them, and re-layouts: 466 us -> 19.5 us
  blocking collectives: 380 us -> 0 us
  other arithmetic: 197 us -> 6.7 us
  matrix products: 188 us -> 6.29 us
    pallas_call x0 -> x11, Pallas kernels: none -> 617 us  [the longest x1 153 us: step_call(): pl.pallas_call(functools.partial(step_kernel, columns, n), out_shape=[sds...]
    psum x13 -> x0, blocking collectives: 365 us -> none  [the longest x5 140 us: norm_forward(): centre = lax.psum(local_sum, 'height') / divisor[:, :, None]]
    reduce_scatter x3 -> x0, waiting for transfers between devices: 356 us -> none  [the longest x1 250 us: body(): lax.psum_scatter(matrix_grad, ('canvas', 'height'), scatter_dimension=0,...]
    all_gather x6 -> x0, waiting for transfers between devices: 213 us -> none  [the longest x2 118 us: attend_forward(): lax.all_gather(keys_local, 'height', axis=1, tiled=True)]
    dot_general x55 -> x2, matrix products: 188 us -> 6.29 us  [attention_output(): jnp.dot(ordered.reshape(px, channels), weight, preferred_element_type=F32)]
    another operation x9 -> x0, local copies, waits for them, and re-layouts: 134 us -> none  [the longest x4 127 us: conv_forward(): jnp.stack(pieces, axis=3)]
    mul x59 -> x0, local copies, waits for them, and re-layouts: 97.2 us -> none  [the longest x19 63.2 us: norm_forward(): normal_form = centered * inverse_pix[..., None]]
    sub x28 -> x0, local copies, waits for them, and re-layouts: 87.3 us -> none  [the longest x19 64.2 us: norm_forward(): centered = grouped - centre_pix[..., None]]
  transfers between devices with their start and end apart: 21 -> 3, of which waited for: 9 -> 2; matrix products, arithmetic and copies ran while one was open for 21% -> 1% of each run, Pallas kernels for 0% -> 25%
where the time goes in v1:
time: 710 us; the launch traced here: 704 us
  Pallas kernels  617 us (87%)
  waiting for transfers between devices  45.2 us (6%)
  local copies, waits for them, and re-layouts  19.5 us (3%)
  starting transfers between devices  8.13 us (1%)
    pallas_call x1, Pallas kernels, step_call(): pl.pallas_call(functools.partial(step_kernel, columns, n), out_shape=[sds...  153 us
    pallas_call x2, Pallas kernels, attention_call(): pl.pallas_call(functools.partial(attention_kernel, keep, chunk, block), o...  87 us
    pallas_call x2, Pallas kernels, resnet_forward_call(): pl.pallas_call(functools.partial(resnet_forward_kernel, n, dims, keep), o...  83.3 us
    pallas_call x2, Pallas kernels, gather_call(): pl.pallas_call(functools.partial(gather_kernel, n), out_shape=sds((n,) +...  79.5 us
    pallas_call x1, Pallas kernels, resnet_backward_call(): pl.pallas_call(functools.partial(resnet_backward_kernel, n, dims), out_sh...  73.4 us
    pallas_call x1, Pallas kernels, spread_call(): pl.pallas_call(functools.partial(spread_kernel, columns, n), out_shape=sd...  65.3 us
    pallas_call x1, Pallas kernels, scatter_call(): pl.pallas_call(functools.partial(scatter_kernel, n), out_shape=sds((2,) +...  47 us
    ppermute x2, waiting for transfers between devices, attention_output(): back = lax.ppermute(o[1], 'height', swap)  45.2 us
  transfers between devices with their start and end apart: 3, of which 2 were waited for; matrix products, arithmetic and copies ran while one was open for 1% of the time, Pallas kernels for 25%

profile of v1, /device:TPU:0, one launch (start us, length us, event | category | flops | bytes accessed | tf_op | source)
XLA Modules:
  0.0 704.2 jit_solution(9427717362041747449)
XLA Ops:
  0.6 0.0 copy-start.13
  0.7 1.3 dynamic-slice_bitcast_fusion.1
  2.0 4.1 collective-permute-start
  6.1 0.0 copy-done.13
  6.1 0.1 slice.46
  6.1 0.1 broadcast_add_fusion
  6.2 0.1 eq.32
  6.3 0.7 fusion.2.spread
  7.0 0.6 fusion.3.pick
  7.6 0.1 reshape.101
  7.7 0.6 pad.14.ids_lane
  8.3 1.0 broadcast_in_dim.6.ids_px
  9.3 28.7 %layout.1 = (f32[8,8,512]{2,1,0:T(8,128)}, f32[128,512]{1,0:T(8,128)}, f32[128,512]{1,0:T(8,128)}, f32[32,128]{1,0:T(8,128)}, f32[32,128]{1,0:T(8,128)}, /*index...) custom-call(bf16[1024,512]{1,0:T(8,128)(2,1)} %bitcast.51, ...), custom_call_target="tpu_custom_call" | custom-call | tf_op jit(solution)/shard_map/layout/pallas_call | solution.py:297
  38.0 0.8 dynamic-slice_bitcast_fusion.3
  38.8 0.0 copy-start.7
  38.8 65.3 %spread_weights.1 = bf16[4,4,2,352,512]{4,3,2,1,0:T(8,128)(2,1)} custom-call(f32[352,512]{1,0:T(8,128)} %w.1), custom_call_target="tpu_custom_call" | custom-call | tf_op jit(solution)/shard_map/spread_weights/pallas_call | solution.py:1212
  104.1 0.0 copy-done.7
  104.1 0.6 fusion.4
  104.7 43.4 %resnet_forward.1 = (f32[1024,512]{1,0:T(8,128)}, bf16[1024,512]{1,0:T(8,128)(2,1)}, f32[1024,512]{1,0:T(8,128)}, bf16[2,10,64,1536]{3,2,1,0:T(8,128)(2,1)}, bf1...) custom-call(bf16[1024,512]{1,0:T(8,128)(2,1)} %bitcast.52, ...), custom_call_target="tpu_custom_call" | custom-call | tf_op jit(solution)/shard_map/resnet_forward/pallas_call | solution.py:463
  148.1 0.0 copy-start.9
  148.1 0.0 copy-start.10
  148.1 39.8 %gather_u.2.ua = bf16[8,512,512]{2,1,0:T(8,128)(2,1)} custom-call(bf16[2,512,512]{2,1,0:T(8,128)(2,1)} %bitcast.66), custom_call_target="tpu_custom_call" | custom-call | tf_op jit(solution)/shard_map/gather_u/pallas_call | solution.py:705
  187.9 0.6 pad.16.vm
  188.5 0.6 pad.17.vs
  189.2 0.6 add_multiply_fusion.offsets
  189.8 1.5 constant_dynamic-slice_fusion
  191.3 0.0 collective-permute-done
  191.3 1.0 pad_maximum_fusion.dz
  192.3 1.0 broadcast_in_dim.8.query_ids
  193.3 61.7 %attention.1 = (bf16[1024,512]{1,0:T(8,128)(2,1)}, bf16[4096,512]{1,0:T(8,128)(2,1)}, bf16[2048,512]{1,0:T(8,128)(2,1)}, f32[8,512]{1,0:T(8,128)}) custom-call(bf16[8,512,512]{2,1,0:T(8,128)(2,1)} %gather_u.2.ua, f32[1,4096]{1,0:T(1,128)} %bitcast.69, f32[1024,128]{1,0:T(8,128)} %broadcast_in_dim.8.query_ids, s32[2]{0:T(128)} %add_multiply_fusion.offsets, ...), custom_call_target="tpu_custom_call" | custom-call | tf_op jit(solution)/shard_map/attention/pallas_call | solution.py:623
  255.0 47.0 %scatter_du.1 = f32[2,512,512]{2,1,0:T(8,128)} custom-call(bf16[8,512,512]{2,1,0:T(8,128)(2,1)} %bitcast.57), custom_call_target="tpu_custom_call" | custom-call | tf_op jit(solution)/shard_map/scatter_du/pallas_call | solution.py:802
  302.0 0.0 copy-start.14
  302.0 73.4 %resnet_backward.1 = (f32[1024,512]{1,0:T(8,128)}, bf16[11264,512]{1,0:T(8,128)(2,1)}, f32[8,512]{1,0:T(8,128)}) custom-call(bf16[1024,512]{1,0:T(8,128)(2,1)} %bitcast.59, f32[1024,512]{1,0:T(8,128)} %bitcast.56, f32[1024,512]{1,0:T(8,128)} %get-tuple-element.51.hid, f32[1024,512]{1,0:T(8,128)} %get-tuple-element.56.y1, bf16[1024,512]{1,0:T(8,128)(2,1)} %bitcast.53, ...), custom_call_target="tpu_custom_call" | custom-call | tf_op jit(solution)/shard_map/resnet_backward/pallas_call | solution.py:1022
  375.4 0.0 copy-done.14
  375.4 1.3 pad_maximum_fusion.1.dvec
  376.8 153.0 %step_weights.1 = (f32[352,512]{1,0:T(8,128)}, f32[352,512]{1,0:T(8,128)}, f32[352,512]{1,0:T(8,128)}, f32[16,512]{1,0:T(8,128)}, f32[16,512]{1,0:T(8,128)}, /*i...) custom-call(bf16[4,4,2,352,512]{4,3,2,1,0:T(8,128)(2,1)} %bitcast.55, f32[352,512]{1,0:T(8,128)} %w.1, f32[352,512]{1,0:T(8,128)} %m.1, ...), custom_call_target="tpu_custom_call" | custom-call | tf_op jit(solution)/shard_map/step_weights/pallas_call | solution.py:1395
  529.8 1.4 reduce_precision.7.vec
  531.1 39.9 %resnet_again.1 = (f32[1024,512]{1,0:T(8,128)}, bf16[1024,512]{1,0:T(8,128)(2,1)}) custom-call(bf16[1024,512]{1,0:T(8,128)(2,1)} %bitcast.54, bf16[32,128]{1,0:T(8,128)(2,1)} %fusion.3.pick, bf16[128,32]{1,0:T(8,128)(2,1)} %fusion.2.spread, f32[32,128]{1,0:T(8,128)} %get-tuple-element.44.cnt, f32[128,512]{1,0:T(8,128)} %get-tuple-element.45.mean1, ...), custom_call_target="tpu_custom_call" | custom-call | tf_op jit(solution)/shard_map/resnet_again/pallas_call | solution.py:463
  571.0 39.8 %gather_u.3.ua = bf16[8,512,512]{2,1,0:T(8,128)(2,1)} custom-call(bf16[2,512,512]{2,1,0:T(8,128)(2,1)} %bitcast.65), custom_call_target="tpu_custom_call" | custom-call | tf_op jit(solution)/shard_map/gather_u/pallas_call | solution.py:705
  610.8 25.3 %attention_again.1 = bf16[1024,512]{1,0:T(8,128)(2,1)} custom-call(bf16[8,512,512]{2,1,0:T(8,128)(2,1)} %gather_u.3.ua, f32[1,4096]{1,0:T(1,128)} %bitcast.70, f32[1024,128]{1,0:T(8,128)} %broadcast_in_dim.8.query_ids, s32[2]{0:T(128)} %add_multiply_fusion.offsets, bf16[1024,512]{1,0:T(8,128)(2,1)} %pad_maximum_fusion.dz, f32[16,512]{1,0:T(8,128)} %reduce_precision.7.vec, ...), custom_call_target="tpu_custom_call" | custom-call | tf_op jit(solution)/shard_map/attention_again/pallas_call | solution.py:623
  636.2 0.0 copy-start.3
  636.2 1.4 slice_bitcast_fusion
  637.5 3.9 collective-permute-start.2
  641.4 0.1 slice_bitcast_fusion.1
  641.5 0.2 collective-permute-start.1
  641.6 0.7 slice.65
  642.4 34.3 %collective-permute-done.2 = bf16[512,512]{1,0:T(8,128)(2,1)S(1)} collective-permute-done((bf16[512,512]{1,0:T(8,128)(2,1)S(1)}, bf16[512,512]{1,0:T(8,128)(2,1)S(1)}, u32[]{:S(2)}, u32[]{:S(2)}) %collective-permute-start.2) | collective-permute-done | bytes 524320 | tf_op jit(solution)/shard_map/ppermute | solution.py:1475
  676.6 11.0 %collective-permute-done.1 = bf16[512,512]{1,0:T(8,128)(2,1)S(1)} collective-permute-done((bf16[512,512]{1,0:T(8,128)(2,1)S(1)}, bf16[512,512]{1,0:T(8,128)(2,1)S(1)}, u32[]{:S(2)}, u32[]{:S(2)}) %collective-permute-start.1) | collective-permute-done | bytes 524320 | tf_op jit(solution)/shard_map/ppermute | solution.py:1475
  687.6 0.3 maximum_select_fusion
  687.9 1.3 copy-done
  689.2 3.2 add_add_fusion.1
  692.4 3.1 add_add_fusion
  695.5 1.3 copy.28
  696.8 1.0 copy-done.1
  697.8 1.3 copy.29
  699.2 0.3 copy-done.6
  699.4 0.9 copy.30
  700.3 0.0 copy-done.5
  700.3 0.9 copy.31
  701.2 0.9 copy.32
  702.0 0.6 copy.33
  702.7 0.0 copy-done.12
  702.7 0.6 copy.34
  703.3 0.6 copy.35
  (21 shorter events, 0.1 us)
Async XLA Ops:
  0.6 5.4 copy-start.13
  2.0 189.3 %collective-permute-start = (bf16[512,512]{1,0:T(8,128)(2,1)S(1)}, bf16[512,512]{1,0:T(8,128)(2,1)S(1)}, u32[]{:S(2)}, u32[]{:S(2)}) collective-permute-start(bf16[512,512]{1,0:T(8,128)(2,1)S(1)} %get-tuple-element.83), channel_id=1, source_target_pairs={{0,4},{1,5},{2,6},{3,7},{4,0},{5,1},{6,2},{7,3},{8,12},{9,13},{10,... | collective-permute-start | bytes 1572872 | tf_op jit(solution)/shard_map/ppermute | solution.py:1469
  38.8 65.3 %copy-start.7 = (f32[11,512]{1,0:T(8,128)S(1)}, f32[11,512]{1,0:T(8,128)}, u32[]{:S(2)}) copy-start(f32[11,512]{1,0:T(8,128)} %param.12) | copy-start | bytes 67588
  148.1 39.8 %copy-start.9 = (f32[11,512]{1,0:T(8,128)S(1)}, f32[11,512]{1,0:T(8,128)}, u32[]{:S(2)}) copy-start(f32[11,512]{1,0:T(8,128)} %param.15) | copy-start | bytes 67588
  148.1 40.4 %copy-start.10 = (f32[11,512]{1,0:T(8,128)S(1)}, f32[11,512]{1,0:T(8,128)}, u32[]{:S(2)}) copy-start(f32[11,512]{1,0:T(8,128)} %param.16) | copy-start | bytes 67588
  302.0 73.4 %copy-start.14 = (f32[8,512]{1,0:T(8,128)S(1)}, f32[8,512]{1,0:T(8,128)}, u32[]{:S(2)}) copy-start(f32[8,512]{1,0:T(8,128)} %get-tuple-element.67) | copy-start | bytes 49156
  636.2 5.2 copy-start.3
  637.5 39.1 %collective-permute-start.2 = (bf16[512,512]{1,0:T(8,128)(2,1)S(1)}, bf16[512,512]{1,0:T(8,128)(2,1)S(1)}, u32[]{:S(2)}, u32[]{:S(2)}) collective-permute-start(bf16[512,512]{1,0:T(8,128)(2,1)S(1)} %get-tuple-element.79), channel_id=1, source_target_pairs={{0,4},{1,5},{2,6},{3,7},{4,0},{5,1},{6,2},{7,3},{8,12},{9,13},{10,... | collective-permute-start | bytes 1572872 | tf_op jit(solution)/shard_map/ppermute | solution.py:1475
  641.5 46.1 %collective-permute-start.1 = (bf16[512,512]{1,0:T(8,128)(2,1)S(1)}, bf16[512,512]{1,0:T(8,128)(2,1)S(1)}, u32[]{:S(2)}, u32[]{:S(2)}) collective-permute-start(bf16[512,512]{1,0:T(8,128)(2,1)S(1)} %get-tuple-element.81), channel_id=1, source_target_pairs={{0,4},{1,5},{2,6},{3,7},{4,0},{5,1},{6,2},{7,3},{8,12},{9,13},{10,... | collective-permute-start | bytes 1572872 | tf_op jit(solution)/shard_map/ppermute | solution.py:1475
  687.6 1.6 copy-start
  689.2 3.2 copy-start.2
  695.5 2.3 copy-start.1
  697.8 1.6 copy-start.6
  697.8 2.5 copy-start.5
  699.4 1.7 copy-start.4
  699.4 2.6 copy-start.8
  699.4 3.2 copy-start.12
  699.4 3.8 copy-start.11

commit v2 on v1

--- a/solution.py
+++ b/solution.py
@@ -93,6 +93,10 @@
 
 def shift_down(packed, q):
     return pltpu.roll(packed, LANES - TILES * q, packed.ndim - 1)
+
+
+def no_pump():
+    return None
 
 
 def greet(n):
@@ -187,12 +191,18 @@
 
 
 def layout_kernel(n, dims, x, pick, spread, ids_px, ids_lane, ids_all, mean_c, inv_c, div, cnt,
-                  col_l, col_r, row_u, row_d, buf, idbuf, halo, tmp_a, tmp_b, send, recv, isend, irecv,
-                  hsend, hrecv):
+                  col_l, col_r, row_u, row_d, *scratch):
+    greet(n)
+    layout_body(n, dims, x, pick, spread, ids_px, ids_lane, ids_all, mean_c, inv_c, div, cnt,
+                col_l, col_r, row_u, row_d, *scratch)
+
+
+def layout_body(n, dims, x, pick, spread, ids_px, ids_lane, ids_all, mean_c, inv_c, div, cnt,
+                col_l, col_r, row_u, row_d, buf, idbuf, halo, tmp_a, tmp_b, send, recv, isend, irecv,
+                hsend, hrecv, pump=no_pump):
     canvases, rows, width = dims
     cells = canvases * rows * width // UNIT
     me = lax.axis_index("height")
-    greet(n)
     id_copies = []
     idbuf[0] = ids_lane[...]
     for d in range(1, n):
@@ -213,6 +223,7 @@
     copies = spread_copies(n, buf, send, recv, 0)
     for cp in copies:
         cp.start()
+    pump()
     wait_halo(n, up, down, halo, -1.0)
     column = lax.broadcasted_iota(jnp.int32, (width, LANES), 0)
     first, last = column == 0, column == width - 1
@@ -229,6 +240,7 @@
                 at = pl.ds((v * rows + r - 1) * width, width)
                 row_u[at, :] = (above == here).astype(F32)
                 row_d[at, :] = (below == here).astype(F32)
+    pump()
     for cp in copies:
         cp.wait_recv()
     mean, inv, divisor = combine_stats(buf[0])
@@ -287,6 +299,24 @@
     @pl.when(me == n - 1)
     def _():
         halo[1] = jnp.full(halo.shape[1:], edge, halo.dtype)
+
+
+def layout_scratch(n, dims, ids_lane):
+    canvases, rows, width = dims
+    cells = canvases * rows * width // UNIT
+    return [
+        pltpu.VMEM((1, n, canvases * CROPS, LANES), F32),
+        pltpu.VMEM((n,) + ids_lane.shape, F32),
+        pltpu.VMEM((2, canvases, width, LANES), F32),
+        pltpu.VMEM((cells, C), F32),
+        pltpu.VMEM((cells, C), F32),
+        pltpu.SemaphoreType.DMA((1, n)),
+        pltpu.SemaphoreType.DMA((1, n)),
+        pltpu.SemaphoreType.DMA((n,)),
+        pltpu.SemaphoreType.DMA((n,)),
+        pltpu.SemaphoreType.DMA((2,)),
+        pltpu.SemaphoreType.DMA((2,)),
+    ]
 
 
 def layout_call(n, dims, x, pick, spread, ids_px, ids_lane):
@@ -309,26 +339,118 @@
         ],
         in_specs=[vmem] * 5,
         out_specs=[vmem] * 9,
-        scratch_shapes=[
-            pltpu.VMEM((1, n, stats, LANES), F32),
-            pltpu.VMEM((n,) + ids_lane.shape, F32),
-            pltpu.VMEM((2, canvases, width, LANES), F32),
-            pltpu.VMEM((cells, C), F32),
-            pltpu.VMEM((cells, C), F32),
-            pltpu.SemaphoreType.DMA((1, n)),
-            pltpu.SemaphoreType.DMA((1, n)),
-            pltpu.SemaphoreType.DMA((n,)),
-            pltpu.SemaphoreType.DMA((n,)),
-            pltpu.SemaphoreType.DMA((2,)),
-            pltpu.SemaphoreType.DMA((2,)),
-        ],
+        scratch_shapes=layout_scratch(n, dims, ids_lane),
         compiler_params=params_of(1),
         name="layout",
     )(x, pick, spread, ids_px, ids_lane)
 
 
+def second_matrix(top, low, dest, sem):
+    return [
+        pltpu.make_async_copy(top.at[pl.ds(9 * C, 2 * C)], dest.at[pl.ds(0, 2 * C)], sem.at[1]),
+        pltpu.make_async_copy(low.at[pl.ds(0, 7 * C)], dest.at[pl.ds(2 * C, 7 * C)], sem.at[2]),
+    ]
+
+
+class Convolver:
+    def __init__(self, n, dims, x, pick, spread, cnt, col_l, col_r, row_u, row_d, halo, buf, tmp_a, tmp_b, send,
+                 recv, hsend, hrecv):
+        self.n, self.dims = n, dims
+        self.x, self.pick, self.spread, self.cnt = x, pick, spread, cnt
+        self.col_l, self.col_r, self.row_u, self.row_d = col_l, col_r, row_u, row_d
+        self.halo, self.buf, self.tmp_a, self.tmp_b = halo, buf, tmp_a, tmp_b
+        self.send, self.recv, self.hsend, self.hrecv = send, recv, hsend, hrecv
+        self.px = dims[0] * dims[1] * dims[2]
+        self.cells = self.px // UNIT
+        self.sent = []
+
+    def activate(self, source, mean, inv, gain, bias, dest, rnd, pump=no_pump):
+        canvases, rows, width = self.dims
+        row_cells = width // UNIT
+        col_l, col_r, halo = self.col_l, self.col_r, self.halo
+
+        def one(v, r):
+            at = pl.ds(pl.multiple_of((v * rows + r) * width, width), width)
+            cell = pl.ds(pl.multiple_of((v * rows + r) * row_cells, row_cells), row_cells)
+            value = source[at, :].astype(F32)
+            m = jnp.broadcast_to(mean[cell, :][:, None, :], (row_cells, UNIT, C)).reshape(width, C)
+            s = jnp.broadcast_to(inv[cell, :][:, None, :], (row_cells, UNIT, C)).reshape(width, C)
+            a = (value - m) * s * gain + bias
+            dest[v, r + 1] = shift_columns(silu(a), col_l[v, r + 1], col_r[v, r + 1])
+
+        def edges(v, _):
+            one(v, 0)
+            if rows > 1:
+                one(v, rows - 1)
+            return 0
+
+        lax.fori_loop(0, canvases, edges, 0)
+        mid = pl.ds(C, C)
+        up, down = halo_copies(self.n, dest.at[:, 1, :, mid], dest.at[:, rows, :, mid], halo.at[rnd],
+                               self.hsend.at[rnd], self.hrecv.at[rnd])
+        start_halo(self.n, up, down)
+        pump()
+
+        def inner(i, _):
+            one(i // (rows - 2), 1 + lax.rem(i, rows - 2))
+            return 0
+
+        if rows > 2:
+            lax.fori_loop(0, canvases * (rows - 2), inner, 0)
+        pump()
+        wait_halo(self.n, up, down, halo.at[rnd], 0.0)
+        for v in range(canvases):
+            for side, r in ((0, 0), (1, rows + 1)):
+                dest[v, r] = shift_columns(halo[rnd, side, v].astype(F32), col_l[v, r], col_r[v, r])
+
+    def convolve(self, source, weights, emit, pump=no_pump):
+        canvases, rows, width = self.dims
+        plane = rows * width
+        for v in range(canvases):
+            at = pl.ds(v * plane, plane)
+            total = None
+            for dr in (1, 0, 2):
+                part = None
+                for lo, hi, ref, row in weights(dr):
+                    lhs = source[v, dr : dr + rows, :, lo:hi].reshape(plane, hi - lo)
+                    term = jnp.dot(lhs, ref[row : row + hi - lo, :], preferred_element_type=F32)
+                    part = term if part is None else part + term
+                if dr == 0:
+                    part = part * wide(self.row_u[at, :])
+                if dr == 2:
+                    part = part * wide(self.row_d[at, :])
+                total = part if total is None else total + part
+            emit(at, total)
+            pump()
+
+    def statistics(self, source, mean, inv, rnd, pump=no_pump):
+        def load(i):
+            return source[pl.ds(i * 16 * UNIT, 16 * UNIT), :]
+
+        self.buf[rnd, 0] = stats_payload(load, self.pick, self.spread, self.cnt, self.cells, self.tmp_a, self.tmp_b)
+        copies = spread_copies(self.n, self.buf, self.send, self.recv, rnd)
+        for cp in copies:
+            cp.start()
+        pump()
+        for cp in copies:
+            cp.wait_recv()
+        m, s, _ = combine_stats(self.buf[rnd])
+        mean[...] = split_dot(self.spread[...], unpack(m))
+        inv[...] = split_dot(self.spread[...], unpack(s))
+        self.sent = self.sent + copies
+
+    def normalise(self, source, mean, inv, gain, bias, dest):
+        def last(i, _):
+            at = pl.ds(i * 16 * UNIT, 16 * UNIT)
+            value = (source[at, :] - over_cells(mean, i)) * over_cells(inv, i)
+            dest[at, :] = (value * gain + bias).astype(B16)
+            return 0
+
+        lax.fori_loop(0, self.cells // 16, last, 0)
+
+
 def resnet_forward_kernel(n, dims, keep, x, pick, spread, cnt, mean1, inv1, col_l, col_r, row_u, row_d,
-                          vec, whole, *refs):
+                          vec, top, low, *refs):
     canvases, rows, width = dims
     px = canvases * rows * width
     cells = px // UNIT
@@ -341,109 +463,40 @@
         y1, s1, s2, mean2, inv2, mean3, inv3 = refs[2:9]
         refs = refs[9:]
     k1, k2, halo, buf, tmp_a, tmp_b, ksem, send, recv, hsend, hrecv = refs
-    load1 = pltpu.make_async_copy(whole.at[pl.ds(0, 9 * C)], k1, ksem.at[0])
-    load2 = pltpu.make_async_copy(whole.at[pl.ds(9 * C, 9 * C)], k2, ksem.at[1])
-    load1.start()
-    load2.start()
+    load1 = [pltpu.make_async_copy(top.at[pl.ds(0, 9 * C)], k1, ksem.at[0])]
+    load2 = second_matrix(top, low, k2, ksem)
+    for cp in load1 + load2:
+        cp.start()
     greet(n)
-    row_cells = width // UNIT
-
-    def activate(source, mean, inv, gain, bias, dest, rnd):
-        def one(v, r):
-            at = pl.ds(pl.multiple_of((v * rows + r) * width, width), width)
-            cell = pl.ds(pl.multiple_of((v * rows + r) * row_cells, row_cells), row_cells)
-            value = source[at, :].astype(F32)
-            m = jnp.broadcast_to(mean[cell, :][:, None, :], (row_cells, UNIT, C)).reshape(width, C)
-            s = jnp.broadcast_to(inv[cell, :][:, None, :], (row_cells, UNIT, C)).reshape(width, C)
-            a = (value - m) * s * gain + bias
-            dest[v, r + 1] = shift_columns(silu(a), col_l[v, r + 1], col_r[v, r + 1])
-
-        def edges(v, _):
-            one(v, 0)
-            if rows > 1:
-                one(v, rows - 1)
-            return 0
-
-        lax.fori_loop(0, canvases, edges, 0)
-        mid = pl.ds(C, C)
-        up, down = halo_copies(n, dest.at[:, 1, :, mid], dest.at[:, rows, :, mid], halo.at[rnd],
-                               hsend.at[rnd], hrecv.at[rnd])
-        start_halo(n, up, down)
-
-        def inner(i, _):
-            one(i // (rows - 2), 1 + lax.rem(i, rows - 2))
-            return 0
-
-        if rows > 2:
-            lax.fori_loop(0, canvases * (rows - 2), inner, 0)
-        wait_halo(n, up, down, halo.at[rnd], 0.0)
-        for v in range(canvases):
-            for side, r in ((0, 0), (1, rows + 1)):
-                dest[v, r] = shift_columns(halo[rnd, side, v].astype(F32), col_l[v, r], col_r[v, r])
-
-    def convolve(source, weight, emit):
-        def body(v, _):
-            at = pl.ds(pl.multiple_of(v * plane, plane), plane)
-            total = None
-            for dr in (1, 0, 2):
-                lhs = source[v, dr : dr + rows].reshape(plane, 3 * C)
-                part = jnp.dot(lhs, weight[3 * C * dr : 3 * C * (dr + 1), :],
-                               preferred_element_type=F32)
-                if dr == 0:
-                    part = part * wide(row_u[at, :])
-                if dr == 2:
-                    part = part * wide(row_d[at, :])
-                total = part if total is None else total + part
-            emit(at, total)
-            return 0
-
-        lax.fori_loop(0, canvases, body, 0)
-
-    def statistics(source, mean, inv, rnd):
-        def load(i):
-            return source[pl.ds(i * 16 * UNIT, 16 * UNIT), :]
-
-        buf[rnd, 0] = stats_payload(load, pick, spread, cnt, cells, tmp_a, tmp_b)
-        copies = spread_copies(n, buf, send, recv, rnd)
+    for_conv = Convolver(n, dims, x, pick, spread, cnt, col_l, col_r, row_u, row_d, halo, buf, tmp_a, tmp_b,
+                         send, recv, hsend, hrecv)
+
+    def wait_all(copies):
         for cp in copies:
-            cp.start()
-        for cp in copies:
-            cp.wait_recv()
-        m, s, _ = combine_stats(buf[rnd])
-        mean[...] = split_dot(spread[...], unpack(m))
-        inv[...] = split_dot(spread[...], unpack(s))
-        return copies
-
-    activate(x, mean1, inv1, vec[0:1, :], vec[1:2, :], s1, 0)
-    load1.wait()
+            cp.wait()
+
+    for_conv.activate(x, mean1, inv1, vec[0:1, :], vec[1:2, :], s1, 0)
+    wait_all(load1)
 
     def emit_first(at, total):
         y1[at, :] = total + vec[2:3, :]
 
-    convolve(s1, k1, emit_first)
-    sent = statistics(y1, mean2, inv2, 0)
-    activate(y1, mean2, inv2, vec[3:4, :], vec[4:5, :], s2, 1)
-    load2.wait()
+    for_conv.convolve(s1, lambda dr: [(0, 3 * C, k1, 3 * C * dr)], emit_first)
+    for_conv.statistics(y1, mean2, inv2, 0)
+    for_conv.activate(y1, mean2, inv2, vec[3:4, :], vec[4:5, :], s2, 1)
+    wait_all(load2)
 
     def emit_second(at, total):
         hid[at, :] = total + vec[5:6, :] + x[at, :].astype(F32)
 
-    convolve(s2, k2, emit_second)
-    sent = sent + statistics(hid, mean3, inv3, 1)
-    gain3, bias3 = vec[6:7, :], vec[7:8, :]
-
-    def last(i, _):
-        at = pl.ds(i * 16 * UNIT, 16 * UNIT)
-        value = (hid[at, :] - over_cells(mean3, i)) * over_cells(inv3, i)
-        u[at, :] = (value * gain3 + bias3).astype(B16)
-        return 0
-
-    lax.fori_loop(0, cells // 16, last, 0)
-    for cp in sent:
+    for_conv.convolve(s2, lambda dr: [(0, 3 * C, k2, 3 * C * dr)], emit_second)
+    for_conv.statistics(hid, mean3, inv3, 1)
+    for_conv.normalise(hid, mean3, inv3, vec[6:7, :], vec[7:8, :], u)
+    for cp in for_conv.sent:
         cp.wait_send()
 
 
-def resnet_forward_call(n, dims, keep, x, pick, spread, cnt, mean1, inv1, masks, vec, whole):
+def resnet_forward_call(n, dims, keep, x, pick, spread, cnt, mean1, inv1, masks, vec, top, low):
     canvases, rows, width = dims
     px = canvases * rows * width
     cells = px // UNIT
@@ -463,7 +516,7 @@
     return pl.pallas_call(
         functools.partial(resnet_forward_kernel, n, dims, keep),
         out_shape=[sds(*s) for s in outs],
-        in_specs=[vmem] * 11 + [anyw],
+        in_specs=[vmem] * 11 + [anyw] * 2,
         out_specs=[vmem] * len(outs),
         scratch_shapes=scratch
         + [
@@ -473,7 +526,7 @@
             pltpu.VMEM((2, n, stats, LANES), F32),
             pltpu.VMEM((cells, C), F32),
             pltpu.VMEM((cells, C), F32),
-            pltpu.SemaphoreType.DMA((2,)),
+            pltpu.SemaphoreType.DMA((3,)),
             pltpu.SemaphoreType.DMA((2, n)),
             pltpu.SemaphoreType.DMA((2, n)),
             pltpu.SemaphoreType.DMA((2, 2)),
@@ -481,10 +534,10 @@
         ],
         compiler_params=params_of(2 if keep else 3),
         name="resnet_forward" if keep else "resnet_again",
-    )(x, pick, spread, cnt, mean1, inv1, *masks, vec, whole)
-
-
-def attention_kernel(keep, chunk, block, ua, key_ids, query_ids, offsets, dz, vec, whole, *refs):
+    )(x, pick, spread, cnt, mean1, inv1, *masks, vec, top, low)
+
+
+def attention_kernel(keep, chunk, block, ua, key_ids, query_ids, offsets, dz, vec, low, *refs):
     total = ua.shape[0] * ua.shape[1]
     queries = query_ids.shape[0]
     segment = ua.shape[1]
@@ -495,7 +548,7 @@
     else:
         out = refs[0]
         u, w, k, v, usem, wsem = refs[1:]
-    load_w = pltpu.make_async_copy(whole.at[pl.ds(18 * C, 4 * C)], w, wsem.at[0])
+    load_w = pltpu.make_async_copy(low.at[pl.ds(7 * C, 4 * C)], w, wsem.at[0])
     load_w.start()
     blocks = ua.shape[0]
     loads = [
@@ -598,7 +651,7 @@
     )
 
 
-def attention_call(keep, ua, key_ids, query_ids, offsets, dz, vec, whole):
+def attention_call(keep, ua, key_ids, query_ids, offsets, dz, vec, low):
     blocks, segment, _ = ua.shape
     total = blocks * segment
     queries = query_ids.shape[0]
@@ -629,7 +682,7 @@
         + [pltpu.SemaphoreType.DMA((blocks,)), pltpu.SemaphoreType.DMA((1,))],
         compiler_params=params_of(),
         name="attention" if keep else "attention_again",
-    )(ua, key_ids, query_ids, offsets, dz, vec, whole)
+    )(ua, key_ids, query_ids, offsets, dz, vec, low)
 
 
 def other_core(h):
@@ -819,8 +872,8 @@
 
 
 def resnet_backward_kernel(n, dims, cot, du, hid, y1, x, mean1, inv1, mean2, inv2, mean3, inv3, s1, s2, pick,
-                           spread, div, col_l, col_r, row_u, row_d, vec, whole, datt, igrad, grads, dvec,
-                           dw1, dw2, k, dh, d3, low, low_u, low_d, part, norm, halo, buf, tmp_a, tmp_b, ksem, send,
+                           spread, div, col_l, col_r, row_u, row_d, vec, top, bottom, datt, igrad, grads, dvec,
+                           dw1, dw2, k, dh, d3, low, low_u, low_d, part, norm, halo, buf, tmp_a, tmp_b, ksem, wsem, send,
                            recv, hsend, hrecv):
     canvases, rows, width = dims
     px = canvases * rows * width
@@ -828,9 +881,10 @@
     plane = rows * width
     nt = (((1,), (1,)), ((), ()))
     tn = (((0,), (0,)), ((), ()))
-    load2 = pltpu.make_async_copy(whole.at[pl.ds(9 * C, 9 * C)], k, ksem.at[0])
-    load1 = pltpu.make_async_copy(whole.at[pl.ds(0, 9 * C)], k, ksem.at[1])
-    load2.start()
+    load2 = second_matrix(top, bottom, k, wsem)
+    load1 = pltpu.make_async_copy(top.at[pl.ds(0, 9 * C)], k, wsem.at[0])
+    for cp in load2:
+        cp.start()
     out_att = pltpu.make_async_copy(datt, grads.at[pl.ds(18 * C, 4 * C)], ksem.at[2])
     out_two = pltpu.make_async_copy(dw2, grads.at[pl.ds(9 * C, 9 * C)], ksem.at[3])
     out_one = pltpu.make_async_copy(dw1, grads.at[pl.ds(0, 9 * C)], ksem.at[4])
@@ -962,7 +1016,8 @@
     mask_rows()
     dc2 = jnp.sum(low[...].astype(F32), axis=0, keepdims=True)
     finish_rows(up, down, 0)
-    load2.wait()
+    for cp in load2:
+        cp.wait()
 
     def emit_part(at, total):
         part[at, :] = total
@@ -1013,8 +1068,8 @@
         cp.wait_send()
 
 
-def resnet_backward_call(n, dims, cid, cot, du, hid, y1, x, norms, s1, s2, pick, spread, div, masks, vec, whole,
-                         datt):
+def resnet_backward_call(n, dims, cid, cot, du, hid, y1, x, norms, s1, s2, pick, spread, div, masks, vec, top,
+                         bottom, datt):
     canvases, rows, width = dims
     px = canvases * rows * width
     cells = px // UNIT
@@ -1022,7 +1077,7 @@
     return pl.pallas_call(
         functools.partial(resnet_backward_kernel, n, dims),
         out_shape=[sds((px, C), F32), sds((22 * C, C), B16), sds((8, C), F32)],
-        in_specs=[vmem] * 21 + [anyw, anyw],
+        in_specs=[vmem] * 21 + [anyw] * 3,
         out_specs=[vmem, anyw, vmem],
         scratch_shapes=[
             pltpu.VMEM((9 * C, C), B16),
@@ -1040,6 +1095,7 @@
             pltpu.VMEM((cells, C), F32),
             pltpu.VMEM((cells, C), F32),
             pltpu.SemaphoreType.DMA((5,)),
+            pltpu.SemaphoreType.DMA((3,)),
             pltpu.SemaphoreType.DMA((3, n)),
             pltpu.SemaphoreType.DMA((3, n)),
             pltpu.SemaphoreType.DMA((2, 2)),
@@ -1047,7 +1103,7 @@
         ],
         compiler_params=params_of(cid),
         name="resnet_backward",
-    )(cot, du, hid, y1, x, *norms, s1, s2, pick, spread, div, *masks, vec, whole, datt)
+    )(cot, du, hid, y1, x, *norms, s1, s2, pick, spread, div, *masks, vec, top, bottom, datt)
 
 
 class Grid:
@@ -1424,6 +1480,1077 @@
     )(grads, w, m, s, dvec, vw, vm, vs)
 
 
+class Engine:
+    def __init__(self, steps):
+        self.steps = steps
+
+    def pump(self, count=1):
+        for _ in range(count):
+            next(self.steps, None)
+
+    def finish(self):
+        for _ in self.steps:
+            pass
+
+
+class Group:
+    def __init__(self, grid, number, half_rows, first=0, size=None):
+        self.g, self.number, self.half = grid, number, half_rows
+        self.first, self.size = first, half_rows if size is None else size
+        self.owner = 2 * number + grid.c // 2
+        self.is_owner = grid.c // 2 == number
+
+    def row(self, q, seat, core):
+        block = (q // 2) * self.g.n + 2 * seat + core
+        return pl.multiple_of((2 * block + lax.rem(q, 2)) * self.half + self.first, 16)
+
+    def rows(self, q, seat, core):
+        return pl.ds(self.row(q, seat, core), self.size)
+
+    def at_column(self, col):
+        return {"canvas": col, "height": self.g.h}
+
+    def halves(self):
+        first = 2 * lax.rem(self.g.c, 2)
+        return [(0, first), (1, first + 1)]
+
+    def part(self, ref, half):
+        return ref.at[pl.ds(half * self.half, self.half)]
+
+    def to_pieces(self, block, piece, send, recv, start):
+        g = self.g
+
+        @pl.when(self.is_owner)
+        def _():
+            for half, col in self.halves():
+                @pl.when(col != g.c)
+                def _():
+                    cp = remote(self.part(block, half), piece, send.at[half], recv.at[0], self.at_column(col))
+                    cp.start() if start else cp.wait_send()
+
+                if start:
+                    @pl.when(col == g.c)
+                    def _():
+                        piece[...] = block[half * self.half : (half + 1) * self.half, :]
+
+    def piece_arrived(self, block, piece, send, recv):
+        @pl.when(self.owner != self.g.c)
+        def _():
+            remote(self.part(block, 0), piece, send.at[0], recv.at[0], self.at_column(self.owner)).wait_recv()
+
+    def to_owner(self, piece, block, send, recv, start):
+        g = self.g
+        half = lax.rem(g.c, 2)
+        where = pl.ds(pl.multiple_of(half * self.half, 16), self.half)
+
+        @pl.when(self.owner != g.c)
+        def _():
+            cp = remote(piece, block.at[where], send.at[0], recv.at[half], self.at_column(self.owner))
+            cp.start() if start else cp.wait_send()
+
+        if start:
+            @pl.when(self.owner == g.c)
+            def _():
+                block[where, :] = piece[...]
+
+    def block_arrived(self, piece, block, send, recv):
+        g = self.g
+
+        @pl.when(self.is_owner)
+        def _():
+            for half, col in self.halves():
+                @pl.when(col != g.c)
+                def _():
+                    remote(piece, self.part(block, half), send.at[0], recv.at[half], self.at_column(col)).wait_recv()
+
+
+def gather_pieces(group, piece, dest, own, zsend, msend, ssend, recv, srecv):
+    g = group.g
+    seats, phases = g.seats, g.phases
+    local = pltpu.make_async_copy(piece, dest.at[group.rows(g.c, g.seat, g.core)], own.at[0])
+    local.start()
+
+    def slot(e, seat):
+        return dest.at[group.rows(g.column(e), seat, g.core)]
+
+    def forward(e, seat, src, start):
+        k_top = phases if e == 0 else lowest_bit(e)
+        for k in range(k_top - 1, -1, -1):
+            cp = remote(src, slot(e, seat), msend.at[k, e, seat], recv.at[e | (1 << k), seat], g.mate(k))
+            cp.start() if start else cp.wait_send()
+        cp = remote(src, slot(e, seat), ssend.at[e, seat], srecv.at[e, seat], g.sibling())
+        cp.start() if start else cp.wait_send()
+
+    def along(seat, step, src, start):
+        cp = remote(src, slot(0, seat), zsend.at[(step + 1) // 2, seat], recv.at[0, seat], g.beside(step))
+        cp.start() if start else cp.wait_send()
+
+    def line(seat, src, start):
+        @pl.when((seat <= g.seat) & (g.seat < seats - 1))
+        def _():
+            along(seat, 1, src, start)
+
+        @pl.when((seat >= g.seat) & (g.seat > 0))
+        def _():
+            along(seat, -1, src, start)
+
+    def handle(e, seat):
+        remote(piece, slot(e, seat), ssend.at[0, 0], recv.at[e, seat], g.sibling()).wait_recv()
+        if e == 0:
+            line(seat, slot(0, seat), True)
+        forward(e, seat, slot(e, seat), True)
+
+    early = sorted((e for e in range(1, 2**phases) if lowest_bit(e) > 0), key=lambda e: -lowest_bit(e))
+    late = [e for e in range(1, 2**phases) if lowest_bit(e) == 0]
+
+    def both_sides(d, todo):
+        for side in (-1, 1):
+            seat = g.seat + side * d
+
+            @pl.when((seat >= 0) & (seat < seats))
+            def _():
+                for e in todo:
+                    handle(e, seat)
+
+    line(g.seat, piece, True)
+    forward(0, g.seat, piece, True)
+    yield
+    for e in early:
+        handle(e, g.seat)
+    yield
+    for d in range(1, seats):
+        both_sides(d, [0] + early)
+        yield
+    for e in late:
+        handle(e, g.seat)
+    yield
+    for d in range(1, seats):
+        both_sides(d, late)
+        yield
+
+    def drain(seat, _):
+        for e in range(2**phases):
+            remote(piece, dest.at[group.rows(g.column(e, g.other_flips), seat, 1 - g.core)], ssend.at[0, 0],
+                   srecv.at[e, seat], g.sibling()).wait_recv()
+            forward(e, seat, slot(e, seat), False)
+        line(seat, slot(0, seat), False)
+        return 0
+
+    lax.fori_loop(0, seats, drain, 0)
+    local.wait()
+
+
+def gather_pieces_scratch(columns, n):
+    seats, phases = n // 2, columns.bit_length() - 1
+    dma = pltpu.SemaphoreType.DMA
+    return [
+        dma((1,)),
+        dma((2, seats)),
+        dma((phases, columns, seats)),
+        dma((columns, seats)),
+        dma((columns, seats)),
+        dma((columns, seats)),
+    ]
+
+
+def reduce_pieces(group, src, piece, sib, got, box, gsend, grecv, psend, precv, usend, urecv):
+    g = group.g
+    seats, phases = g.seats, g.phases
+    slots = 2**phases
+    order = sorted(range(slots), key=lambda e: (lowest_bit(e) if e else phases, e == (e & -e)))
+    turns = [i // 2 if i % 2 == 0 else seats - 1 - i // 2 for i in range(seats)]
+
+    def mine(e, seat):
+        return group.rows(g.column(e), seat, g.core)
+
+    def sibling_copy(e, seat):
+        return remote(src.at[group.rows(g.column(e, g.other_flips), seat, 1 - g.core)], sib.at[e, seat],
+                      gsend.at[e, seat], grecv.at[e, seat], g.sibling())
+
+    def phase_copy(k, e, seat):
+        at = (k, e >> (k + 1), seat)
+        return remote(src.at[mine(e, seat), :], got.at[at], psend.at[at], precv.at[at], g.mate(k))
+
+    def line_copy(seat):
+        return remote(src.at[mine(0, seat), :], box.at[g.seat], usend.at[seat], urecv.at[g.seat],
+                      {"canvas": g.c, "height": 2 * seat + g.core})
+
+    def line_arrival(seat):
+        return remote(src.at[mine(0, seat), :], box.at[seat], usend.at[seat], urecv.at[seat],
+                      {"canvas": g.c, "height": 2 * seat + g.core})
+
+    def local(e, seat, below):
+        total = src[mine(e, seat), :].astype(F32) + sib[e, seat].astype(F32)
+        for k in range(below):
+            total = total + got[k, e >> (k + 1), seat].astype(F32)
+        return total
+
+    for e in order:
+        for seat in turns:
+            sibling_copy(e, seat).start()
+    yield
+    for e in order:
+        if e == 0:
+            break
+        k = lowest_bit(e)
+        for seat in turns:
+            sibling_copy(e, seat).wait_recv()
+            for q in range(k):
+                phase_copy(q, e | (1 << q), seat).wait_recv()
+            src[mine(e, seat), :] = local(e, seat, k).astype(B16)
+            phase_copy(k, e, seat).start()
+            yield
+    for seat in turns:
+        sibling_copy(0, seat).wait_recv()
+        for q in range(phases):
+            phase_copy(q, 1 << q, seat).wait_recv()
+
+        @pl.when(seat != g.seat)
+        def _():
+            src[mine(0, seat), :] = local(0, seat, phases).astype(B16)
+            line_copy(seat).start()
+
+        yield
+    total = local(0, g.seat, phases)
+    for seat in turns:
+        @pl.when(seat != g.seat)
+        def _():
+            line_arrival(seat).wait_recv()
+
+        total = total + jnp.where(seat == g.seat, 0.0, box[seat].astype(F32))
+    piece[...] = total.astype(B16)
+    yield
+
+    def drain(seat, _):
+        for e in range(slots):
+            sibling_copy(e, seat).wait_send()
+            if e > 0:
+                phase_copy(lowest_bit(e), e, seat).wait_send()
+
+        @pl.when(seat != g.seat)
+        def _():
+            line_copy(seat).wait_send()
+
+        return 0
+
+    lax.fori_loop(0, seats, drain, 0)
+
+
+def reduce_pieces_scratch(columns, n, half_rows):
+    seats, phases = n // 2, columns.bit_length() - 1
+    half = columns // 2
+    dma = pltpu.SemaphoreType.DMA
+    block = (half_rows, C)
+    return [
+        pltpu.VMEM((columns, seats) + block, B16),
+        pltpu.VMEM((phases, half, seats) + block, B16),
+        pltpu.VMEM((seats,) + block, B16),
+        dma((columns, seats)),
+        dma((columns, seats)),
+        dma((phases, half, seats)),
+        dma((phases, half, seats)),
+        dma((seats,)),
+        dma((seats,)),
+    ]
+
+
+class Named:
+    def __init__(self, shapes, refs):
+        refs = list(refs)
+        for name, shape in shapes.items():
+            if isinstance(shape, list):
+                setattr(self, name, [refs.pop(0) for _ in shape])
+            else:
+                setattr(self, name, refs.pop(0))
+
+
+def named_call(kernel, name, cid, inputs, outputs, scratch):
+    shapes = {**inputs, **outputs, **scratch}
+    flat = []
+    for value in scratch.values():
+        flat += value if isinstance(value, list) else [value]
+    results = pl.pallas_call(
+        lambda *refs: kernel(Named(shapes, refs)),
+        out_shape=[sds(shape, kind) for shape, kind, _ in outputs.values()],
+        in_specs=[spec for _, spec in inputs.values()],
+        out_specs=[spec for _, _, spec in outputs.values()],
+        scratch_shapes=flat,
+        compiler_params=params_of(cid),
+        name=name,
+    )(*[array for array, _ in inputs.values()])
+    return dict(zip(outputs, results))
+
+
+def greet_all(grid):
+    barrier = pltpu.get_barrier_semaphore()
+    for d in range(1, grid.n):
+        pl.semaphore_signal(
+            barrier, inc=1, device_id={"canvas": grid.c, "height": lax.rem(grid.h + d, grid.n)}, device_id_type=MESH)
+    for d in range(1, grid.columns):
+        pl.semaphore_signal(
+            barrier, inc=1, device_id={"canvas": lax.rem(grid.c + d, grid.columns), "height": grid.h},
+            device_id_type=MESH)
+    pl.semaphore_wait(barrier, grid.n - 1 + grid.columns - 1)
+
+
+def first_kernel(columns, n, dims, R):
+    g = Grid(columns, n)
+    half = R.block.shape[0] // 2
+    groups = [Group(g, i, half) for i in range(2)]
+    R.low[...] = R.block[...].astype(B16)
+    greet_all(g)
+    for i, group in enumerate(groups):
+        group.to_pieces(R.low, R.pieces.at[i], R.tsend.at[i], R.trecv.at[i], True)
+    weights = [R.w_top, R.w_low]
+    engines = [
+        Engine(gather_pieces(group, R.pieces.at[i], weights[i], *(R.gather0 if i == 0 else R.gather1)))
+        for i, group in enumerate(groups)
+    ]
+    turn = [0]
+    mine = g.h // (n // 2)
+    cot_copy = remote(R.cot.at[1 - mine], R.far_cot, R.csem.at[0], R.csem.at[1],
+                      {"canvas": g.c, "height": lax.rem(g.h + n // 2, n)})
+
+    def pump():
+        if turn[0] == 0:
+            groups[0].piece_arrived(R.low, R.pieces.at[0], R.tsend.at[0], R.trecv.at[0])
+        engines[0].pump()
+        if turn[0] == g.seats:
+            cot_copy.start()
+        turn[0] += 1
+
+    layout_body(n, dims, R.x, R.pick, R.spread, R.ids_px, R.ids_lane, R.ids_all, R.mean1, R.inv1, R.div, R.cnt,
+                R.col_l, R.col_r, R.row_u, R.row_d, *R.layout, pump=pump)
+    pump()
+    conv = Convolver(n, dims, R.x, R.pick, R.spread, R.cnt, R.col_l, R.col_r, R.row_u, R.row_d, R.halo, R.buf,
+                     R.tmp_a, R.tmp_b, R.send, R.recv, R.hsend, R.hrecv)
+    vec = R.vec
+    conv.activate(R.x, R.mean1, R.inv1, vec[0:1, :], vec[1:2, :], R.s1, 0, pump)
+    out_s1 = pltpu.make_async_copy(R.s1, R.s1_out, R.osem.at[0])
+    out_s1.start()
+    while turn[0] <= g.seats:
+        pump()
+    engines[0].finish()
+    out_top = pltpu.make_async_copy(R.w_top, R.top, R.osem.at[1])
+    out_top.start()
+    groups[1].piece_arrived(R.low, R.pieces.at[1], R.tsend.at[1], R.trecv.at[1])
+    pump_low = engines[1].pump
+    pump_low()
+
+    def emit_first(at, total):
+        R.y1[at, :] = total + vec[2:3, :]
+
+    conv.convolve(R.s1, lambda dr: [(0, 3 * C, R.w_top, 3 * C * dr)], emit_first, pump_low)
+    out_y1 = pltpu.make_async_copy(R.y1, R.y1_out, R.osem.at[2])
+    out_y1.start()
+    conv.statistics(R.y1, R.mean2, R.inv2, 0, pump_low)
+    conv.activate(R.y1, R.mean2, R.inv2, vec[3:4, :], vec[4:5, :], R.s2, 1, pump_low)
+    out_s2 = pltpu.make_async_copy(R.s2, R.s2_out, R.osem.at[3])
+    out_s2.start()
+    engines[1].finish()
+    out_low = pltpu.make_async_copy(R.w_low, R.bottom, R.osem.at[4])
+    out_low.start()
+
+    def emit_second(at, total):
+        R.hid[at, :] = total + vec[5:6, :] + R.x[at, :].astype(F32)
+
+    def second(dr):
+        if dr == 0:
+            return [(0, 2 * C, R.w_top, 9 * C), (2 * C, 3 * C, R.w_low, 0)]
+        return [(0, 3 * C, R.w_low, 3 * C * dr - 2 * C)]
+
+    conv.convolve(R.s2, second, emit_second)
+    conv.statistics(R.hid, R.mean3, R.inv3, 1)
+    conv.normalise(R.hid, R.mean3, R.inv3, vec[6:7, :], vec[7:8, :], R.u)
+    for cp in conv.sent:
+        cp.wait_send()
+    for i, group in enumerate(groups):
+        group.to_pieces(R.low, R.pieces.at[i], R.tsend.at[i], R.trecv.at[i], False)
+    for cp in (out_s1, out_top, out_y1, out_s2, out_low, cot_copy):
+        cp.wait()
+
+
+def first_call(columns, n, dims, x, pick, spread, ids_px, ids_lane, vec, block, cot):
+    canvases, rows, width = dims
+    px = canvases * rows * width
+    cells = px // UNIT
+    stats = canvases * CROPS
+    tall = (canvases, rows + 2, width)
+    half = block.shape[0] // 2
+    dma = pltpu.SemaphoreType.DMA
+    inputs = dict(x=(x, vmem), pick=(pick, vmem), spread=(spread, vmem), ids_px=(ids_px, vmem),
+                  ids_lane=(ids_lane, vmem), vec=(vec, vmem), block=(block, vmem),
+                  cot=(cot, anyw))
+    cell = ((cells, C), F32, vmem)
+    outputs = dict(
+        ids_all=((n,) + ids_lane.shape, F32, vmem), mean1=cell, inv1=cell, div=((stats, LANES), F32, vmem),
+        cnt=((stats, LANES), F32, vmem), col_l=(tall + (LANES,), F32, vmem), col_r=(tall + (LANES,), F32, vmem),
+        row_u=((px, LANES), F32, vmem), row_d=((px, LANES), F32, vmem), hid=((px, C), F32, vmem),
+        u=((px, C), B16, vmem), mean2=cell, inv2=cell, mean3=cell, inv3=cell, y1_out=((px, C), F32, anyw),
+        s1_out=(tall + (3 * C,), B16, anyw), s2_out=(tall + (3 * C,), B16, anyw),
+        top=((11 * C, C), B16, anyw), bottom=((11 * C, C), B16, anyw), far_cot=(cot.shape[1:], B16, anyw))
+    scratch = dict(
+        csem=dma((2,)), y1=pltpu.VMEM((px, C), F32), s1=pltpu.VMEM(tall + (3 * C,), B16), s2=pltpu.VMEM(tall + (3 * C,), B16),
+        w_top=pltpu.VMEM((11 * C, C), B16), w_low=pltpu.VMEM((11 * C, C), B16), low=pltpu.VMEM(block.shape, B16),
+        pieces=pltpu.VMEM((2, half, C), B16), tsend=dma((2, 2)), trecv=dma((2, 1)),
+        gather0=gather_pieces_scratch(columns, n), gather1=gather_pieces_scratch(columns, n),
+        layout=layout_scratch(n, dims, ids_lane), halo=pltpu.VMEM((2, 2, canvases, width, C), B16),
+        buf=pltpu.VMEM((2, n, stats, LANES), F32), tmp_a=pltpu.VMEM((cells, C), F32),
+        tmp_b=pltpu.VMEM((cells, C), F32), send=dma((2, n)), recv=dma((2, n)), hsend=dma((2, 2)),
+        hrecv=dma((2, 2)), osem=dma((5,)))
+    return named_call(functools.partial(first_kernel, columns, n, dims), "first_forward", 1, inputs, outputs, scratch)
+
+
+class Backer:
+    def __init__(self, n, dims, R):
+        self.n, self.dims, self.R = n, dims, R
+        self.px = dims[0] * dims[1] * dims[2]
+        self.cells = self.px // UNIT
+        self.sent = []
+
+    @staticmethod
+    def pixels(i):
+        return pl.ds(i * 16 * UNIT, 16 * UNIT)
+
+    def norm_sums(self, grad_of, source, mean, inv, gain, rnd):
+        R = self.R
+
+        def body(i, carry):
+            dg, db = carry
+            at = self.pixels(i)
+            unit = (source[at, :].astype(F32) - over_cells(mean, i)) * over_cells(inv, i)
+            d = grad_of(i, unit)
+            R.norm[at, :] = unit
+            e = d * gain
+            R.part[at, :] = e
+            cross = d * unit
+            here = pl.ds(i * 16, 16)
+            R.tmp_a[here, :] = jnp.sum(e.reshape(16, UNIT, C), axis=1)
+            R.tmp_b[here, :] = jnp.sum((cross * gain).reshape(16, UNIT, C), axis=1)
+            return (dg + jnp.sum(cross, axis=0, keepdims=True), db + jnp.sum(d, axis=0, keepdims=True))
+
+        zero = jnp.zeros((1, C), F32)
+        dg, db = lax.fori_loop(0, self.cells // 16, body, (zero, zero))
+        R.buf[rnd, 0] = pack([group_totals(R.pick, R.tmp_a[...]), group_totals(R.pick, R.tmp_b[...])])
+        copies = spread_copies(self.n, R.buf, R.send, R.recv, rnd)
+        for cp in copies:
+            cp.start()
+        self.sent = self.sent + copies
+        return copies, dg, db
+
+    def norm_finish(self, copies, rnd, inv, emit):
+        R = self.R
+        for cp in copies:
+            cp.wait_recv()
+        gathered = jnp.sum(R.buf[rnd], axis=0) / R.div[...]
+        R.tmp_a[...] = split_dot(R.spread[...], unpack(gathered))
+        R.tmp_b[...] = split_dot(R.spread[...], unpack(shift_down(gathered, 1)))
+
+        def body(i, _):
+            at = self.pixels(i)
+            emit(i, over_cells(inv, i) * (
+                R.part[at, :] - over_cells(R.tmp_a, i) - R.norm[at, :] * over_cells(R.tmp_b, i)))
+            return 0
+
+        lax.fori_loop(0, self.cells // 16, body, 0)
+
+    def send_rows(self, source, rnd):
+        R = self.R
+        canvases, rows, width = self.dims
+
+        def one(v, r):
+            at = pl.ds(pl.multiple_of((v * rows + r) * width, width), width)
+            R.d3[v, r + 1] = shift_columns(source[at, :].astype(F32), R.col_l[v, r + 1], R.col_r[v, r + 1])
+
+        def edges(v, _):
+            one(v, 0)
+            one(v, rows - 1)
+            return 0
+
+        lax.fori_loop(0, canvases, edges, 0)
+        mid = pl.ds(C, C)
+        up, down = halo_copies(self.n, R.d3.at[:, 1, :, mid], R.d3.at[:, rows, :, mid], R.halo.at[rnd],
+                               R.hsend.at[rnd], R.hrecv.at[rnd])
+        start_halo(self.n, up, down)
+
+        def inner(i, _):
+            one(i // (rows - 2), 1 + lax.rem(i, rows - 2))
+            return 0
+
+        if rows > 2:
+            lax.fori_loop(0, canvases * (rows - 2), inner, 0)
+        return up, down
+
+    def finish_rows(self, up, down, rnd):
+        R = self.R
+        canvases, rows, _ = self.dims
+        wait_halo(self.n, up, down, R.halo.at[rnd], 0.0)
+        for v in range(canvases):
+            for side, r in ((0, 0), (1, rows + 1)):
+                R.d3[v, r] = shift_columns(R.halo[rnd, side, v].astype(F32), R.col_l[v, r], R.col_r[v, r])
+
+    def convolve_back(self, weights, pump=no_pump):
+        R = self.R
+        canvases, rows, width = self.dims
+        plane = rows * width
+        nt = (((1,), (1,)), ((), ()))
+        for v in range(canvases):
+            at = pl.ds(v * plane, plane)
+            total = None
+            for dr in (1, 0, 2):
+                acc = None
+                for dc in range(3):
+                    ref, row = weights(3 * (2 - dr) + (2 - dc))
+                    lhs = R.d3[v, dr : dr + rows, :, dc * C : (dc + 1) * C].reshape(plane, C)
+                    term = lax.dot_general(lhs, ref[row : row + C, :], nt, preferred_element_type=F32)
+                    acc = term if acc is None else acc + term
+                if dr == 0:
+                    acc = acc * wide(R.row_u[at, :])
+                if dr == 2:
+                    acc = acc * wide(R.row_d[at, :])
+                total = acc if total is None else total + acc
+                pump()
+            R.part[at, :] = total
+
+    def mask_rows(self, source):
+        R = self.R
+
+        def body(i, _):
+            at = self.pixels(i)
+            value = source[at, :].astype(F32)
+            R.low_u[at, :] = (value * wide(R.row_u[at, :])).astype(B16)
+            R.low_d[at, :] = (value * wide(R.row_d[at, :])).astype(B16)
+            return 0
+
+        lax.fori_loop(0, self.cells // 16, body, 0)
+
+    def weight_grad(self, s, grad, dest, pump=no_pump):
+        R = self.R
+        canvases, rows, width = self.dims
+        plane = rows * width
+        tn = (((0,), (0,)), ((), ()))
+        for dr, source in ((0, R.low_u), (1, grad), (2, R.low_d)):
+            for dc in range(3):
+                acc = None
+                for v in range(canvases):
+                    lhs = s[v, dr : dr + rows, :, dc * C : (dc + 1) * C].reshape(plane, C)
+                    term = lax.dot_general(
+                        lhs, source[v * plane : (v + 1) * plane, :], tn, preferred_element_type=F32)
+                    acc = term if acc is None else acc + term
+                ref, row = dest(3 * dr + dc)
+                ref[row : row + C, :] = acc.astype(B16)
+                pump()
+
+
+def back_kernel(columns, n, dims, R):
+    g = Grid(columns, n)
+    half = R.sum_low.shape[0]
+    group = Group(g, 1, half)
+    load_s = pltpu.make_async_copy(R.s2, R.s, R.lsem.at[0])
+    load_s.start()
+    load_k = second_matrix(R.top, R.bottom, R.k, R.ksem)
+    load_att = pltpu.make_async_copy(R.datt, R.g_low.at[pl.ds(7 * C, 4 * C)], R.lsem.at[1])
+    for cp in load_k + [load_att]:
+        cp.start()
+    greet_all(g)
+    vec = R.vec
+    back = Backer(n, dims, R)
+    copies, dg3, db3 = back.norm_sums(lambda i, unit: R.du[back.pixels(i), :], R.hid, R.mean3, R.inv3, vec[6:7, :], 0)
+
+    def emit_hidden(i, value):
+        at = back.pixels(i)
+        total = R.cot[at, :].astype(F32) + value
+        R.dh[at, :] = total
+        R.grad[at, :] = total.astype(B16)
+
+    back.norm_finish(copies, 0, R.inv3, emit_hidden)
+    up, down = back.send_rows(R.grad, 0)
+    back.mask_rows(R.grad)
+    load_s.wait()
+
+    def dest_two(tap):
+        return (R.g_top, (9 + tap) * C) if tap < 2 else (R.g_low, (tap - 2) * C)
+
+    back.weight_grad(R.s, R.grad, dest_two)
+    load_s = pltpu.make_async_copy(R.s1, R.s, R.lsem.at[0])
+    load_s.start()
+    load_att.wait()
+    engine = Engine(reduce_pieces(group, R.g_low, R.sum_low, *R.reduce))
+    engine.pump()
+    dc2 = jnp.sum(R.grad[...].astype(F32), axis=0, keepdims=True)
+    back.finish_rows(up, down, 0)
+    for cp in load_k:
+        cp.wait()
+    back.convolve_back(lambda tap: (R.k, tap * C), engine.pump)
+    gain2, bias2 = vec[3:4, :], vec[4:5, :]
+
+    def grad_two(i, unit):
+        return R.part[back.pixels(i), :] * silu_slope(unit * gain2 + bias2)
+
+    copies, dg2, db2 = back.norm_sums(grad_two, R.y1, R.mean2, R.inv2, gain2, 1)
+    engine.pump(2)
+
+    def emit_grad(i, value):
+        R.grad[back.pixels(i), :] = value.astype(B16)
+
+    back.norm_finish(copies, 1, R.inv2, emit_grad)
+    engine.pump(2)
+    back.mask_rows(R.grad)
+    dc1 = jnp.sum(R.grad[...].astype(F32), axis=0, keepdims=True)
+    load_s.wait()
+    back.weight_grad(R.s, R.grad, lambda tap: (R.g_top, tap * C), engine.pump)
+    R.dvec[...] = jnp.concatenate([dc1, dg2, db2, dc2, dg3, db3, jnp.zeros((2, C), F32)], axis=0)
+    engine.finish()
+    for cp in back.sent:
+        cp.wait_send()
+
+
+def back_call(columns, n, dims, cot, du, hid, y1, norms, s1, s2, pick, spread, div, masks, vec, top, bottom, datt,
+              block_rows):
+    canvases, rows, width = dims
+    px = canvases * rows * width
+    cells = px // UNIT
+    stats = canvases * CROPS
+    dma = pltpu.SemaphoreType.DMA
+    names = ("mean2", "inv2", "mean3", "inv3")
+    inputs = dict(cot=(cot, vmem), du=(du, vmem), hid=(hid, vmem), y1=(y1, vmem), s1=(s1, anyw), s2=(s2, anyw),
+                  pick=(pick, vmem), spread=(spread, vmem), div=(div, vmem), vec=(vec, vmem), top=(top, anyw),
+                  bottom=(bottom, anyw), datt=(datt, anyw),
+                  **{k: (v, vmem) for k, v in zip(names, norms)},
+                  **{k: (v, vmem) for k, v in zip(("col_l", "col_r", "row_u", "row_d"), masks)})
+    outputs = dict(dh=((px, C), F32, vmem), grad=((px, C), B16, vmem), g_top=((11 * C, C), B16, vmem),
+                   dvec=((8, C), F32, vmem), sum_low=((block_rows // 2, C), B16, vmem))
+    scratch = dict(
+        g_low=pltpu.VMEM((11 * C, C), B16), s=pltpu.VMEM(s1.shape, B16), k=pltpu.VMEM((9 * C, C), B16),
+        d3=pltpu.VMEM(s1.shape, B16), low_u=pltpu.VMEM((px, C), B16), low_d=pltpu.VMEM((px, C), B16),
+        part=pltpu.VMEM((px, C), F32), norm=pltpu.VMEM((px, C), F32),
+        halo=pltpu.VMEM((1, 2, canvases, width, C), B16), buf=pltpu.VMEM((2, n, stats, LANES), F32),
+        tmp_a=pltpu.VMEM((cells, C), F32), tmp_b=pltpu.VMEM((cells, C), F32),
+        reduce=reduce_pieces_scratch(columns, n, block_rows // 2), lsem=dma((5,)), ksem=dma((3,)),
+        send=dma((2, n)), recv=dma((2, n)), hsend=dma((1, 2)), hrecv=dma((1, 2)))
+    return named_call(functools.partial(back_kernel, columns, n, dims), "back", 7, inputs, outputs, scratch)
+
+
+def update_kernel(columns, n, dims, R):
+    g = Grid(columns, n)
+    half = R.w.shape[0] // 2
+    upper, lower = Group(g, 0, half), Group(g, 1, half)
+    load_k = pltpu.make_async_copy(R.top.at[pl.ds(0, 9 * C)], R.k, R.ksem.at[0])
+    load_k.start()
+    load_g = pltpu.make_async_copy(R.g_in, R.g_top, R.ksem.at[1])
+    load_g.start()
+    load_p = pltpu.make_async_copy(R.bottom.at[pl.ds(10 * C, C)], R.wp, R.ksem.at[2])
+    load_p.start()
+    greet_all(g)
+    vec = R.vec
+    lower.to_owner(R.sum_low, R.totals.at[1], R.asend.at[1], R.arecv.at[1], True)
+    load_g.wait()
+    reducer = Engine(reduce_pieces(upper, R.g_top, R.sum_top, *R.reduce))
+    reducer.pump()
+    back = Backer(n, dims, R)
+    up, down = back.send_rows(R.grad, 0)
+    reducer.pump(2)
+
+    def adam(group, totals):
+        @pl.when(group.is_owner)
+        def _():
+            total = totals[...].astype(F32)
+            next_w, R.new_m[...], R.new_s[...] = adam_update(R.w[...], total, R.m[...], R.v[...], matrix_rate)
+            R.new_w[...] = next_w
+            R.fresh[...] = next_w.astype(B16)
+
+    load_p.wait()
+    for v in range(dims[0]):
+        at = pl.ds(v * dims[1] * dims[2], dims[1] * dims[2])
+        R.output[at, :] = (
+            R.hid[at, :] + jnp.dot(R.o[at, :], R.wp[...], preferred_element_type=F32) + vec[10:11, :])
+    lower.block_arrived(R.sum_low, R.totals.at[1], R.asend.at[1], R.arecv.at[1])
+    adam(lower, R.totals.at[1])
+    lower.to_pieces(R.fresh, R.pieces.at[1], R.tsend.at[1], R.trecv.at[1], True)
+    reducer.pump(2)
+    back.finish_rows(up, down, 0)
+    load_k.wait()
+    back.convolve_back(lambda tap: (R.k, tap * C), reducer.pump)
+    lower.piece_arrived(R.fresh, R.pieces.at[1], R.tsend.at[1], R.trecv.at[1])
+    gather_low = Engine(gather_pieces(lower, R.pieces.at[1], R.new_low, *R.gather1))
+    gain1, bias1 = vec[0:1, :], vec[1:2, :]
+
+    def grad_one(i, unit):
+        return R.part[back.pixels(i), :] * silu_slope(unit * gain1 + bias1)
+
+    copies, dg1, db1 = back.norm_sums(grad_one, R.x, R.mean1, R.inv1, gain1, 0)
+    reducer.pump(2)
+    R.vbuf[g.h] = jnp.concatenate([dg1, db1, R.dvec[0:6, :], R.dvec_att[...]], axis=0)
+    vector_sends = [
+        remote(R.vbuf.at[g.h], R.vbuf.at[g.h], R.vsend.at[d], R.vrecv.at[g.h],
+               {"canvas": g.c, "height": lax.rem(g.h + d, n)})
+        for d in range(1, n)
+    ]
+    for cp in vector_sends:
+        cp.start()
+
+    def emit_input(i, value):
+        at = back.pixels(i)
+        R.igrad[at, :] = R.dh[at, :] + value
+
+    back.norm_finish(copies, 0, R.inv1, emit_input)
+    reducer.pump(2)
+    for d in range(1, n):
+        src = lax.rem(g.h + d, n)
+        remote(R.vbuf.at[src], R.vbuf.at[src], R.vsend.at[d], R.vrecv.at[src],
+               {"canvas": g.c, "height": src}).wait_recv()
+    R.vtrade[0, 0] = jnp.sum(R.vbuf[...], axis=0)
+
+    def trade(k):
+        return remote(R.vtrade.at[k, 0], R.vtrade.at[k, 1], R.qsend.at[k], R.qrecv.at[k], g.mate(k))
+
+    trade(0).start()
+    reducer.finish()
+    upper.to_owner(R.sum_top, R.totals.at[0], R.asend.at[0], R.arecv.at[0], True)
+    gather_low.pump()
+    for k in range(g.phases):
+        trade(k).wait_recv()
+        R.vtrade[k + 1, 0] = R.vtrade[k, 0] + R.vtrade[k, 1]
+        if k + 1 < g.phases:
+            trade(k + 1).start()
+    R.new_vw[...], R.new_vm[...], R.new_vs[...] = adam_update(
+        R.vw[...], R.vtrade[g.phases, 0], R.vm[...], R.vs[...], vector_rate)
+    upper.block_arrived(R.sum_top, R.totals.at[0], R.asend.at[0], R.arecv.at[0])
+    adam(upper, R.totals.at[0])
+    upper.to_pieces(R.fresh, R.pieces.at[0], R.tsend.at[0], R.trecv.at[0], True)
+    gather_low.pump()
+    upper.piece_arrived(R.fresh, R.pieces.at[0], R.tsend.at[0], R.trecv.at[0])
+    gather_top = Engine(gather_pieces(upper, R.pieces.at[0], R.new_top, *R.gather0))
+    gather_top.pump()
+    for _ in range(2 * g.seats + 2):
+        gather_low.pump()
+        gather_top.pump()
+    gather_low.finish()
+    gather_top.finish()
+    for cp in back.sent + vector_sends:
+        cp.wait_send()
+    for k in range(g.phases):
+        trade(k).wait_send()
+    for i, group in enumerate((upper, lower)):
+        group.to_owner((R.sum_top, R.sum_low)[i], R.totals.at[i], R.asend.at[i], R.arecv.at[i], False)
+        group.to_pieces(R.fresh, R.pieces.at[i], R.tsend.at[i], R.trecv.at[i], False)
+
+
+def update_call(columns, n, dims, grad, dh, x, mean1, inv1, pick, spread, div, masks, vec, top, bottom, g_top, sum_low, dvec,
+                dvec_att, w, m, v, vw, vm, vs, hid, o):
+    canvases, rows, width = dims
+    px = canvases * rows * width
+    cells = px // UNIT
+    stats = canvases * CROPS
+    block = w.shape
+    half = block[0] // 2
+    seats, phases = n // 2, columns.bit_length() - 1
+    dma = pltpu.SemaphoreType.DMA
+    tall = (canvases, rows + 2, width, 3 * C)
+    arrays = dict(grad=grad, dh=dh, x=x, mean1=mean1, inv1=inv1, pick=pick, spread=spread, div=div, vec=vec,
+                  g_in=g_top, sum_low=sum_low, dvec=dvec, dvec_att=dvec_att, w=w, m=m, v=v, vw=vw, vm=vm, vs=vs, hid=hid, o=o)
+    inputs = dict(top=(top, anyw), bottom=(bottom, anyw), **{k: (a, vmem) for k, a in arrays.items()},
+                  **{k: (a, vmem) for k, a in zip(("col_l", "col_r", "row_u", "row_d"), masks)})
+    inputs["g_in"] = (g_top, anyw)
+    outputs = dict(igrad=((px, C), F32, vmem), output=((px, C), F32, vmem), new_w=(block, F32, vmem), new_m=(block, F32, vmem),
+                   new_s=(block, F32, vmem), new_vw=(vw.shape, F32, vmem), new_vm=(vw.shape, F32, vmem),
+                   new_vs=(vw.shape, F32, vmem), new_top=((11 * C, C), B16, anyw), new_low=((11 * C, C), B16, anyw))
+    scratch = dict(
+        g_top=pltpu.VMEM((11 * C, C), B16), sum_top=pltpu.VMEM((half, C), B16), totals=pltpu.VMEM((2,) + block, B16),
+        fresh=pltpu.VMEM(block, B16), pieces=pltpu.VMEM((2, half, C), B16), k=pltpu.VMEM((9 * C, C), B16),
+        d3=pltpu.VMEM(tall, B16), part=pltpu.VMEM((px, C), F32), norm=pltpu.VMEM((px, C), F32),
+        halo=pltpu.VMEM((1, 2, canvases, width, C), B16), buf=pltpu.VMEM((1, n, stats, LANES), F32),
+        tmp_a=pltpu.VMEM((cells, C), F32), tmp_b=pltpu.VMEM((cells, C), F32),
+        vbuf=pltpu.VMEM((n,) + vw.shape, F32), vtrade=pltpu.VMEM((phases + 1, 2) + vw.shape, F32),
+        reduce=reduce_pieces_scratch(columns, n, half), gather0=gather_pieces_scratch(columns, n),
+        gather1=gather_pieces_scratch(columns, n), wp=pltpu.VMEM((C, C), B16), ksem=dma((3,)), asend=dma((2, 1)), arecv=dma((2, 2)),
+        tsend=dma((2, 2)), trecv=dma((2, 1)), vsend=dma((n,)), vrecv=dma((n,)), qsend=dma((phases,)),
+        qrecv=dma((phases,)), send=dma((1, n)), recv=dma((1, n)), hsend=dma((1, 2)), hrecv=dma((1, 2)))
+    return named_call(functools.partial(update_kernel, columns, n, dims), "update", 9, inputs, outputs, scratch)
+
+
+def attend_kernel(n, keep, R):
+    me = lax.axis_index("height")
+    half = n // 2
+    mine = me // half
+    base = mine * half
+    core = lax.rem(me, 2)
+    partner = lax.rem(me + half, n)
+    sibling = other_core(me)
+    mates = half // 2
+    seat = (me - base) // 2
+    seg = R.u.shape[1]
+    total = n * seg
+    scale = C ** (-0.5)
+    nt = (((1,), (1,)), ((), ()))
+    tn = (((0,), (0,)), ((), ()))
+    vec = R.vec
+
+    def mate(j, c=core):
+        return base + c + 2 * lax.rem(seat + j, mates)
+
+    def far_of(b):
+        return lax.rem(b + half, n)
+
+    def to(h):
+        return {"canvas": lax.axis_index("canvas"), "height": h}
+
+    loads = [pltpu.make_async_copy(R.low.at[pl.ds(7 * C, 4 * C)], R.w, R.lsem.at[0])]
+    if keep:
+        loads += [
+            pltpu.make_async_copy(R.far_cot, R.dz.at[pl.ds(0, seg)], R.lsem.at[1]),
+            pltpu.make_async_copy(R.cot.at[mine], R.dz.at[pl.ds(seg, seg)], R.lsem.at[2]),
+        ]
+    for cp in loads:
+        cp.start()
+    own = pltpu.make_async_copy(R.u_in.at[mine], R.u.at[me], R.lsem.at[3])
+    own.start()
+    barrier = pltpu.get_barrier_semaphore()
+    peers = [partner, sibling] + [mate(j) for j in range(1, mates)]
+    for p in peers:
+        pl.semaphore_signal(barrier, inc=1, device_id=to(p), device_id_type=MESH)
+    pl.semaphore_wait(barrier, len(peers))
+    started = []
+
+    def push(src, slot, dest):
+        cp = remote(src, R.u.at[slot], R.gsend.at[len(started)], R.grecv.at[slot], to(dest))
+        cp.start()
+        started.append(cp)
+
+    def block(b):
+        return pl.ds(pl.multiple_of(b * seg, seg), seg)
+
+    def project(b):
+        piece = R.u[b]
+        R.k[block(b), :] = jnp.dot(piece, R.w[C : 2 * C, :], preferred_element_type=F32).astype(B16)
+        R.v[block(b), :] = (
+            jnp.dot(piece, R.w[2 * C : 3 * C, :], preferred_element_type=F32) + vec[9:10, :]
+        ).astype(B16)
+
+    def arrived(slot):
+        remote(R.u_in.at[0], R.u.at[slot], R.gsend.at[0], R.grecv.at[slot], to(partner)).wait_recv()
+
+    push(R.u_in.at[1 - mine], me, partner)
+    for j in range(1, mates):
+        push(R.u_in.at[mine], me, mate(j))
+    push(R.u_in.at[mine], me, sibling)
+    for cp in loads:
+        cp.wait()
+    own.wait()
+    project(me)
+    arrived(sibling)
+    project(sibling)
+    key_ids = jnp.concatenate([R.ids_all[b, pl.ds(mine, 1), :] for b in range(n)], axis=1)
+    for i, b in enumerate((partner, me)):
+        turned = jnp.transpose(R.ids_all[b])
+        picked = jnp.where(mine == 0, turned[:, 0:1], turned[:, 1:2])
+        R.qid[i * seg : (i + 1) * seg, :] = jnp.broadcast_to(picked, (seg, LANES))
+    if keep:
+        R.dout[...] = lax.dot_general(
+            R.dz[...], R.w[3 * C : 4 * C, :], nt, preferred_element_type=F32).astype(B16)
+    arrived(partner)
+    for j in range(1, mates):
+        push(R.u.at[partner], partner, mate(j))
+    push(R.u.at[partner], partner, sibling)
+    project(partner)
+    for j in range(1, mates):
+        friend = mate(mates - j)
+        arrived(friend)
+        push(R.u.at[friend], friend, sibling)
+        project(friend)
+    arrived(far_of(sibling))
+    project(far_of(sibling))
+    for j in range(1, mates):
+        friend = far_of(mate(mates - j))
+        arrived(friend)
+        push(R.u.at[friend], friend, sibling)
+        project(friend)
+    for j in range(1, mates):
+        friend = mate(mates - j, 1 - core)
+        arrived(friend)
+        project(friend)
+        arrived(far_of(friend))
+        project(far_of(friend))
+
+    rows = R.rows
+    per = seg // rows
+    o_home = R.o_home
+    far_out = remote(R.out.at[pl.ds(0, seg)], o_home.at[mine], R.osem.at[0], R.osem.at[1], to(partner))
+
+    def attend(i, _):
+        at = pl.ds(pl.multiple_of(i * rows, rows), rows)
+        b = jnp.where(i < per, partner, me)
+        uq = R.u[b, pl.ds(pl.multiple_of(lax.rem(i, per) * rows, rows), rows), :]
+        qb = (jnp.dot(uq, R.w[0:C, :], preferred_element_type=F32) + vec[8:9, :]).astype(B16)
+        s = lax.dot_general(qb, R.k[...], nt, preferred_element_type=F32) * scale
+        s = jnp.where(R.qid[at, :][:, :1] == key_ids, s, mask_fill)
+        e = jnp.exp(s - jnp.max(s, axis=1, keepdims=True))
+        p = e * (1.0 / jnp.sum(e, axis=1, keepdims=True))
+        pb = p.astype(B16)
+        R.out[at, :] = jnp.dot(pb, R.v[...], preferred_element_type=F32).astype(B16)
+        if keep:
+            R.pbuf[at, :] = pb
+            R.q[at, :] = qb
+            dp = lax.dot_general(R.dout[at, :], R.v[...], nt, preferred_element_type=F32)
+            delta = jnp.sum(p * dp, axis=1, keepdims=True)
+            ds = (p * (dp - delta)).astype(B16)
+            R.sbuf[at, :] = ds
+            R.dq[at, :] = (jnp.dot(ds, R.k[...], preferred_element_type=F32) * scale).astype(B16)
+
+        @pl.when(i == per - 1)
+        def _():
+            far_out.start()
+
+        return 0
+
+    lax.fori_loop(0, 2 * per, attend, 0)
+    own_out = pltpu.make_async_copy(R.out.at[pl.ds(seg, seg)], o_home.at[mine], R.lsem.at[4])
+    own_out.start()
+    if not keep:
+        own_out.wait()
+        far_out.wait_recv()
+        bias = vec[10:11, :]
+        for v in range(2):
+            at = pl.ds(v * seg, seg)
+            R.final[at, :] = (
+                R.hid[at, :] + jnp.dot(o_home[v], R.w[3 * C : 4 * C, :], preferred_element_type=F32) + bias)
+        far_out.wait_send()
+        for cp in started:
+            cp.wait_send()
+        return
+    zero = jnp.zeros((C, C), F32)
+    pairs = 2 * mates
+
+    def share(b, carry):
+        dwk, dwv, dbv = carry
+        at = block(b)
+        dk = (lax.dot_general(R.sbuf[:, at], R.q[...], tn, preferred_element_type=F32) * scale).astype(B16)
+        dvf = lax.dot_general(R.pbuf[:, at], R.dout[...], tn, preferred_element_type=F32)
+        dv = dvf.astype(B16)
+        du = lax.dot_general(dk, R.w[C : 2 * C, :], nt, preferred_element_type=F32)
+        du = du + lax.dot_general(dv, R.w[2 * C : 3 * C, :], nt, preferred_element_type=F32)
+        piece = R.u[b]
+        dwk = dwk + lax.dot_general(piece, dk, tn, preferred_element_type=F32)
+        dwv = dwv + lax.dot_general(piece, dv, tn, preferred_element_type=F32)
+        return du, (dwk, dwv, dbv + jnp.sum(dvf, axis=0, keepdims=True))
+
+    def place(t):
+        other = t < pairs - 2
+        return jnp.where(other, t // 2 + 1, 0), 1 - lax.rem(t, 2)
+
+    def sib_copy(t):
+        return remote(R.for_sib.at[t], R.from_sib.at[t], R.ssend.at[t], R.srecv.at[t], to(sibling))
+
+    def mate_copy(t):
+        j, _ = place(t)
+        return remote(R.sums.at[t], R.from_mate.at[t], R.msend.at[t], R.mrecv.at[t], to(mate(j)))
+
+    def back(t, carry):
+        j, far = place(t)
+        theirs, ours = mate(j, 1 - core), mate(j)
+        du, carry = share(lax.rem(theirs + far * half, n), carry)
+        R.for_sib[t] = du.astype(B16)
+        sib_copy(t).start()
+        du, carry = share(lax.rem(ours + far * half, n), carry)
+        sib_copy(t).wait_recv()
+        R.sums[t] = (du + R.from_sib[t].astype(F32)).astype(B16)
+
+        @pl.when(t < pairs - 2)
+        def _():
+            mate_copy(t).start()
+
+        return carry
+
+    dwk, dwv, dbv = lax.fori_loop(0, pairs, back, (zero, zero, jnp.zeros((1, C), F32)))
+
+    def gathered(far):
+        at = pl.ds(0, seg) if far else pl.ds(seg, seg)
+        value = lax.dot_general(R.dq[at, :], R.w[0:C, :], nt, preferred_element_type=F32)
+        value = value + R.sums[pairs - 1 - far].astype(F32)
+        for j in range(1, mates):
+            t = 2 * (j - 1) + 1 - far
+            mate_copy(t).wait_recv()
+            value = value + R.from_mate[t].astype(F32)
+        return value
+
+    R.for_home[...] = gathered(1).astype(B16)
+    home = remote(R.for_home, R.from_partner, R.hsem.at[0], R.hsem.at[1], to(partner))
+    home.start()
+    R.du[mine] = gathered(0)
+    R.dw[C : 2 * C, :] = dwk.astype(B16)
+    R.dw[2 * C : 3 * C, :] = dwv.astype(B16)
+    R.dw[3 * C : 4 * C, :] = lax.dot_general(
+        R.out[...], R.dz[...], tn, preferred_element_type=F32).astype(B16)
+    dwq = lax.dot_general(R.u[partner], R.dq[0:seg, :], tn, preferred_element_type=F32)
+    dwq = dwq + lax.dot_general(R.u[me], R.dq[seg : 2 * seg, :], tn, preferred_element_type=F32)
+    R.dw[0:C, :] = dwq.astype(B16)
+    R.dvec[...] = jnp.concatenate(
+        [
+            jnp.sum(R.dq[...].astype(F32), axis=0, keepdims=True),
+            dbv,
+            jnp.sum(R.dz[...].astype(F32), axis=0, keepdims=True),
+            jnp.zeros((5, C), F32),
+        ],
+        axis=0,
+    )
+    home.wait_recv()
+    R.du[1 - mine] = R.from_partner[...].astype(F32)
+    home.wait_send()
+    own_out.wait()
+    far_out.wait()
+    for cp in started:
+        cp.wait_send()
+
+    def drain(t, _):
+        sib_copy(t).wait_send()
+
+        @pl.when(t < pairs - 2)
+        def _():
+            mate_copy(t).wait_send()
+
+        return 0
+
+    lax.fori_loop(0, pairs, drain, 0)
+
+
+def attend_call(n, keep, cid, u, ids_all, vec, low, cot=None, far_cot=None, hid=None):
+    seg = u.shape[1]
+    half = n // 2
+    mates = half // 2
+    pairs = 2 * mates
+    total = n * seg
+    dma = pltpu.SemaphoreType.DMA
+    inputs = dict(u_in=(u, anyw), ids_all=(ids_all, vmem), vec=(vec, vmem), low=(low, anyw))
+    piece = (seg, C)
+    home = (2,) + piece
+    scratch = dict(
+        u=pltpu.VMEM((n,) + piece, B16), w=pltpu.VMEM((4 * C, C), B16), k=pltpu.VMEM((total, C), B16),
+        v=pltpu.VMEM((total, C), B16), qid=pltpu.VMEM((2 * seg, LANES), F32), out=pltpu.VMEM((2 * seg, C), B16),
+        lsem=dma((5,)), gsend=dma((4 * mates,)), grecv=dma((n,)), osem=dma((2,)))
+    if keep:
+        inputs.update(cot=(cot, anyw), far_cot=(far_cot, anyw))
+        outputs = dict(o_home=(home, B16, anyw), dw=((4 * C, C), B16, vmem), dvec=((8, C), F32, vmem),
+                       du=(home, F32, vmem))
+        scratch.update(
+            dz=pltpu.VMEM((2 * seg, C), B16), dout=pltpu.VMEM((2 * seg, C), B16), q=pltpu.VMEM((2 * seg, C), B16),
+            dq=pltpu.VMEM((2 * seg, C), B16), pbuf=pltpu.VMEM((2 * seg, total), B16),
+            sbuf=pltpu.VMEM((2 * seg, total), B16), for_sib=pltpu.VMEM((pairs,) + piece, B16),
+            from_sib=pltpu.VMEM((pairs,) + piece, B16), sums=pltpu.VMEM((pairs,) + piece, B16),
+            from_mate=pltpu.VMEM((pairs - 2,) + piece, B16), for_home=pltpu.VMEM(piece, B16),
+            from_partner=pltpu.VMEM(piece, B16), ssend=dma((pairs,)), srecv=dma((pairs,)), msend=dma((pairs,)),
+            mrecv=dma((pairs,)), hsem=dma((2,)))
+    else:
+        inputs.update(hid=(hid, vmem))
+        outputs = dict(final=((2 * seg, C), F32, vmem))
+        scratch.update(o_home=pltpu.VMEM(home, B16))
+
+    def kernel(R):
+        R.rows = min(256, seg)
+        attend_kernel(n, keep, R)
+
+    return named_call(kernel, "attend" if keep else "attend_again", cid, inputs, outputs, scratch)
+
+
 def rounded_vectors(vectors):
     return lax.reduce_precision(vectors, exponent_bits=8, mantissa_bits=7)
 
@@ -1439,13 +2566,12 @@
     mine = me // half
     partner = lax.rem(me + half, n)
     swap = [(i, (i + half) % n) for i in range(n)]
-
     count = vectors.shape[0]
+    joined = columns == 4 and params.shape[0] % 32 == 0 and rows > 2
 
     def padded(value):
         return jnp.pad(value, ((0, 16 - count), (0, 0)))
 
-    whole = spread_call(columns, n, 8, params).reshape(-1, channels)
     wide_vectors = padded(vectors)
     vec = rounded_vectors(wide_vectors)
     cell_ids = crop_ids[:, :, ::UNIT] + CROPS * jnp.arange(canvases, dtype=jnp.int32)[:, None, None]
@@ -1458,46 +2584,76 @@
     ids_lane = jnp.pad(ids.reshape(canvases, plane), ((0, 8 - canvases), (0, 0)))
     x = latents.reshape(px, channels)
     cot = cotangent.reshape(px, channels)
-    ids_all, mean1, inv1, div, cnt, *masks = layout_call(n, dims, x, pick, spread, ids_px, ids_lane)
-    canvas_ids = lax.dynamic_index_in_dim(ids_all, mine, axis=1, keepdims=False)
-    key_ids = canvas_ids.reshape(1, n * plane)
-    query_ids = jnp.stack([canvas_ids[me], canvas_ids[partner]]).reshape(2 * plane, 1)
-    query_ids = jnp.broadcast_to(query_ids, (2 * plane, LANES))
-    offsets = jnp.stack([me, partner]) * plane
     cot3 = cotangent.reshape(canvases, plane, channels)
-    own_cot = lax.dynamic_index_in_dim(cot3, mine, axis=0, keepdims=False)
-    far_cot = lax.ppermute(
-        lax.dynamic_index_in_dim(cot3, 1 - mine, axis=0, keepdims=False), "height", swap)
-    dz = jnp.concatenate([own_cot, far_cot], axis=0)
-
-    def attention_output(o, hid, weight, bias):
-        o = o.reshape(2, plane, channels)
-        back = lax.ppermute(o[1], "height", swap)
-        ordered = jnp.where(mine == 0, jnp.stack([o[0], back]), jnp.stack([back, o[0]]))
-        product = jnp.dot(ordered.reshape(px, channels), weight, preferred_element_type=F32)
-        return hid + product + bias
-
-    hid, u, y1, s1, s2, mean2, inv2, mean3, inv3 = resnet_forward_call(
-        n, dims, True, x, pick, spread, cnt, mean1, inv1, masks, vec, whole)
-    ua = gather_call(n, 4, u.reshape(canvases, plane, channels))
-    o, dup, dw_att, dvec_att = attention_call(True, ua, key_ids, query_ids, offsets, dz, vec, whole)
-    first_output = attention_output(o, hid, whole[21 * C :], vec[10])
-    du = scatter_call(n, 6, dup.reshape(n, plane, channels)).reshape(px, channels)
-    norms = (mean1, inv1, mean2, inv2, mean3, inv3)
-    input_grad, matrix_grad, dvec = resnet_backward_call(
-        n, dims, 7, cot, du, hid, y1, x, norms, s1, s2, pick, spread, div, masks, vec, whole, dw_att)
-    vector_grad = jnp.concatenate([dvec, dvec_att], axis=0)
-    new_params, new_first, new_second, *new_small, new_whole = step_call(
-        columns, n, 9, matrix_grad.reshape((columns, half, 2) + params.shape), params, first_moment, second_moment,
-        vector_grad, wide_vectors, padded(vector_first), padded(vector_second))
+
+    if joined:
+        first = first_call(columns, n, dims, x, pick, spread, ids_px, ids_lane, vec, params, cot3)
+        ids_all, mean1, inv1, div, cnt = (first[k] for k in ("ids_all", "mean1", "inv1", "div", "cnt"))
+        masks = [first[k] for k in ("col_l", "col_r", "row_u", "row_d")]
+        hid, u, y1, s1, s2 = (first[k] for k in ("hid", "u", "y1_out", "s1_out", "s2_out"))
+        mean2, inv2, mean3, inv3 = (first[k] for k in ("mean2", "inv2", "mean3", "inv3"))
+        top, low = first["top"], first["bottom"]
+    else:
+        whole = spread_call(columns, n, 8, params).reshape(-1, channels)
+        top, low = whole[: 11 * C], whole[11 * C :]
+        ids_all, mean1, inv1, div, cnt, *masks = layout_call(n, dims, x, pick, spread, ids_px, ids_lane)
+        hid, u, y1, s1, s2, mean2, inv2, mean3, inv3 = resnet_forward_call(
+            n, dims, True, x, pick, spread, cnt, mean1, inv1, masks, vec, top, low)
+    small = (wide_vectors, padded(vector_first), padded(vector_second))
+    u = u.reshape(canvases, plane, channels)
+    if joined:
+        att = attend_call(n, True, 4, u, ids_all, vec, low, cot3, first["far_cot"])
+        du = att["du"].reshape(px, channels)
+        back = back_call(columns, n, dims, cot, du, hid, y1, (mean2, inv2, mean3, inv3), s1, s2, pick, spread, div,
+                         masks, vec, top, low, att["dw"], params.shape[0])
+        new = update_call(columns, n, dims, back["grad"], back["dh"], x, mean1, inv1, pick, spread, div, masks, vec,
+                          top, low, back["g_top"], back["sum_low"], back["dvec"], att["dvec"], params, first_moment,
+                          second_moment, *small, hid, att["o_home"].reshape(px, channels))
+        first_output = new["output"]
+        input_grad, new_params, new_first, new_second = (new[k] for k in ("igrad", "new_w", "new_m", "new_s"))
+        new_small = [new[k] for k in ("new_vw", "new_vm", "new_vs")]
+        new_vec = rounded_vectors(new_small[0])
+        hid2, u2 = resnet_forward_call(
+            n, dims, False, x, pick, spread, cnt, mean1, inv1, masks, new_vec, new["new_top"], new["new_low"])
+        second_output = attend_call(
+            n, False, 5, u2.reshape(canvases, plane, channels), ids_all, new_vec, new["new_low"], hid=hid2)["final"]
+    else:
+        own_cot = lax.dynamic_index_in_dim(cot3, mine, axis=0, keepdims=False)
+        far_cot = lax.ppermute(
+            lax.dynamic_index_in_dim(cot3, 1 - mine, axis=0, keepdims=False), "height", swap)
+        dz = jnp.concatenate([own_cot, far_cot], axis=0)
+        canvas_ids = lax.dynamic_index_in_dim(ids_all, mine, axis=1, keepdims=False)
+        key_ids = canvas_ids.reshape(1, n * plane)
+        query_ids = jnp.stack([canvas_ids[me], canvas_ids[partner]]).reshape(2 * plane, 1)
+        query_ids = jnp.broadcast_to(query_ids, (2 * plane, LANES))
+        offsets = jnp.stack([me, partner]) * plane
+
+        def attention_output(o, hid, low, bias):
+            back = lax.ppermute(o[plane:], "height", swap)
+            ordered = jnp.where(mine == 0, jnp.stack([o[:plane], back]), jnp.stack([back, o[:plane]]))
+            product = jnp.dot(ordered.reshape(px, channels), low[10 * C :], preferred_element_type=F32)
+            return hid + product + bias
+
+        ua = gather_call(n, 4, u)
+        o, dup, dw_att, dvec_att = attention_call(True, ua, key_ids, query_ids, offsets, dz, vec, low)
+        first_output = attention_output(o, hid, low, vec[10])
+        du = scatter_call(n, 6, dup.reshape(n, plane, channels)).reshape(px, channels)
+        norms = (mean1, inv1, mean2, inv2, mean3, inv3)
+        input_grad, matrix_grad, dvec = resnet_backward_call(
+            n, dims, 7, cot, du, hid, y1, x, norms, s1, s2, pick, spread, div, masks, vec, top, low, dw_att)
+        vector_grad = jnp.concatenate([dvec, dvec_att], axis=0)
+        new_params, new_first, new_second, *new_small, new_whole = step_call(
+            columns, n, 9, matrix_grad.reshape((columns, half, 2) + params.shape), params, first_moment,
+            second_moment, vector_grad, *small)
+        new_whole = new_whole.reshape(-1, channels)
+        new_top, new_low = new_whole[: 11 * C], new_whole[11 * C :]
+        new_vec = rounded_vectors(new_small[0])
+        hid2, u2 = resnet_forward_call(
+            n, dims, False, x, pick, spread, cnt, mean1, inv1, masks, new_vec, new_top, new_low)
+        ua2 = gather_call(n, 5, u2.reshape(canvases, plane, channels))
+        (o2,) = attention_call(False, ua2, key_ids, query_ids, offsets, dz, new_vec, new_low)
+        second_output = attention_output(o2, hid2, new_low, new_vec[10])
     new_vectors, new_vector_first, new_vector_second = [a[:count] for a in new_small]
-    new_whole = new_whole.reshape(-1, channels)
-    new_vec = rounded_vectors(new_small[0])
-    hid2, u2 = resnet_forward_call(
-        n, dims, False, x, pick, spread, cnt, mean1, inv1, masks, new_vec, new_whole)
-    ua2 = gather_call(n, 5, u2.reshape(canvases, plane, channels))
-    (o2,) = attention_call(False, ua2, key_ids, query_ids, offsets, dz, new_vec, new_whole)
-    second_output = attention_output(o2, hid2, new_whole[21 * C :], new_vec[10])
     shape = latents.shape
     return (
         hid.reshape(shape),

time: 710 us -> 572 us (0.81)
  Pallas kernels: 617 us -> 543 us
  waiting for transfers between devices: 45.2 us -> 0 us
  starting transfers between devices: 8.13 us -> 0 us
    ppermute x3 -> x0, waiting for transfers between devices: 45.2 us -> none  [the longest x2 45.2 us: attention_output(): back = lax.ppermute(o[1], 'height', swap)]
    pallas_call x2 -> x1, Pallas kernels: 83.3 us -> 39.5 us  [resnet_forward_call(): pl.pallas_call(functools.partial(resnet_forward_kernel, n, dims, keep), o...]
    pallas_call x9 -> x5, Pallas kernels: 534 us -> 503 us  [named_call(): pl.pallas_call(lambda *refs: kernel(Named(shapes, refs)), out_shape=[sds(...]
    ppermute x3 -> x0, starting transfers between devices: 8.13 us -> none  [the longest x1 4.1 us: body(): lax.ppermute(lax.dynamic_index_in_dim(cot3, 1 - mine, axis=0, keepdims=Fa...]
  transfers between devices with their start and end apart: 3 -> 0, of which waited for: 2 -> 0; matrix products, arithmetic and copies ran while one was open for 1% -> 0% of each run, Pallas kernels for 25% -> 0%
where the time goes in v2:
time: 572 us; the launch traced here: 566 us
  Pallas kernels  543 us (95%)
  local copies, waits for them, and re-layouts  16.9 us (3%)
    pallas_call x5, Pallas kernels, named_call(): pl.pallas_call(lambda *refs: kernel(Named(shapes, refs)), out_shape=[sds(...  503 us
    pallas_call x1, Pallas kernels, resnet_forward_call(): pl.pallas_call(functools.partial(resnet_forward_kernel, n, dims, keep), o...  39.5 us
    unnamed x34, local copies, waits for them, and re-layouts  13.1 us

profile of v2, /device:TPU:0, one launch (start us, length us, event | category | flops | bytes accessed | tf_op | source)
XLA Modules:
  0.0 565.8 jit_solution(8253023911328985314)
XLA Ops:
  0.6 1.4 fusion.2
  2.0 0.8 slice.12
  2.8 0.1 broadcast_add_fusion
  2.9 0.1 eq.28
  3.0 0.7 fusion.refs_2_.refs_7_.refs_8_.spread
  3.7 0.6 fusion.1.refs_1_.refs_6_.refs_7_.pick
  4.3 0.7 convert_element_type.17
  5.0 1.0 broadcast_in_dim.2.refs_3_
  6.0 0.1 reshape.66
  6.1 0.6 pad.14.refs_4_
  6.7 117.2 %first_forward.1 = (f32[8,8,512]{2,1,0:T(8,128)}, f32[128,512]{1,0:T(8,128)}, f32[128,512]{1,0:T(8,128)}, f32[32,128]{1,0:T(8,128)}, f32[32,128]{1,0:T(8,128)}, ...) custom-call(bf16[1024,512]{1,0:T(8,128)(2,1)} %bitcast.15, ...), custom_call_target="tpu_custom_call" | custom-call | tf_op jit(solution)/shard_map/first_forward/pallas_call | solution.py:1772
  123.9 115.5 %attend.1 = (bf16[2,512,512]{2,1,0:T(8,128)(2,1)}, bf16[2048,512]{1,0:T(8,128)(2,1)}, f32[8,512]{1,0:T(8,128)}, f32[2,512,512]{2,1,0:T(8,128)}) custom-call(bf16[2,512,512]{2,1,0:T(8,128)(2,1)} %bitcast.26, f32[8,8,512]{2,1,0:T(8,128)} %get-tuple-element.56.refs_1_, f32[16,512]{1,0:T(8,128)} %get-tuple-element.95.refs_5_.refs_2_.refs_9_.refs_10_, ...), custom_call_target="tpu_custom_call" | custom-call | tf_op jit(solution)/shard_map/attend/pallas_call | solution.py:1772
  239.4 0.0 copy-start.8
  239.4 0.0 copy-start.9
  239.4 62.4 %back.1 = (f32[1024,512]{1,0:T(8,128)}, bf16[1024,512]{1,0:T(8,128)(2,1)}, bf16[5632,512]{1,0:T(8,128)(2,1)}, f32[8,512]{1,0:T(8,128)}, bf16[176,512]{1,0:T(8,128)(2,1)}) custom-call(bf16[1024,512]{1,0:T(8,128)(2,1)} %bitcast.20, f32[1024,512]{1,0:T(8,128)} %bitcast.22, f32[1024,512]{1,0:T(8,128)} %get-tuple-element.52.refs_2_.refs_21_, ...), custom_call_target="tpu_custom_call" | custom-call | tf_op jit(solution)/shard_map/back/pallas_call | solution.py:1772
  301.8 0.0 copy-done.8
  301.8 0.6 pad.16.refs_19_
  302.4 0.0 copy-done.9
  302.4 0.6 pad.17.refs_20_
  303.1 131.6 %update.1 = (f32[1024,512]{1,0:T(8,128)}, f32[1024,512]{1,0:T(8,128)}, f32[352,512]{1,0:T(8,128)}, f32[352,512]{1,0:T(8,128)}, f32[352,512]{1,0:T(8,128)}, /*ind...) custom-call(bf16[5632,512]{1,0:T(8,128)(2,1)} %get-tuple-element.53., ...), custom_call_target="tpu_custom_call" | custom-call | tf_op jit(solution)/shard_map/update/pallas_call | solution.py:1772
  434.7 1.4 reduce_precision.7.vec.refs_2_
  436.0 39.5 %resnet_again.1 = (f32[1024,512]{1,0:T(8,128)}, bf16[1024,512]{1,0:T(8,128)(2,1)}) custom-call(bf16[1024,512]{1,0:T(8,128)(2,1)} %bitcast.17, bf16[32,128]{1,0:T(8,128)(2,1)} %fusion.1.refs_1_.refs_6_.refs_7_.pick, bf16[128,32]{1,0:T(8,128)(2,1)} %fusion.refs_2_.refs_7_.refs_8_.spread, f32[32,128]{1,0:T(8,128)} %get-tuple-element.82.cnt, ...), custom_call_target="tpu_custom_call" | custom-call | tf_op jit(solution)/shard_map/resnet_again/pallas_call | solution.py:516
  475.6 0.0 copy-start
  475.6 76.7 %attend_again.1 = f32[1024,512]{1,0:T(8,128)} custom-call(bf16[2,512,512]{2,1,0:T(8,128)(2,1)} %bitcast.27, f32[8,8,512]{2,1,0:T(8,128)} %get-tuple-element.56.refs_1_, f32[16,512]{1,0:T(8,128)} %reduce_precision.7.vec.refs_2_, bf16[5632,512]{1,0:T(8,128)(2,1)} %get-tuple-element.85.low.refs_3_, f32[1024,512]{1,0:T(8,128)} %get-tuple-element.87.refs_4_), custom_call_target="tpu_custom_call" | custom-call | tf_op jit(solution)/shard_map/attend_again/pallas_call | solution.py:1772
  552.3 0.0 copy-done
  552.3 0.0 copy-start.3
  552.3 1.3 copy.29
  553.6 1.0 copy-done.3
  554.7 0.0 copy-start.1
  554.7 1.3 copy.30
  556.0 1.0 copy-done.1
  557.0 0.0 copy-start.2
  557.0 1.3 copy.31
  558.3 1.0 copy-done.2
  559.4 0.0 copy-start.6
  559.4 0.0 copy-start.5
  559.4 1.3 copy.32
  560.7 0.3 copy-done.6
  561.0 0.0 copy-start.4
  561.0 0.0 copy-start.7
  561.0 0.0 copy-start.11
  561.0 0.0 copy-start.10
  561.0 0.9 copy.33
  561.8 0.0 copy-done.5
  561.8 0.9 copy.34
  562.7 0.0 copy-done.4
  562.7 0.9 copy.35
  563.6 0.0 copy-done.7
  563.6 0.6 copy.36
  564.2 0.0 copy-done.11
  564.2 0.6 copy.37
  564.8 0.0 copy-done.10
  564.8 0.6 copy.38
  (1 shorter events, 0.0 us)
Async XLA Ops:
  239.4 62.4 %copy-start.8 = (f32[11,512]{1,0:T(8,128)S(1)}, f32[11,512]{1,0:T(8,128)}, u32[]{:S(2)}) copy-start(f32[11,512]{1,0:T(8,128)} %param.15) | copy-start | bytes 67588
  239.4 63.0 %copy-start.9 = (f32[11,512]{1,0:T(8,128)S(1)}, f32[11,512]{1,0:T(8,128)}, u32[]{:S(2)}) copy-start(f32[11,512]{1,0:T(8,128)} %param.16) | copy-start | bytes 67588
  475.6 76.7 %copy-start = (f32[1024,512]{1,0:T(8,128)S(1)}, f32[1024,512]{1,0:T(8,128)}, u32[]{:S(2)}) copy-start(f32[1024,512]{1,0:T(8,128)} %get-tuple-element.52.refs_2_.refs_21_) | copy-start | bytes 6291460
  552.3 2.3 copy-start.3
  554.7 2.3 copy-start.1
  557.0 2.3 copy-start.2
  559.4 1.6 copy-start.6
  559.4 2.5 copy-start.5
  561.0 1.7 copy-start.4
  561.0 2.6 copy-start.7
  561.0 3.2 copy-start.11
  561.0 3.8 copy-start.10

commit v3 on v2

--- a/solution.py
+++ b/solution.py
@@ -1488,6 +1488,11 @@
         for _ in range(count):
             next(self.steps, None)
 
+    def ready(self):
+        for done in self.steps:
+            if done:
+                return
+
     def finish(self):
         for _ in self.steps:
             pass
@@ -1564,11 +1569,22 @@
                     remote(piece, self.part(block, half), send.at[0], recv.at[half], self.at_column(col)).wait_recv()
 
 
-def gather_pieces(group, piece, dest, own, zsend, msend, ssend, recv, srecv):
+def gate(only, q, seat, core, do):
+    if only is None:
+        do()
+    else:
+        pl.when(only(q, seat, core))(do)
+
+
+def gather_pieces(group, piece, dest, own, zsend, msend, ssend, recv, srecv, only=None):
     g = group.g
     seats, phases = g.seats, g.phases
     local = pltpu.make_async_copy(piece, dest.at[group.rows(g.c, g.seat, g.core)], own.at[0])
-    local.start()
+
+    def gated(e, seat, do):
+        gate(only, g.column(e), seat, g.core, do)
+
+    gated(0, g.seat, local.start)
 
     def slot(e, seat):
         return dest.at[group.rows(g.column(e), seat, g.core)]
@@ -1595,10 +1611,13 @@
             along(seat, -1, src, start)
 
     def handle(e, seat):
-        remote(piece, slot(e, seat), ssend.at[0, 0], recv.at[e, seat], g.sibling()).wait_recv()
-        if e == 0:
-            line(seat, slot(0, seat), True)
-        forward(e, seat, slot(e, seat), True)
+        def do():
+            remote(piece, slot(e, seat), ssend.at[0, 0], recv.at[e, seat], g.sibling()).wait_recv()
+            if e == 0:
+                line(seat, slot(0, seat), True)
+            forward(e, seat, slot(e, seat), True)
+
+        gated(e, seat, do)
 
     early = sorted((e for e in range(1, 2**phases) if lowest_bit(e) > 0), key=lambda e: -lowest_bit(e))
     late = [e for e in range(1, 2**phases) if lowest_bit(e) == 0]
@@ -1612,8 +1631,11 @@
                 for e in todo:
                     handle(e, seat)
 
-    line(g.seat, piece, True)
-    forward(0, g.seat, piece, True)
+    def first():
+        line(g.seat, piece, True)
+        forward(0, g.seat, piece, True)
+
+    gated(0, g.seat, first)
     yield
     for e in early:
         handle(e, g.seat)
@@ -1628,16 +1650,29 @@
         both_sides(d, late)
         yield
 
+    def siblings(seat, _):
+        for e in range(2**phases):
+            q = g.column(e, g.other_flips)
+            cp = remote(piece, dest.at[group.rows(q, seat, 1 - g.core)], ssend.at[0, 0], srecv.at[e, seat],
+                        g.sibling())
+            gate(only, q, seat, 1 - g.core, cp.wait_recv)
+        return 0
+
+    lax.fori_loop(0, seats, siblings, 0)
+    gated(0, g.seat, local.wait)
+    yield True
+
     def drain(seat, _):
+        def sent(e):
+            forward(e, seat, slot(e, seat), False)
+            if e == 0:
+                line(seat, slot(0, seat), False)
+
         for e in range(2**phases):
-            remote(piece, dest.at[group.rows(g.column(e, g.other_flips), seat, 1 - g.core)], ssend.at[0, 0],
-                   srecv.at[e, seat], g.sibling()).wait_recv()
-            forward(e, seat, slot(e, seat), False)
-        line(seat, slot(0, seat), False)
+            gated(e, seat, functools.partial(sent, e))
         return 0
 
     lax.fori_loop(0, seats, drain, 0)
-    local.wait()
 
 
 def gather_pieces_scratch(columns, n):
@@ -1653,7 +1688,7 @@
     ]
 
 
-def reduce_pieces(group, src, piece, sib, got, box, gsend, grecv, psend, precv, usend, urecv):
+def reduce_pieces(group, src, piece, sib, got, box, gsend, grecv, psend, precv, usend, urecv, only=None):
     g = group.g
     seats, phases = g.seats, g.phases
     slots = 2**phases
@@ -1685,22 +1720,32 @@
             total = total + got[k, e >> (k + 1), seat].astype(F32)
         return total
 
+    def gated(e, seat, do):
+        gate(only, g.column(e), seat, g.core, do)
+
+    def gated_sibling(e, seat, do):
+        gate(only, g.column(e, g.other_flips), seat, 1 - g.core, do)
+
     for e in order:
         for seat in turns:
-            sibling_copy(e, seat).start()
+            gated_sibling(e, seat, sibling_copy(e, seat).start)
     yield
+
+    def pass_on(e, k, seat):
+        sibling_copy(e, seat).wait_recv()
+        for q in range(k):
+            phase_copy(q, e | (1 << q), seat).wait_recv()
+        src[mine(e, seat), :] = local(e, seat, k).astype(B16)
+        phase_copy(k, e, seat).start()
+
     for e in order:
         if e == 0:
             break
-        k = lowest_bit(e)
         for seat in turns:
-            sibling_copy(e, seat).wait_recv()
-            for q in range(k):
-                phase_copy(q, e | (1 << q), seat).wait_recv()
-            src[mine(e, seat), :] = local(e, seat, k).astype(B16)
-            phase_copy(k, e, seat).start()
+            gated(e, seat, functools.partial(pass_on, e, lowest_bit(e), seat))
             yield
-    for seat in turns:
+
+    def own_column(seat):
         sibling_copy(0, seat).wait_recv()
         for q in range(phases):
             phase_copy(q, 1 << q, seat).wait_recv()
@@ -1710,27 +1755,35 @@
             src[mine(0, seat), :] = local(0, seat, phases).astype(B16)
             line_copy(seat).start()
 
+    for seat in turns:
+        gated(0, seat, functools.partial(own_column, seat))
         yield
-    total = local(0, g.seat, phases)
-    for seat in turns:
-        @pl.when(seat != g.seat)
-        def _():
-            line_arrival(seat).wait_recv()
-
-        total = total + jnp.where(seat == g.seat, 0.0, box[seat].astype(F32))
-    piece[...] = total.astype(B16)
-    yield
+
+    def last():
+        total = local(0, g.seat, phases)
+        for seat in turns:
+            @pl.when(seat != g.seat)
+            def _():
+                line_arrival(seat).wait_recv()
+
+            total = total + jnp.where(seat == g.seat, 0.0, box[seat].astype(F32))
+        piece[...] = total.astype(B16)
+
+    gated(0, g.seat, last)
+    yield True
 
     def drain(seat, _):
-        for e in range(slots):
-            sibling_copy(e, seat).wait_send()
+        def sent(e):
             if e > 0:
                 phase_copy(lowest_bit(e), e, seat).wait_send()
-
-        @pl.when(seat != g.seat)
-        def _():
-            line_copy(seat).wait_send()
-
+            else:
+                @pl.when(seat != g.seat)
+                def _():
+                    line_copy(seat).wait_send()
+
+        for e in range(slots):
+            gated_sibling(e, seat, sibling_copy(e, seat).wait_send)
+            gated(e, seat, functools.partial(sent, e))
         return 0
 
     lax.fori_loop(0, seats, drain, 0)
@@ -1793,30 +1846,54 @@
     pl.semaphore_wait(barrier, grid.n - 1 + grid.columns - 1)
 
 
+def across(top, low):
+    def taps(dr):
+        if dr == 0:
+            return [(0, 2 * C, top, 9 * C), (2 * C, 3 * C, low, 0)]
+        return [(0, 3 * C, low, 3 * C * dr - 2 * C)]
+
+    return taps
+
+
 def first_kernel(columns, n, dims, R):
     g = Grid(columns, n)
     half = R.block.shape[0] // 2
     groups = [Group(g, i, half) for i in range(2)]
     R.low[...] = R.block[...].astype(B16)
+    count = R.vectors.shape[0]
+    R.vec[...] = jnp.zeros(R.vec.shape, F32)
+    R.vec[0:count, :] = R.vectors[...].astype(B16).astype(F32)
+    canvases, rows, width = dims
+    turned = jnp.transpose(R.ids_lane[...])
+    for v in range(canvases):
+        R.ids_px[v] = jnp.broadcast_to(turned[:, v : v + 1], (rows * width, LANES)).reshape(rows, width, LANES)
     greet_all(g)
     for i, group in enumerate(groups):
         group.to_pieces(R.low, R.pieces.at[i], R.tsend.at[i], R.trecv.at[i], True)
-    weights = [R.w_top, R.w_low]
     engines = [
-        Engine(gather_pieces(group, R.pieces.at[i], weights[i], *(R.gather0 if i == 0 else R.gather1)))
-        for i, group in enumerate(groups)
+        Engine(gather_pieces(groups[0], R.pieces.at[0], R.w_top, *R.gather0)),
+        Engine(gather_pieces(groups[1], R.pieces.at[1], R.w_low, *R.gather1)),
     ]
+    each = rows * width // UNIT
+    for v in range(canvases):
+        cell_ids = R.ids_px[v].reshape(each, UNIT, LANES)[:, 0, :] + float(CROPS * v)
+        lane = lax.broadcasted_iota(jnp.int32, (each, LANES), 1).astype(F32)
+        R.hot[v * each : (v + 1) * each, :] = (cell_ids == lane).astype(F32)
+    stats = canvases * CROPS
+    R.spread[...] = R.hot[:, :stats].astype(B16)
+    R.pick[...] = jnp.transpose(R.hot[...])[:stats, :].astype(B16)
     turn = [0]
-    mine = g.h // (n // 2)
-    cot_copy = remote(R.cot.at[1 - mine], R.far_cot, R.csem.at[0], R.csem.at[1],
-                      {"canvas": g.c, "height": lax.rem(g.h + n // 2, n)})
+    lag = 2 * g.seats - 3
 
     def pump():
         if turn[0] == 0:
             groups[0].piece_arrived(R.low, R.pieces.at[0], R.tsend.at[0], R.trecv.at[0])
-        engines[0].pump()
-        if turn[0] == g.seats:
-            cot_copy.start()
+        if turn[0] < 2 * g.seats + 1:
+            engines[0].pump()
+        if turn[0] == lag:
+            groups[1].piece_arrived(R.low, R.pieces.at[1], R.tsend.at[1], R.trecv.at[1])
+        if turn[0] >= lag:
+            engines[1].pump()
         turn[0] += 1
 
     layout_body(n, dims, R.x, R.pick, R.spread, R.ids_px, R.ids_lane, R.ids_all, R.mean1, R.inv1, R.div, R.cnt,
@@ -1828,14 +1905,15 @@
     conv.activate(R.x, R.mean1, R.inv1, vec[0:1, :], vec[1:2, :], R.s1, 0, pump)
     out_s1 = pltpu.make_async_copy(R.s1, R.s1_out, R.osem.at[0])
     out_s1.start()
-    while turn[0] <= g.seats:
+    while turn[0] < 2 * g.seats + 1:
         pump()
-    engines[0].finish()
+    engines[0].ready()
     out_top = pltpu.make_async_copy(R.w_top, R.top, R.osem.at[1])
     out_top.start()
-    groups[1].piece_arrived(R.low, R.pieces.at[1], R.tsend.at[1], R.trecv.at[1])
     pump_low = engines[1].pump
-    pump_low()
+    if turn[0] <= lag:
+        groups[1].piece_arrived(R.low, R.pieces.at[1], R.tsend.at[1], R.trecv.at[1])
+        pump_low()
 
     def emit_first(at, total):
         R.y1[at, :] = total + vec[2:3, :]
@@ -1847,30 +1925,27 @@
     conv.activate(R.y1, R.mean2, R.inv2, vec[3:4, :], vec[4:5, :], R.s2, 1, pump_low)
     out_s2 = pltpu.make_async_copy(R.s2, R.s2_out, R.osem.at[3])
     out_s2.start()
-    engines[1].finish()
+    engines[1].ready()
     out_low = pltpu.make_async_copy(R.w_low, R.bottom, R.osem.at[4])
     out_low.start()
 
     def emit_second(at, total):
         R.hid[at, :] = total + vec[5:6, :] + R.x[at, :].astype(F32)
 
-    def second(dr):
-        if dr == 0:
-            return [(0, 2 * C, R.w_top, 9 * C), (2 * C, 3 * C, R.w_low, 0)]
-        return [(0, 3 * C, R.w_low, 3 * C * dr - 2 * C)]
-
-    conv.convolve(R.s2, second, emit_second)
+    conv.convolve(R.s2, across(R.w_top, R.w_low), emit_second)
     conv.statistics(R.hid, R.mean3, R.inv3, 1)
     conv.normalise(R.hid, R.mean3, R.inv3, vec[6:7, :], vec[7:8, :], R.u)
     for cp in conv.sent:
         cp.wait_send()
     for i, group in enumerate(groups):
         group.to_pieces(R.low, R.pieces.at[i], R.tsend.at[i], R.trecv.at[i], False)
-    for cp in (out_s1, out_top, out_y1, out_s2, out_low, cot_copy):
+    for cp in (out_s1, out_top, out_y1, out_s2, out_low):
         cp.wait()
-
-
-def first_call(columns, n, dims, x, pick, spread, ids_px, ids_lane, vec, block, cot):
+    for engine in engines:
+        engine.finish()
+
+
+def first_call(columns, n, dims, x, ids_lane, vectors, block):
     canvases, rows, width = dims
     px = canvases * rows * width
     cells = px // UNIT
@@ -1878,19 +1953,19 @@
     tall = (canvases, rows + 2, width)
     half = block.shape[0] // 2
     dma = pltpu.SemaphoreType.DMA
-    inputs = dict(x=(x, vmem), pick=(pick, vmem), spread=(spread, vmem), ids_px=(ids_px, vmem),
-                  ids_lane=(ids_lane, vmem), vec=(vec, vmem), block=(block, vmem),
-                  cot=(cot, anyw))
+    inputs = dict(x=(x, vmem), ids_lane=(ids_lane, vmem), vectors=(vectors, vmem), block=(block, vmem))
     cell = ((cells, C), F32, vmem)
     outputs = dict(
+        vec=((16, C), F32, vmem), pick=((stats, cells), B16, vmem), spread=((cells, stats), B16, vmem),
         ids_all=((n,) + ids_lane.shape, F32, vmem), mean1=cell, inv1=cell, div=((stats, LANES), F32, vmem),
         cnt=((stats, LANES), F32, vmem), col_l=(tall + (LANES,), F32, vmem), col_r=(tall + (LANES,), F32, vmem),
         row_u=((px, LANES), F32, vmem), row_d=((px, LANES), F32, vmem), hid=((px, C), F32, vmem),
         u=((px, C), B16, vmem), mean2=cell, inv2=cell, mean3=cell, inv3=cell, y1_out=((px, C), F32, anyw),
         s1_out=(tall + (3 * C,), B16, anyw), s2_out=(tall + (3 * C,), B16, anyw),
-        top=((11 * C, C), B16, anyw), bottom=((11 * C, C), B16, anyw), far_cot=(cot.shape[1:], B16, anyw))
+        top=((11 * C, C), B16, anyw), bottom=((11 * C, C), B16, anyw))
     scratch = dict(
-        csem=dma((2,)), y1=pltpu.VMEM((px, C), F32), s1=pltpu.VMEM(tall + (3 * C,), B16), s2=pltpu.VMEM(tall + (3 * C,), B16),
+        ids_px=pltpu.VMEM(dims + (LANES,), F32), hot=pltpu.VMEM((cells, LANES), F32),
+        y1=pltpu.VMEM((px, C), F32), s1=pltpu.VMEM(tall + (3 * C,), B16), s2=pltpu.VMEM(tall + (3 * C,), B16),
         w_top=pltpu.VMEM((11 * C, C), B16), w_low=pltpu.VMEM((11 * C, C), B16), low=pltpu.VMEM(block.shape, B16),
         pieces=pltpu.VMEM((2, half, C), B16), tsend=dma((2, 2)), trecv=dma((2, 1)),
         gather0=gather_pieces_scratch(columns, n), gather1=gather_pieces_scratch(columns, n),
@@ -2065,6 +2140,10 @@
 
     back.norm_finish(copies, 0, R.inv3, emit_hidden)
     up, down = back.send_rows(R.grad, 0)
+    plane = dims[1] * dims[2]
+    o_back = remote(R.o.at[pl.ds(plane, plane)], R.o_back, R.lsem.at[2], R.lsem.at[3],
+                    {"canvas": g.c, "height": lax.rem(g.h + n // 2, n)})
+    o_back.start()
     back.mask_rows(R.grad)
     load_s.wait()
 
@@ -2072,9 +2151,9 @@
         return (R.g_top, (9 + tap) * C) if tap < 2 else (R.g_low, (tap - 2) * C)
 
     back.weight_grad(R.s, R.grad, dest_two)
+    load_att.wait()
     load_s = pltpu.make_async_copy(R.s1, R.s, R.lsem.at[0])
     load_s.start()
-    load_att.wait()
     engine = Engine(reduce_pieces(group, R.g_low, R.sum_low, *R.reduce))
     engine.pump()
     dc2 = jnp.sum(R.grad[...].astype(F32), axis=0, keepdims=True)
@@ -2100,12 +2179,14 @@
     load_s.wait()
     back.weight_grad(R.s, R.grad, lambda tap: (R.g_top, tap * C), engine.pump)
     R.dvec[...] = jnp.concatenate([dc1, dg2, db2, dc2, dg3, db3, jnp.zeros((2, C), F32)], axis=0)
+    engine.ready()
     engine.finish()
     for cp in back.sent:
         cp.wait_send()
-
-
-def back_call(columns, n, dims, cot, du, hid, y1, norms, s1, s2, pick, spread, div, masks, vec, top, bottom, datt,
+    o_back.wait()
+
+
+def back_call(columns, n, dims, cot, du, hid, y1, norms, s1, s2, pick, spread, div, masks, vec, top, bottom, datt, o,
               block_rows):
     canvases, rows, width = dims
     px = canvases * rows * width
@@ -2115,32 +2196,45 @@
     names = ("mean2", "inv2", "mean3", "inv3")
     inputs = dict(cot=(cot, vmem), du=(du, vmem), hid=(hid, vmem), y1=(y1, vmem), s1=(s1, anyw), s2=(s2, anyw),
                   pick=(pick, vmem), spread=(spread, vmem), div=(div, vmem), vec=(vec, vmem), top=(top, anyw),
-                  bottom=(bottom, anyw), datt=(datt, anyw),
+                  bottom=(bottom, anyw), datt=(datt, anyw), o=(o, anyw),
                   **{k: (v, vmem) for k, v in zip(names, norms)},
                   **{k: (v, vmem) for k, v in zip(("col_l", "col_r", "row_u", "row_d"), masks)})
     outputs = dict(dh=((px, C), F32, vmem), grad=((px, C), B16, vmem), g_top=((11 * C, C), B16, vmem),
-                   dvec=((8, C), F32, vmem), sum_low=((block_rows // 2, C), B16, vmem))
+                   dvec=((8, C), F32, vmem), sum_low=((block_rows // 2, C), B16, vmem),
+                   o_back=((px // canvases, C), B16, anyw))
     scratch = dict(
         g_low=pltpu.VMEM((11 * C, C), B16), s=pltpu.VMEM(s1.shape, B16), k=pltpu.VMEM((9 * C, C), B16),
         d3=pltpu.VMEM(s1.shape, B16), low_u=pltpu.VMEM((px, C), B16), low_d=pltpu.VMEM((px, C), B16),
         part=pltpu.VMEM((px, C), F32), norm=pltpu.VMEM((px, C), F32),
         halo=pltpu.VMEM((1, 2, canvases, width, C), B16), buf=pltpu.VMEM((2, n, stats, LANES), F32),
         tmp_a=pltpu.VMEM((cells, C), F32), tmp_b=pltpu.VMEM((cells, C), F32),
-        reduce=reduce_pieces_scratch(columns, n, block_rows // 2), lsem=dma((5,)), ksem=dma((3,)),
+        reduce=reduce_pieces_scratch(columns, n, block_rows // 2),
+        lsem=dma((5,)), ksem=dma((3,)),
         send=dma((2, n)), recv=dma((2, n)), hsend=dma((1, 2)), hrecv=dma((1, 2)))
     return named_call(functools.partial(back_kernel, columns, n, dims), "back", 7, inputs, outputs, scratch)
 
 
-def update_kernel(columns, n, dims, R):
+def renew_kernel(columns, n, dims, R):
     g = Grid(columns, n)
-    half = R.w.shape[0] // 2
+    half = R.fresh.shape[0] // 2
     upper, lower = Group(g, 0, half), Group(g, 1, half)
+    load_g = pltpu.make_async_copy(R.g_in, R.g_top, R.ksem.at[1])
+    load_g.start()
     load_k = pltpu.make_async_copy(R.top.at[pl.ds(0, 9 * C)], R.k, R.ksem.at[0])
     load_k.start()
-    load_g = pltpu.make_async_copy(R.g_in, R.g_top, R.ksem.at[1])
-    load_g.start()
-    load_p = pltpu.make_async_copy(R.bottom.at[pl.ds(10 * C, C)], R.wp, R.ksem.at[2])
-    load_p.start()
+    loads = [
+        pltpu.make_async_copy(src, dst, R.ksem.at[2 + i])
+        for i, (src, dst) in enumerate(((R.w, R.new_w), (R.m, R.new_m), (R.v, R.new_s), (R.dh, R.igrad)))
+    ]
+    for cp in loads:
+        cp.start()
+    piece_loads = []
+    for i, src in enumerate((R.w, R.m, R.v)):
+        here = pltpu.make_async_copy(src.at[pl.ds(0, half)], R.piece_in.at[i], R.psem.at[i])
+        there = pltpu.make_async_copy(R.shares.at[i], R.piece_in.at[i], R.psem.at[i])
+        pl.when(g.c == 0)(here.start)
+        pl.when(g.c != 0)(there.start)
+        piece_loads.append(there)
     greet_all(g)
     vec = R.vec
     lower.to_owner(R.sum_low, R.totals.at[1], R.asend.at[1], R.arecv.at[1], True)
@@ -2150,20 +2244,18 @@
     back = Backer(n, dims, R)
     up, down = back.send_rows(R.grad, 0)
     reducer.pump(2)
+    for cp in loads:
+        cp.wait()
 
     def adam(group, totals):
         @pl.when(group.is_owner)
         def _():
             total = totals[...].astype(F32)
-            next_w, R.new_m[...], R.new_s[...] = adam_update(R.w[...], total, R.m[...], R.v[...], matrix_rate)
+            next_w, R.new_m[...], R.new_s[...] = adam_update(
+                R.new_w[...], total, R.new_m[...], R.new_s[...], matrix_rate)
             R.new_w[...] = next_w
             R.fresh[...] = next_w.astype(B16)
 
-    load_p.wait()
-    for v in range(dims[0]):
-        at = pl.ds(v * dims[1] * dims[2], dims[1] * dims[2])
-        R.output[at, :] = (
-            R.hid[at, :] + jnp.dot(R.o[at, :], R.wp[...], preferred_element_type=F32) + vec[10:11, :])
     lower.block_arrived(R.sum_low, R.totals.at[1], R.asend.at[1], R.arecv.at[1])
     adam(lower, R.totals.at[1])
     lower.to_pieces(R.fresh, R.pieces.at[1], R.tsend.at[1], R.trecv.at[1], True)
@@ -2171,8 +2263,6 @@
     back.finish_rows(up, down, 0)
     load_k.wait()
     back.convolve_back(lambda tap: (R.k, tap * C), reducer.pump)
-    lower.piece_arrived(R.fresh, R.pieces.at[1], R.tsend.at[1], R.trecv.at[1])
-    gather_low = Engine(gather_pieces(lower, R.pieces.at[1], R.new_low, *R.gather1))
     gain1, bias1 = vec[0:1, :], vec[1:2, :]
 
     def grad_one(i, unit):
@@ -2188,13 +2278,25 @@
     ]
     for cp in vector_sends:
         cp.start()
+    lower.piece_arrived(R.fresh, R.pieces.at[1], R.tsend.at[1], R.trecv.at[1])
+    gather_low = Engine(gather_pieces(lower, R.pieces.at[1], R.new_low, *R.gather1))
+    gather_low.pump()
+    reducer.ready()
+    for cp in piece_loads:
+        cp.wait()
+    next_piece, _, _ = adam_update(
+        R.piece_in[0], R.sum_top[...].astype(F32), R.piece_in[1], R.piece_in[2], matrix_rate)
+    R.pieces[0] = next_piece.astype(B16)
+    gather_top = Engine(gather_pieces(upper, R.pieces.at[0], R.new_top, *R.gather0))
+    gather_top.pump()
+    upper.to_owner(R.sum_top, R.totals.at[0], R.asend.at[0], R.arecv.at[0], True)
 
     def emit_input(i, value):
         at = back.pixels(i)
-        R.igrad[at, :] = R.dh[at, :] + value
+        R.igrad[at, :] = R.igrad[at, :] + value
 
     back.norm_finish(copies, 0, R.inv1, emit_input)
-    reducer.pump(2)
+    gather_top.pump()
     for d in range(1, n):
         src = lax.rem(g.h + d, n)
         remote(R.vbuf.at[src], R.vbuf.at[src], R.vsend.at[d], R.vrecv.at[src],
@@ -2205,39 +2307,58 @@
         return remote(R.vtrade.at[k, 0], R.vtrade.at[k, 1], R.qsend.at[k], R.qrecv.at[k], g.mate(k))
 
     trade(0).start()
-    reducer.finish()
-    upper.to_owner(R.sum_top, R.totals.at[0], R.asend.at[0], R.arecv.at[0], True)
-    gather_low.pump()
+    gather_top.pump()
     for k in range(g.phases):
         trade(k).wait_recv()
         R.vtrade[k + 1, 0] = R.vtrade[k, 0] + R.vtrade[k, 1]
         if k + 1 < g.phases:
             trade(k + 1).start()
+        gather_top.pump()
+    count = R.vw.shape[0]
     R.new_vw[...], R.new_vm[...], R.new_vs[...] = adam_update(
-        R.vw[...], R.vtrade[g.phases, 0], R.vm[...], R.vs[...], vector_rate)
+        R.vw[...], R.vtrade[g.phases, 0][0:count, :], R.vm[...], R.vs[...], vector_rate)
+    R.new_vec[...] = jnp.zeros(R.new_vec.shape, F32)
+    R.new_vec[0:count, :] = R.new_vw[...].astype(B16).astype(F32)
+    new_vec, s1, y1 = R.new_vec, R.d3, R.part
+    conv = Convolver(n, dims, R.x, R.pick, R.spread, R.cnt, R.col_l, R.col_r, R.row_u, R.row_d, R.chalo, R.cbuf,
+                     R.tmp_a, R.tmp_b, R.csend, R.crecv, R.chsend, R.chrecv)
+    conv.activate(R.x, R.mean1, R.inv1, new_vec[0:1, :], new_vec[1:2, :], s1, 0, gather_top.pump)
+    gather_top.ready()
+    pump = gather_low.pump
+    pump()
+
+    def emit_first(at, total):
+        y1[at, :] = total + new_vec[2:3, :]
+
+    conv.convolve(s1, lambda dr: [(0, 3 * C, R.new_top, 3 * C * dr)], emit_first, pump)
+    conv.statistics(y1, R.mean2, R.inv2, 0, pump)
+    conv.activate(y1, R.mean2, R.inv2, new_vec[3:4, :], new_vec[4:5, :], R.s2, 1, pump)
+    gather_low.ready()
+    out_att = pltpu.make_async_copy(R.new_low.at[pl.ds(7 * C, 4 * C)], R.new_att, R.ksem.at[0])
+    out_att.start()
+
+    def emit_second(at, total):
+        R.hid[at, :] = total + new_vec[5:6, :] + R.x[at, :].astype(F32)
+
+    conv.convolve(R.s2, across(R.new_top, R.new_low), emit_second)
+    conv.statistics(R.hid, R.mean2, R.inv2, 1)
     upper.block_arrived(R.sum_top, R.totals.at[0], R.asend.at[0], R.arecv.at[0])
     adam(upper, R.totals.at[0])
-    upper.to_pieces(R.fresh, R.pieces.at[0], R.tsend.at[0], R.trecv.at[0], True)
-    gather_low.pump()
-    upper.piece_arrived(R.fresh, R.pieces.at[0], R.tsend.at[0], R.trecv.at[0])
-    gather_top = Engine(gather_pieces(upper, R.pieces.at[0], R.new_top, *R.gather0))
-    gather_top.pump()
-    for _ in range(2 * g.seats + 2):
-        gather_low.pump()
-        gather_top.pump()
-    gather_low.finish()
-    gather_top.finish()
-    for cp in back.sent + vector_sends:
+    conv.normalise(R.hid, R.mean2, R.inv2, new_vec[6:7, :], new_vec[7:8, :], R.u)
+    for engine in (gather_low, gather_top, reducer):
+        engine.finish()
+    for cp in back.sent + conv.sent + vector_sends:
         cp.wait_send()
     for k in range(g.phases):
         trade(k).wait_send()
     for i, group in enumerate((upper, lower)):
         group.to_owner((R.sum_top, R.sum_low)[i], R.totals.at[i], R.asend.at[i], R.arecv.at[i], False)
-        group.to_pieces(R.fresh, R.pieces.at[i], R.tsend.at[i], R.trecv.at[i], False)
-
-
-def update_call(columns, n, dims, grad, dh, x, mean1, inv1, pick, spread, div, masks, vec, top, bottom, g_top, sum_low, dvec,
-                dvec_att, w, m, v, vw, vm, vs, hid, o):
+    lower.to_pieces(R.fresh, R.pieces.at[1], R.tsend.at[1], R.trecv.at[1], False)
+    out_att.wait()
+
+
+def renew_call(columns, n, dims, grad, dh, x, mean1, inv1, pick, spread, div, cnt, masks, vec, top, g_top, sum_low,
+               dvec, dvec_att, w, m, v, shares, vw, vm, vs):
     canvases, rows, width = dims
     px = canvases * rows * width
     cells = px // UNIT
@@ -2247,26 +2368,32 @@
     seats, phases = n // 2, columns.bit_length() - 1
     dma = pltpu.SemaphoreType.DMA
     tall = (canvases, rows + 2, width, 3 * C)
-    arrays = dict(grad=grad, dh=dh, x=x, mean1=mean1, inv1=inv1, pick=pick, spread=spread, div=div, vec=vec,
-                  g_in=g_top, sum_low=sum_low, dvec=dvec, dvec_att=dvec_att, w=w, m=m, v=v, vw=vw, vm=vm, vs=vs, hid=hid, o=o)
-    inputs = dict(top=(top, anyw), bottom=(bottom, anyw), **{k: (a, vmem) for k, a in arrays.items()},
+    arrays = dict(grad=grad, x=x, mean1=mean1, inv1=inv1, pick=pick, spread=spread, div=div, cnt=cnt, vec=vec,
+                  sum_low=sum_low, dvec=dvec, dvec_att=dvec_att, vw=vw, vm=vm, vs=vs)
+    inputs = dict(top=(top, anyw), g_in=(g_top, anyw), w=(w, anyw), m=(m, anyw), v=(v, anyw), shares=(shares, anyw), dh=(dh, anyw),
+                  **{k: (a, vmem) for k, a in arrays.items()},
                   **{k: (a, vmem) for k, a in zip(("col_l", "col_r", "row_u", "row_d"), masks)})
-    inputs["g_in"] = (g_top, anyw)
-    outputs = dict(igrad=((px, C), F32, vmem), output=((px, C), F32, vmem), new_w=(block, F32, vmem), new_m=(block, F32, vmem),
+    outputs = dict(igrad=((px, C), F32, vmem), new_w=(block, F32, vmem), new_m=(block, F32, vmem),
                    new_s=(block, F32, vmem), new_vw=(vw.shape, F32, vmem), new_vm=(vw.shape, F32, vmem),
-                   new_vs=(vw.shape, F32, vmem), new_top=((11 * C, C), B16, anyw), new_low=((11 * C, C), B16, anyw))
+                   new_vs=(vw.shape, F32, vmem), new_vec=((16, C), F32, vmem), hid=((px, C), F32, vmem),
+                   u=((px, C), B16, vmem), new_att=((4 * C, C), B16, anyw))
     scratch = dict(
         g_top=pltpu.VMEM((11 * C, C), B16), sum_top=pltpu.VMEM((half, C), B16), totals=pltpu.VMEM((2,) + block, B16),
+        new_top=pltpu.VMEM((11 * C, C), B16), new_low=pltpu.VMEM((11 * C, C), B16),
         fresh=pltpu.VMEM(block, B16), pieces=pltpu.VMEM((2, half, C), B16), k=pltpu.VMEM((9 * C, C), B16),
-        d3=pltpu.VMEM(tall, B16), part=pltpu.VMEM((px, C), F32), norm=pltpu.VMEM((px, C), F32),
-        halo=pltpu.VMEM((1, 2, canvases, width, C), B16), buf=pltpu.VMEM((1, n, stats, LANES), F32),
+        d3=pltpu.VMEM(tall, B16), s2=pltpu.VMEM(tall, B16), part=pltpu.VMEM((px, C), F32),
+        norm=pltpu.VMEM((px, C), F32), mean2=pltpu.VMEM((cells, C), F32), inv2=pltpu.VMEM((cells, C), F32),
+        halo=pltpu.VMEM((1, 2, canvases, width, C), B16), chalo=pltpu.VMEM((2, 2, canvases, width, C), B16),
+        buf=pltpu.VMEM((1, n, stats, LANES), F32), cbuf=pltpu.VMEM((2, n, stats, LANES), F32),
         tmp_a=pltpu.VMEM((cells, C), F32), tmp_b=pltpu.VMEM((cells, C), F32),
-        vbuf=pltpu.VMEM((n,) + vw.shape, F32), vtrade=pltpu.VMEM((phases + 1, 2) + vw.shape, F32),
+        vbuf=pltpu.VMEM((n, 16, C), F32), vtrade=pltpu.VMEM((phases + 1, 2, 16, C), F32),
         reduce=reduce_pieces_scratch(columns, n, half), gather0=gather_pieces_scratch(columns, n),
-        gather1=gather_pieces_scratch(columns, n), wp=pltpu.VMEM((C, C), B16), ksem=dma((3,)), asend=dma((2, 1)), arecv=dma((2, 2)),
+        gather1=gather_pieces_scratch(columns, n),
+        piece_in=pltpu.VMEM((3, half, C), F32), psem=dma((3,)), ksem=dma((6,)), asend=dma((2, 1)), arecv=dma((2, 2)),
         tsend=dma((2, 2)), trecv=dma((2, 1)), vsend=dma((n,)), vrecv=dma((n,)), qsend=dma((phases,)),
-        qrecv=dma((phases,)), send=dma((1, n)), recv=dma((1, n)), hsend=dma((1, 2)), hrecv=dma((1, 2)))
-    return named_call(functools.partial(update_kernel, columns, n, dims), "update", 9, inputs, outputs, scratch)
+        qrecv=dma((phases,)), send=dma((1, n)), recv=dma((1, n)), hsend=dma((1, 2)), hrecv=dma((1, 2)),
+        csend=dma((2, n)), crecv=dma((2, n)), chsend=dma((2, 2)), chrecv=dma((2, 2)))
+    return named_call(functools.partial(renew_kernel, columns, n, dims), "renew", 9, inputs, outputs, scratch)
 
 
 def attend_kernel(n, keep, R):
@@ -2295,22 +2422,38 @@
     def to(h):
         return {"canvas": lax.axis_index("canvas"), "height": h}
 
-    loads = [pltpu.make_async_copy(R.low.at[pl.ds(7 * C, 4 * C)], R.w, R.lsem.at[0])]
+    loads = [pltpu.make_async_copy(R.low.at[pl.ds(R.low.shape[0] - 4 * C, 4 * C)], R.w, R.lsem.at[0])]
     if keep:
-        loads += [
-            pltpu.make_async_copy(R.far_cot, R.dz.at[pl.ds(0, seg)], R.lsem.at[1]),
-            pltpu.make_async_copy(R.cot.at[mine], R.dz.at[pl.ds(seg, seg)], R.lsem.at[2]),
-        ]
+        loads.append(pltpu.make_async_copy(R.cot.at[mine], R.dz.at[pl.ds(0, seg)], R.lsem.at[1]))
     for cp in loads:
         cp.start()
     own = pltpu.make_async_copy(R.u_in.at[mine], R.u.at[me], R.lsem.at[3])
     own.start()
     barrier = pltpu.get_barrier_semaphore()
-    peers = [partner, sibling] + [mate(j) for j in range(1, mates)]
+    peers = [to(p) for p in [partner, sibling] + [mate(j) for j in range(1, mates)]]
+    column = lax.axis_index("canvas")
+    if keep:
+        peers += [{"canvas": lax.rem(column + d, 4), "height": me} for d in range(1, 4)]
     for p in peers:
-        pl.semaphore_signal(barrier, inc=1, device_id=to(p), device_id_type=MESH)
+        pl.semaphore_signal(barrier, inc=1, device_id=p, device_id_type=MESH)
     pl.semaphore_wait(barrier, len(peers))
     started = []
+
+    def share(from_column, half_number, to_column, begin):
+        rows = R.shares.shape[1]
+        for i, src in enumerate((R.params, R.first, R.second)):
+            cp = remote(src.at[pl.ds(half_number * rows, rows)], R.shares.at[i], R.wsend.at[half_number, i],
+                        R.wrecv.at[i], {"canvas": to_column, "height": me})
+            if begin:
+                pl.when(column == from_column)(cp.start)
+            else:
+                pl.when(column == from_column)(cp.wait_send)
+                pl.when(column == to_column)(cp.wait_recv)
+
+    moves = ((0, 1, 1), (1, 0, 2), (1, 1, 3))
+    if keep:
+        for move in moves:
+            share(*move, True)
 
     def push(src, slot, dest):
         cp = remote(src, R.u.at[slot], R.gsend.at[len(started)], R.grecv.at[slot], to(dest))
@@ -2341,13 +2484,13 @@
     arrived(sibling)
     project(sibling)
     key_ids = jnp.concatenate([R.ids_all[b, pl.ds(mine, 1), :] for b in range(n)], axis=1)
-    for i, b in enumerate((partner, me)):
+    order = (me, partner) if keep else (partner, me)
+    first_far = 1 if keep else 0
+    far_rows, own_rows = pl.ds(first_far * seg, seg), pl.ds((1 - first_far) * seg, seg)
+    for i, b in enumerate(order):
         turned = jnp.transpose(R.ids_all[b])
         picked = jnp.where(mine == 0, turned[:, 0:1], turned[:, 1:2])
         R.qid[i * seg : (i + 1) * seg, :] = jnp.broadcast_to(picked, (seg, LANES))
-    if keep:
-        R.dout[...] = lax.dot_general(
-            R.dz[...], R.w[3 * C : 4 * C, :], nt, preferred_element_type=F32).astype(B16)
     arrived(partner)
     for j in range(1, mates):
         push(R.u.at[partner], partner, mate(j))
@@ -2374,12 +2517,29 @@
 
     rows = R.rows
     per = seg // rows
+
+    def swap_cot(i):
+        here = pl.ds(pl.multiple_of(i * rows, rows), rows)
+        there = pl.ds(pl.multiple_of(seg + i * rows, rows), rows)
+        return remote(R.cot.at[1 - mine, here], R.dz.at[there], R.csend.at[i], R.crecv.at[i], to(partner))
+
+    if keep:
+        for i in range(per):
+            swap_cot(i).start()
     o_home = R.o_home
-    far_out = remote(R.out.at[pl.ds(0, seg)], o_home.at[mine], R.osem.at[0], R.osem.at[1], to(partner))
+
+    def far_out(i):
+        here = pl.ds(pl.multiple_of(i * rows, rows), rows)
+        return remote(R.out.at[here], o_home.at[mine, here], R.osend.at[i], R.orecv.at[i], to(partner))
 
     def attend(i, _):
         at = pl.ds(pl.multiple_of(i * rows, rows), rows)
-        b = jnp.where(i < per, partner, me)
+        b = jnp.where(i < per, order[0], order[1])
+        if keep:
+            @pl.when(i >= per)
+            def _():
+                swap_cot(i - per).wait_recv()
+
         uq = R.u[b, pl.ds(pl.multiple_of(lax.rem(i, per) * rows, rows), rows), :]
         qb = (jnp.dot(uq, R.w[0:C, :], preferred_element_type=F32) + vec[8:9, :]).astype(B16)
         s = lax.dot_general(qb, R.k[...], nt, preferred_element_type=F32) * scale
@@ -2391,37 +2551,38 @@
         if keep:
             R.pbuf[at, :] = pb
             R.q[at, :] = qb
-            dp = lax.dot_general(R.dout[at, :], R.v[...], nt, preferred_element_type=F32)
+            dout = lax.dot_general(
+                R.dz[at, :], R.w[3 * C : 4 * C, :], nt, preferred_element_type=F32).astype(B16)
+            R.dout[at, :] = dout
+            dp = lax.dot_general(dout, R.v[...], nt, preferred_element_type=F32)
             delta = jnp.sum(p * dp, axis=1, keepdims=True)
             ds = (p * (dp - delta)).astype(B16)
             R.sbuf[at, :] = ds
             R.dq[at, :] = (jnp.dot(ds, R.k[...], preferred_element_type=F32) * scale).astype(B16)
 
-        @pl.when(i == per - 1)
-        def _():
-            far_out.start()
+        if not keep:
+            @pl.when(i < per)
+            def _():
+                far_out(i).start()
 
         return 0
 
     lax.fori_loop(0, 2 * per, attend, 0)
-    own_out = pltpu.make_async_copy(R.out.at[pl.ds(seg, seg)], o_home.at[mine], R.lsem.at[4])
-    own_out.start()
     if not keep:
+        own_out = pltpu.make_async_copy(R.out.at[own_rows], o_home.at[mine], R.lsem.at[2])
+        own_out.start()
         own_out.wait()
-        far_out.wait_recv()
-        bias = vec[10:11, :]
-        for v in range(2):
-            at = pl.ds(v * seg, seg)
-            R.final[at, :] = (
-                R.hid[at, :] + jnp.dot(o_home[v], R.w[3 * C : 4 * C, :], preferred_element_type=F32) + bias)
-        far_out.wait_send()
+        for i in range(per):
+            far_out(i).wait()
         for cp in started:
             cp.wait_send()
         return
+    all_out = pltpu.make_async_copy(R.out, o_home, R.lsem.at[2])
+    all_out.start()
     zero = jnp.zeros((C, C), F32)
     pairs = 2 * mates
 
-    def share(b, carry):
+    def du_of(b, carry):
         dwk, dwv, dbv = carry
         at = block(b)
         dk = (lax.dot_general(R.sbuf[:, at], R.q[...], tn, preferred_element_type=F32) * scale).astype(B16)
@@ -2435,54 +2596,69 @@
         return du, (dwk, dwv, dbv + jnp.sum(dvf, axis=0, keepdims=True))
 
     def place(t):
-        other = t < pairs - 2
-        return jnp.where(other, t // 2 + 1, 0), 1 - lax.rem(t, 2)
+        far = 1 - t // mates
+        return lax.rem(lax.rem(t, mates) + 1, mates), far
 
     def sib_copy(t):
         return remote(R.for_sib.at[t], R.from_sib.at[t], R.ssend.at[t], R.srecv.at[t], to(sibling))
 
-    def mate_copy(t):
+    def mate_copy(t, part):
         j, _ = place(t)
-        return remote(R.sums.at[t], R.from_mate.at[t], R.msend.at[t], R.mrecv.at[t], to(mate(j)))
+        here = pl.ds(part * (seg // 2), seg // 2)
+        return remote(R.sums.at[t, here], R.from_mate.at[t, here], R.msend.at[t, part], R.mrecv.at[t, part],
+                      to(mate(j)))
+
+    def home_copy(part):
+        here = pl.ds(part * (seg // 2), seg // 2)
+        return remote(R.for_home.at[here], R.from_partner.at[here], R.hsend.at[part], R.hrecv.at[part], to(partner))
+
+    def gathered(far, part):
+        count = seg // 2
+        at = pl.ds((first_far if far else 1 - first_far) * seg + part * count, count)
+        here = pl.ds(part * count, count)
+        value = lax.dot_general(R.dq[at, :], R.w[0:C, :], nt, preferred_element_type=F32)
+        first_t = 0 if far else mates
+        value = value + R.sums[first_t + mates - 1, here, :].astype(F32)
+        for t in range(first_t, first_t + mates - 1):
+            mate_copy(t, part).wait_recv()
+            value = value + R.from_mate[t, here, :].astype(F32)
+        return value
+
+    def send_home(part):
+        R.for_home[pl.ds(part * (seg // 2), seg // 2), :] = gathered(1, part).astype(B16)
+        home_copy(part).start()
 
     def back(t, carry):
         j, far = place(t)
         theirs, ours = mate(j, 1 - core), mate(j)
-        du, carry = share(lax.rem(theirs + far * half, n), carry)
+        du, carry = du_of(lax.rem(theirs + far * half, n), carry)
         R.for_sib[t] = du.astype(B16)
         sib_copy(t).start()
-        du, carry = share(lax.rem(ours + far * half, n), carry)
+        du, carry = du_of(lax.rem(ours + far * half, n), carry)
         sib_copy(t).wait_recv()
         R.sums[t] = (du + R.from_sib[t].astype(F32)).astype(B16)
 
-        @pl.when(t < pairs - 2)
+        @pl.when(j != 0)
         def _():
-            mate_copy(t).start()
+            for part in range(2):
+                mate_copy(t, part).start()
+
+        @pl.when(t == pairs - 2)
+        def _():
+            send_home(0)
 
         return carry
 
     dwk, dwv, dbv = lax.fori_loop(0, pairs, back, (zero, zero, jnp.zeros((1, C), F32)))
-
-    def gathered(far):
-        at = pl.ds(0, seg) if far else pl.ds(seg, seg)
-        value = lax.dot_general(R.dq[at, :], R.w[0:C, :], nt, preferred_element_type=F32)
-        value = value + R.sums[pairs - 1 - far].astype(F32)
-        for j in range(1, mates):
-            t = 2 * (j - 1) + 1 - far
-            mate_copy(t).wait_recv()
-            value = value + R.from_mate[t].astype(F32)
-        return value
-
-    R.for_home[...] = gathered(1).astype(B16)
-    home = remote(R.for_home, R.from_partner, R.hsem.at[0], R.hsem.at[1], to(partner))
-    home.start()
-    R.du[mine] = gathered(0)
+    send_home(1)
+    for part in range(2):
+        R.du[mine, pl.ds(part * (seg // 2), seg // 2), :] = gathered(0, part)
     R.dw[C : 2 * C, :] = dwk.astype(B16)
     R.dw[2 * C : 3 * C, :] = dwv.astype(B16)
     R.dw[3 * C : 4 * C, :] = lax.dot_general(
         R.out[...], R.dz[...], tn, preferred_element_type=F32).astype(B16)
-    dwq = lax.dot_general(R.u[partner], R.dq[0:seg, :], tn, preferred_element_type=F32)
-    dwq = dwq + lax.dot_general(R.u[me], R.dq[seg : 2 * seg, :], tn, preferred_element_type=F32)
+    dwq = lax.dot_general(R.u[partner], R.dq[far_rows, :], tn, preferred_element_type=F32)
+    dwq = dwq + lax.dot_general(R.u[me], R.dq[own_rows, :], tn, preferred_element_type=F32)
     R.dw[0:C, :] = dwq.astype(B16)
     R.dvec[...] = jnp.concatenate(
         [
@@ -2493,32 +2669,37 @@
         ],
         axis=0,
     )
-    home.wait_recv()
+    for part in range(2):
+        home_copy(part).wait()
     R.du[1 - mine] = R.from_partner[...].astype(F32)
-    home.wait_send()
-    own_out.wait()
-    far_out.wait()
+    for move in moves:
+        share(*move, False)
+    all_out.wait()
+    for i in range(per):
+        swap_cot(i).wait_send()
     for cp in started:
         cp.wait_send()
 
     def drain(t, _):
         sib_copy(t).wait_send()
 
-        @pl.when(t < pairs - 2)
+        @pl.when(place(t)[0] != 0)
         def _():
-            mate_copy(t).wait_send()
+            for part in range(2):
+                mate_copy(t, part).wait_send()
 
         return 0
 
     lax.fori_loop(0, pairs, drain, 0)
 
 
-def attend_call(n, keep, cid, u, ids_all, vec, low, cot=None, far_cot=None, hid=None):
+def attend_call(n, keep, cid, u, ids_all, vec, low, cot=None, state=None):
     seg = u.shape[1]
     half = n // 2
     mates = half // 2
     pairs = 2 * mates
     total = n * seg
+    rows = min(256, seg)
     dma = pltpu.SemaphoreType.DMA
     inputs = dict(u_in=(u, anyw), ids_all=(ids_all, vmem), vec=(vec, vmem), low=(low, anyw))
     piece = (seg, C)
@@ -2526,29 +2707,85 @@
     scratch = dict(
         u=pltpu.VMEM((n,) + piece, B16), w=pltpu.VMEM((4 * C, C), B16), k=pltpu.VMEM((total, C), B16),
         v=pltpu.VMEM((total, C), B16), qid=pltpu.VMEM((2 * seg, LANES), F32), out=pltpu.VMEM((2 * seg, C), B16),
-        lsem=dma((5,)), gsend=dma((4 * mates,)), grecv=dma((n,)), osem=dma((2,)))
+        lsem=dma((4,)), gsend=dma((4 * mates,)), grecv=dma((n,)))
     if keep:
-        inputs.update(cot=(cot, anyw), far_cot=(far_cot, anyw))
-        outputs = dict(o_home=(home, B16, anyw), dw=((4 * C, C), B16, vmem), dvec=((8, C), F32, vmem),
-                       du=(home, F32, vmem))
+        inputs.update(cot=(cot, anyw), **{k: (a, anyw) for k, a in zip(("params", "first", "second"), state)})
+        outputs = dict(o_home=((2 * seg, C), B16, anyw), dw=((4 * C, C), B16, vmem), dvec=((8, C), F32, vmem),
+                       du=(home, F32, vmem), shares=((3, state[0].shape[0] // 2, C), F32, anyw))
         scratch.update(
-            dz=pltpu.VMEM((2 * seg, C), B16), dout=pltpu.VMEM((2 * seg, C), B16), q=pltpu.VMEM((2 * seg, C), B16),
+            csend=dma((seg // rows,)), crecv=dma((seg // rows,)), dz=pltpu.VMEM((2 * seg, C), B16), dout=pltpu.VMEM((2 * seg, C), B16), q=pltpu.VMEM((2 * seg, C), B16),
             dq=pltpu.VMEM((2 * seg, C), B16), pbuf=pltpu.VMEM((2 * seg, total), B16),
             sbuf=pltpu.VMEM((2 * seg, total), B16), for_sib=pltpu.VMEM((pairs,) + piece, B16),
             from_sib=pltpu.VMEM((pairs,) + piece, B16), sums=pltpu.VMEM((pairs,) + piece, B16),
-            from_mate=pltpu.VMEM((pairs - 2,) + piece, B16), for_home=pltpu.VMEM(piece, B16),
-            from_partner=pltpu.VMEM(piece, B16), ssend=dma((pairs,)), srecv=dma((pairs,)), msend=dma((pairs,)),
-            mrecv=dma((pairs,)), hsem=dma((2,)))
+            from_mate=pltpu.VMEM((pairs - 1,) + piece, B16), for_home=pltpu.VMEM(piece, B16),
+            from_partner=pltpu.VMEM(piece, B16), ssend=dma((pairs,)), srecv=dma((pairs,)), msend=dma((pairs, 2)),
+            mrecv=dma((pairs, 2)), hsend=dma((2,)), hrecv=dma((2,)), wsend=dma((2, 3)), wrecv=dma((3,)))
     else:
-        inputs.update(hid=(hid, vmem))
-        outputs = dict(final=((2 * seg, C), F32, vmem))
-        scratch.update(o_home=pltpu.VMEM(home, B16))
+        outputs = dict(o_home=(home, B16, anyw))
+        scratch.update(osend=dma((seg // rows,)), orecv=dma((seg // rows,)))
 
     def kernel(R):
-        R.rows = min(256, seg)
+        R.rows = rows
         attend_kernel(n, keep, R)
 
     return named_call(kernel, "attend" if keep else "attend_again", cid, inputs, outputs, scratch)
+
+
+def outputs_kernel(n, R):
+    mine = lax.axis_index("height") // (n // 2)
+    seg = R.o_back.shape[0]
+    own, other = (pl.ds(pl.multiple_of(i * seg, seg), seg) for i in (mine, 1 - mine))
+    loads = [
+        pltpu.make_async_copy(R.low.at[pl.ds(R.low.shape[0] - C, C)], R.w.at[0], R.sem.at[0]),
+        pltpu.make_async_copy(R.new_low.at[pl.ds(R.new_low.shape[0] - C, C)], R.w.at[1], R.sem.at[1]),
+        pltpu.make_async_copy(R.hid, R.hid_in, R.sem.at[2]),
+        pltpu.make_async_copy(R.hid2, R.hid2_in, R.sem.at[3]),
+        pltpu.make_async_copy(R.o.at[pl.ds(0, seg)], R.o_in.at[0, own], R.sem.at[4]),
+        pltpu.make_async_copy(R.o_back, R.o_in.at[0, other], R.sem.at[5]),
+        pltpu.make_async_copy(R.o2, R.o_in.at[1], R.sem.at[6]),
+        pltpu.make_async_copy(R.igrad, R.igrad_in, R.sem.at[7]),
+    ]
+    for cp in loads:
+        cp.start()
+    for cp in loads:
+        cp.wait()
+    backs = [
+        pltpu.make_async_copy(R.hid_in, R.hid_out, R.sem.at[2]),
+        pltpu.make_async_copy(R.igrad_in, R.igrad_out, R.sem.at[7]),
+    ]
+    for cp in backs:
+        cp.start()
+    count = R.part.shape[1]
+    parts = R.hid.shape[0] // count
+    last = {}
+    for i in range(2 * parts):
+        which, at = i // parts, pl.ds((i % parts) * count, count)
+        base = (R.hid_in, R.hid2_in)[which]
+        vec = (R.vec, R.new_vec)[which]
+        slot = i % 2
+        if slot in last:
+            last[slot].wait()
+        R.part[slot] = (
+            base[at, :] + jnp.dot(R.o_in[which, at, :], R.w[which], preferred_element_type=F32) + vec[10:11, :])
+        cp = pltpu.make_async_copy(R.part.at[slot], (R.first, R.second)[which].at[at], R.sem.at[8 + slot])
+        cp.start()
+        last[slot] = cp
+    for cp in backs + list(last.values()):
+        cp.wait()
+
+
+def outputs_call(n, hid, hid2, o, o_back, o2, igrad, vec, new_vec, low, new_low):
+    px = hid.shape[0]
+    inputs = dict(hid=(hid, anyw), hid2=(hid2, anyw), o=(o, anyw), o_back=(o_back, anyw), o2=(o2, anyw),
+                  igrad=(igrad, anyw),
+                  vec=(vec, vmem), new_vec=(new_vec, vmem), low=(low, anyw), new_low=(new_low, anyw))
+    whole = ((px, C), F32, anyw)
+    outputs = dict(hid_out=whole, first=whole, second=whole, igrad_out=whole)
+    scratch = dict(
+        w=pltpu.VMEM((2, C, C), B16), hid_in=pltpu.VMEM((px, C), F32), hid2_in=pltpu.VMEM((px, C), F32),
+        igrad_in=pltpu.VMEM((px, C), F32), o_in=pltpu.VMEM((2, px, C), B16), part=pltpu.VMEM((2, min(256, px), C), F32),
+        sem=pltpu.SemaphoreType.DMA((10,)))
+    return named_call(functools.partial(outputs_kernel, n), "outputs", None, inputs, outputs, scratch)
 
 
 def rounded_vectors(vectors):
@@ -2569,6 +2806,37 @@
     count = vectors.shape[0]
     joined = columns == 4 and params.shape[0] % 32 == 0 and rows > 2
 
+    ids = crop_ids.astype(F32)
+    ids_lane = jnp.pad(ids.reshape(canvases, plane), ((0, 8 - canvases), (0, 0)))
+    x = latents.reshape(px, channels)
+    cot = cotangent.reshape(px, channels)
+    cot3 = cotangent.reshape(canvases, plane, channels)
+    shape = latents.shape
+    if joined:
+        first = first_call(columns, n, dims, x, ids_lane, vectors, params)
+        ids_all, mean1, inv1, div, cnt, pick, spread, vec = (
+            first[k] for k in ("ids_all", "mean1", "inv1", "div", "cnt", "pick", "spread", "vec"))
+        masks = [first[k] for k in ("col_l", "col_r", "row_u", "row_d")]
+        hid, u, y1, s1, s2 = (first[k] for k in ("hid", "u", "y1_out", "s1_out", "s2_out"))
+        norms = [first[k] for k in ("mean2", "inv2", "mean3", "inv3")]
+        top, low = first["top"], first["bottom"]
+        att = attend_call(n, True, 4, u.reshape(canvases, plane, channels), ids_all, vec, low, cot3,
+                          (params, first_moment, second_moment))
+        du = att["du"].reshape(px, channels)
+        back = back_call(columns, n, dims, cot, du, hid, y1, norms, s1, s2, pick, spread, div, masks, vec, top, low,
+                         att["dw"], att["o_home"], params.shape[0])
+        new = renew_call(columns, n, dims, back["grad"], back["dh"], x, mean1, inv1, pick, spread, div, cnt, masks, vec,
+                         top, back["g_top"], back["sum_low"], back["dvec"], att["dvec"], params, first_moment,
+                         second_moment, att["shares"], vectors, vector_first, vector_second)
+        new_vec, new_att = new["new_vec"], new["new_att"]
+        o2 = attend_call(n, False, 5, new["u"].reshape(canvases, plane, channels), ids_all, new_vec, new_att)["o_home"]
+        last = outputs_call(n, hid, new["hid"], att["o_home"], back["o_back"], o2.reshape(px, channels), new["igrad"],
+                            vec, new_vec, low, new_att)
+        return (
+            *(last[k].reshape(shape) for k in ("hid_out", "first", "second", "igrad_out")),
+            *(new[k] for k in ("new_w", "new_m", "new_s", "new_vw", "new_vm", "new_vs")),
+        )
+
     def padded(value):
         return jnp.pad(value, ((0, 16 - count), (0, 0)))
 
@@ -2579,93 +2847,53 @@
     stat = jnp.arange(canvases * CROPS, dtype=jnp.int32)[:, None]
     pick = (cell_ids == stat).astype(B16)
     spread = (cell_ids.reshape(-1, 1) == stat.reshape(1, -1)).astype(B16)
-    ids = crop_ids.astype(F32)
     ids_px = jnp.broadcast_to(ids[..., None], (canvases, rows, width, LANES))
-    ids_lane = jnp.pad(ids.reshape(canvases, plane), ((0, 8 - canvases), (0, 0)))
-    x = latents.reshape(px, channels)
-    cot = cotangent.reshape(px, channels)
-    cot3 = cotangent.reshape(canvases, plane, channels)
-
-    if joined:
-        first = first_call(columns, n, dims, x, pick, spread, ids_px, ids_lane, vec, params, cot3)
-        ids_all, mean1, inv1, div, cnt = (first[k] for k in ("ids_all", "mean1", "inv1", "div", "cnt"))
-        masks = [first[k] for k in ("col_l", "col_r", "row_u", "row_d")]
-        hid, u, y1, s1, s2 = (first[k] for k in ("hid", "u", "y1_out", "s1_out", "s2_out"))
-        mean2, inv2, mean3, inv3 = (first[k] for k in ("mean2", "inv2", "mean3", "inv3"))
-        top, low = first["top"], first["bottom"]
-    else:
-        whole = spread_call(columns, n, 8, params).reshape(-1, channels)
-        top, low = whole[: 11 * C], whole[11 * C :]
-        ids_all, mean1, inv1, div, cnt, *masks = layout_call(n, dims, x, pick, spread, ids_px, ids_lane)
-        hid, u, y1, s1, s2, mean2, inv2, mean3, inv3 = resnet_forward_call(
-            n, dims, True, x, pick, spread, cnt, mean1, inv1, masks, vec, top, low)
-    small = (wide_vectors, padded(vector_first), padded(vector_second))
-    u = u.reshape(canvases, plane, channels)
-    if joined:
-        att = attend_call(n, True, 4, u, ids_all, vec, low, cot3, first["far_cot"])
-        du = att["du"].reshape(px, channels)
-        back = back_call(columns, n, dims, cot, du, hid, y1, (mean2, inv2, mean3, inv3), s1, s2, pick, spread, div,
-                         masks, vec, top, low, att["dw"], params.shape[0])
-        new = update_call(columns, n, dims, back["grad"], back["dh"], x, mean1, inv1, pick, spread, div, masks, vec,
-                          top, low, back["g_top"], back["sum_low"], back["dvec"], att["dvec"], params, first_moment,
-                          second_moment, *small, hid, att["o_home"].reshape(px, channels))
-        first_output = new["output"]
-        input_grad, new_params, new_first, new_second = (new[k] for k in ("igrad", "new_w", "new_m", "new_s"))
-        new_small = [new[k] for k in ("new_vw", "new_vm", "new_vs")]
-        new_vec = rounded_vectors(new_small[0])
-        hid2, u2 = resnet_forward_call(
-            n, dims, False, x, pick, spread, cnt, mean1, inv1, masks, new_vec, new["new_top"], new["new_low"])
-        second_output = attend_call(
-            n, False, 5, u2.reshape(canvases, plane, channels), ids_all, new_vec, new["new_low"], hid=hid2)["final"]
-    else:
-        own_cot = lax.dynamic_index_in_dim(cot3, mine, axis=0, keepdims=False)
-        far_cot = lax.ppermute(
-            lax.dynamic_index_in_dim(cot3, 1 - mine, axis=0, keepdims=False), "height", swap)
-        dz = jnp.concatenate([own_cot, far_cot], axis=0)
-        canvas_ids = lax.dynamic_index_in_dim(ids_all, mine, axis=1, keepdims=False)
-        key_ids = canvas_ids.reshape(1, n * plane)
-        query_ids = jnp.stack([canvas_ids[me], canvas_ids[partner]]).reshape(2 * plane, 1)
-        query_ids = jnp.broadcast_to(query_ids, (2 * plane, LANES))
-        offsets = jnp.stack([me, partner]) * plane
-
-        def attention_output(o, hid, low, bias):
-            back = lax.ppermute(o[plane:], "height", swap)
-            ordered = jnp.where(mine == 0, jnp.stack([o[:plane], back]), jnp.stack([back, o[:plane]]))
-            product = jnp.dot(ordered.reshape(px, channels), low[10 * C :], preferred_element_type=F32)
-            return hid + product + bias
-
-        ua = gather_call(n, 4, u)
-        o, dup, dw_att, dvec_att = attention_call(True, ua, key_ids, query_ids, offsets, dz, vec, low)
-        first_output = attention_output(o, hid, low, vec[10])
-        du = scatter_call(n, 6, dup.reshape(n, plane, channels)).reshape(px, channels)
-        norms = (mean1, inv1, mean2, inv2, mean3, inv3)
-        input_grad, matrix_grad, dvec = resnet_backward_call(
-            n, dims, 7, cot, du, hid, y1, x, norms, s1, s2, pick, spread, div, masks, vec, top, low, dw_att)
-        vector_grad = jnp.concatenate([dvec, dvec_att], axis=0)
-        new_params, new_first, new_second, *new_small, new_whole = step_call(
-            columns, n, 9, matrix_grad.reshape((columns, half, 2) + params.shape), params, first_moment,
-            second_moment, vector_grad, *small)
-        new_whole = new_whole.reshape(-1, channels)
-        new_top, new_low = new_whole[: 11 * C], new_whole[11 * C :]
-        new_vec = rounded_vectors(new_small[0])
-        hid2, u2 = resnet_forward_call(
-            n, dims, False, x, pick, spread, cnt, mean1, inv1, masks, new_vec, new_top, new_low)
-        ua2 = gather_call(n, 5, u2.reshape(canvases, plane, channels))
-        (o2,) = attention_call(False, ua2, key_ids, query_ids, offsets, dz, new_vec, new_low)
-        second_output = attention_output(o2, hid2, new_low, new_vec[10])
-    new_vectors, new_vector_first, new_vector_second = [a[:count] for a in new_small]
-    shape = latents.shape
+    whole = spread_call(columns, n, 8, params).reshape(-1, channels)
+    top, low = whole[: 11 * C], whole[11 * C :]
+    ids_all, mean1, inv1, div, cnt, *masks = layout_call(n, dims, x, pick, spread, ids_px, ids_lane)
+    hid, u, y1, s1, s2, mean2, inv2, mean3, inv3 = resnet_forward_call(
+        n, dims, True, x, pick, spread, cnt, mean1, inv1, masks, vec, top, low)
+    own_cot = lax.dynamic_index_in_dim(cot3, mine, axis=0, keepdims=False)
+    far_cot = lax.ppermute(
+        lax.dynamic_index_in_dim(cot3, 1 - mine, axis=0, keepdims=False), "height", swap)
+    dz = jnp.concatenate([own_cot, far_cot], axis=0)
+    canvas_ids = lax.dynamic_index_in_dim(ids_all, mine, axis=1, keepdims=False)
+    key_ids = canvas_ids.reshape(1, n * plane)
+    query_ids = jnp.stack([canvas_ids[me], canvas_ids[partner]]).reshape(2 * plane, 1)
+    query_ids = jnp.broadcast_to(query_ids, (2 * plane, LANES))
+    offsets = jnp.stack([me, partner]) * plane
+
+    def attention_output(o, hid, low, bias):
+        back = lax.ppermute(o[plane:], "height", swap)
+        ordered = jnp.where(mine == 0, jnp.stack([o[:plane], back]), jnp.stack([back, o[:plane]]))
+        product = jnp.dot(ordered.reshape(px, channels), low[10 * C :], preferred_element_type=F32)
+        return hid + product + bias
+
+    ua = gather_call(n, 4, u.reshape(canvases, plane, channels))
+    o, dup, dw_att, dvec_att = attention_call(True, ua, key_ids, query_ids, offsets, dz, vec, low)
+    first_output = attention_output(o, hid, low, vec[10])
+    du = scatter_call(n, 6, dup.reshape(n, plane, channels)).reshape(px, channels)
+    norms = (mean1, inv1, mean2, inv2, mean3, inv3)
+    input_grad, matrix_grad, dvec = resnet_backward_call(
+        n, dims, 7, cot, du, hid, y1, x, norms, s1, s2, pick, spread, div, masks, vec, top, low, dw_att)
+    vector_grad = jnp.concatenate([dvec, dvec_att], axis=0)
+    new_params, new_first, new_second, *new_small, new_whole = step_call(
+        columns, n, 9, matrix_grad.reshape((columns, half, 2) + params.shape), params, first_moment,
+        second_moment, vector_grad, wide_vectors, padded(vector_first), padded(vector_second))
+    new_whole = new_whole.reshape(-1, channels)
+    new_top, new_low = new_whole[: 11 * C], new_whole[11 * C :]
+    new_vec = rounded_vectors(new_small[0])
+    hid2, u2 = resnet_forward_call(
+        n, dims, False, x, pick, spread, cnt, mean1, inv1, masks, new_vec, new_top, new_low)
+    ua2 = gather_call(n, 5, u2.reshape(canvases, plane, channels))
+    (o2,) = attention_call(False, ua2, key_ids, query_ids, offsets, dz, new_vec, new_low)
+    second_output = attention_output(o2, hid2, new_low, new_vec[10])
     return (
-        hid.reshape(shape),
-        first_output.reshape(shape),
-        second_output.reshape(shape),
-        input_grad.reshape(shape),
+        *(a.reshape(shape) for a in (hid, first_output, second_output, input_grad)),
         new_params,
         new_first,
         new_second,
-        new_vectors,
-        new_vector_first,
-        new_vector_second,
+        *(a[:count] for a in new_small),
     )
 
 

time: 572 us -> 537 us (0.939)
  Pallas kernels: 543 us -> 524 us
  local copies, waits for them, and re-layouts: 16.9 us -> 5.14 us
    pallas_call x1 -> x0, Pallas kernels: 39.5 us -> none  [resnet_forward_call(): pl.pallas_call(functools.partial(resnet_forward_kernel, n, dims, keep), o...]
    pallas_call x5 -> x6, Pallas kernels: 503 us -> 524 us  [named_call(): pl.pallas_call(lambda *refs: kernel(Named(shapes, refs)), out_shape=[sds(...]
    unnamed x34 -> x18, local copies, waits for them, and re-layouts: 13.1 us -> 4.45 us
where the time goes in v3:
time: 537 us; the launch traced here: 531 us
  Pallas kernels  524 us (98%)
    pallas_call x6, Pallas kernels, named_call(): pl.pallas_call(lambda *refs: kernel(Named(shapes, refs)), out_shape=[sds(...  524 us

profile of v3, /device:TPU:0, one launch (start us, length us, event | category | flops | bytes accessed | tf_op | source)
XLA Modules:
  0.0 531.3 jit_solution(15832861484502789704)
XLA Ops:
  0.6 0.7 convert_element_type.5
  1.3 0.1 reshape.57
  1.4 0.6 pad.4.refs_1_
  2.0 105.1 %first_forward.1 = (f32[16,512]{1,0:T(8,128)}, bf16[32,128]{1,0:T(8,128)(2,1)}, bf16[128,32]{1,0:T(8,128)(2,1)}, f32[8,8,512]{2,1,0:T(8,128)}, f32[128,512]{1,0:...) custom-call(bf16[1024,512]{1,0:T(8,128)(2,1)} %bitcast.13, ...), custom_call_target="tpu_custom_call" | custom-call | tf_op jit(solution)/shard_map/first_forward/pallas_call | solution.py:1825
  107.1 117.6 %attend.1 = (bf16[1024,512]{1,0:T(8,128)(2,1)}, bf16[2048,512]{1,0:T(8,128)(2,1)}, f32[8,512]{1,0:T(8,128)}, f32[2,512,512]{2,1,0:T(8,128)}, f32[3,176,512]{2,1,0:T(8,128)}) custom-call(bf16[2,512,512]{2,1,0:T(8,128)(2,1)} %bitcast.17, f32[8,8,512]{2,1,0:T(8,128)} %get-tuple-element.62.refs_1_, f32[16,512]{1,0:T(8,128)} %get-tuple-element.63.refs_2_.refs_9_.refs_15_.refs_6_, ...), custom_call_target="tpu_custom_call" | custom-call | tf_op jit(solution)/shard_map/attend/pallas_call | solution.py:1825
  224.8 70.9 %back.1 = (f32[1024,512]{1,0:T(8,128)}, bf16[1024,512]{1,0:T(8,128)(2,1)}, bf16[5632,512]{1,0:T(8,128)(2,1)}, f32[8,512]{1,0:T(8,128)}, bf16[176,512]{1,0:T(8,128)(2,1)}, /*index=5*/bf16[512,512]{1,0:T(8,128)(2,1)}) custom-call(bf16[1024,512]{1,0:T(8,128)(2,1)} %bitcast.12, f32[1024,512]{1,0:T(8,128)} %bitcast.16, ...), custom_call_target="tpu_custom_call" | custom-call | tf_op jit(solution)/shard_map/back/pallas_call | solution.py:1825
  295.6 150.3 %renew.1 = (f32[1024,512]{1,0:T(8,128)}, f32[352,512]{1,0:T(8,128)}, f32[352,512]{1,0:T(8,128)}, f32[352,512]{1,0:T(8,128)}, f32[11,512]{1,0:T(8,128)}, /*index=...) custom-call(bf16[5632,512]{1,0:T(8,128)(2,1)} %get-tuple-element.60., ...), custom_call_target="tpu_custom_call" | custom-call | tf_op jit(solution)/shard_map/renew/pallas_call | solution.py:1825
  446.0 69.8 %attend_again.1 = bf16[2,512,512]{2,1,0:T(8,128)(2,1)} custom-call(bf16[2,512,512]{2,1,0:T(8,128)(2,1)} %bitcast.18, f32[8,8,512]{2,1,0:T(8,128)} %get-tuple-element.62.refs_1_, f32[16,512]{1,0:T(8,128)} %get-tuple-element.95.refs_2_.refs_7_, bf16[2048,512]{1,0:T(8,128)(2,1)} %get-tuple-element.96.refs_3_.refs_9_), custom_call_target="tpu_custom_call" | custom-call | tf_op jit(solution)/shard_map/attend_again/pallas_call | solution.py:1825
  515.8 0.0 copy-start.2
  515.8 0.0 copy-start.1
  515.9 10.5 %outputs.1 = (f32[1024,512]{1,0:T(8,128)}, f32[1024,512]{1,0:T(8,128)}, f32[1024,512]{1,0:T(8,128)}, f32[1024,512]{1,0:T(8,128)}) custom-call(f32[1024,512]{1,0:T(8,128)} %get-tuple-element.59.refs_2_.refs_0_, f32[1024,512]{1,0:T(8,128)} %get-tuple-element.92.refs_1_, bf16[1024,512]{1,0:T(8,128)(2,1)} %get-tuple-element.73.refs_13_.refs_2_, ...), custom_call_target="tpu_custom_call" | custom-call | tf_op jit(solution)/shard_map/outputs/pallas_call | solution.py:1825
  526.4 0.0 copy-start
  526.4 0.0 copy-done.2
  526.4 0.0 copy-start.5
  526.4 0.0 copy-start.4
  526.4 0.0 copy-start.3
  526.4 0.9 copy.25
  527.3 0.0 copy-done.1
  527.3 0.9 copy.26
  528.2 0.0 copy-done
  528.2 0.9 copy.27
  529.0 0.0 copy-done.5
  529.0 0.6 copy.28
  529.6 0.0 copy-done.4
  529.6 0.6 copy.29
  530.2 0.0 copy-done.3
  530.2 0.6 copy.30
Async XLA Ops:
  515.8 10.6 %copy-start.2 = (f32[352,512]{1,0:T(8,128)S(1)}, f32[352,512]{1,0:T(8,128)}, u32[]{:S(2)}) copy-start(f32[352,512]{1,0:T(8,128)} %get-tuple-element.122) | copy-start | bytes 2162692
  515.8 11.4 %copy-start.1 = (f32[352,512]{1,0:T(8,128)S(1)}, f32[352,512]{1,0:T(8,128)}, u32[]{:S(2)}) copy-start(f32[352,512]{1,0:T(8,128)} %get-tuple-element.123) | copy-start | bytes 2162692
  526.4 1.8 copy-start
  526.4 2.6 copy-start.5
  526.4 3.2 copy-start.4
  526.4 3.8 copy-start.3

commit v4 on v3

--- a/solution.py
+++ b/solution.py
@@ -21,6 +21,11 @@
 matrix_rate = 0.015
 vector_rate = 0.2
 mask_fill = -1e30
+
+HEIGHT = "height"
+CANVAS = "canvas"
+LOAD = "load"
+STORE = "store"
 
 F32 = jnp.float32
 B16 = jnp.bfloat16
@@ -99,28 +104,38 @@
     return None
 
 
+def fold(packed):
+    rows = packed.shape[0] // 2
+    sub = lax.broadcasted_iota(jnp.int32, (rows, LANES), 1) & (SPAN - 1)
+    return jnp.where(sub < 2 * TILES, packed[:rows], pltpu.roll(packed[rows:], 2 * TILES, 1))
+
+
+def unfold(folded):
+    return jnp.concatenate([folded, pltpu.roll(folded, LANES - 2 * TILES, folded.ndim - 1)], axis=folded.ndim - 2)
+
+
 def greet(n):
-    me = lax.axis_index("height")
+    me = lax.axis_index(HEIGHT)
     barrier = pltpu.get_barrier_semaphore()
     for d in range(1, n):
         pl.semaphore_signal(
-            barrier, inc=1, device_id={"height": lax.rem(me + d, n)}, device_id_type=MESH
+            barrier, inc=1, device_id={HEIGHT: lax.rem(me + d, n)}, device_id_type=MESH
         )
     pl.semaphore_wait(barrier, n - 1)
 
 
 def spread_copies(n, buf, send, recv, rnd):
-    me = lax.axis_index("height")
+    me = lax.axis_index(HEIGHT)
     return [
         pltpu.make_async_remote_copy(
             src_ref=buf.at[rnd, 0],
             dst_ref=buf.at[rnd, d],
             send_sem=send.at[rnd, d],
             recv_sem=recv.at[rnd, d],
-            device_id={"height": lax.rem(me + d, n)},
+            device_id={HEIGHT: lax.rem(me + d, n)},
             device_id_type=MESH,
         )
-        for d in range(1, n)
+        for d in sorted(range(1, n), key=lambda d: abs(d - n // 2))
     ]
 
 
@@ -142,7 +157,7 @@
     return [lane_group_sum(t) for t in tiles_of(split_dot(pick_ref[...], cell_value))]
 
 
-def stats_payload(load, pick_ref, spread_ref, count_ref, cells, tmp_a, tmp_b):
+def stats_payload(load, pick_ref, spread_ref, count_ref, cells, tmp_a, tmp_b, counted=True):
     cell_totals(load, tmp_a, cells)
     sums = group_totals(pick_ref, tmp_a[...])
     count = count_ref[...]
@@ -156,13 +171,13 @@
 
     cell_totals(centred, tmp_a, cells)
     squares = group_totals(pick_ref, tmp_a[...])
-    return pack([sums, squares, [count] * TILES])
-
-
-def combine_stats(gathered):
+    return pack([sums, squares, [count] * TILES]) if counted else fold(pack([sums, squares]))
+
+
+def combine_stats(gathered, counts=None):
     sums = gathered
     squares = shift_down(gathered, 1)
-    counts = shift_down(gathered, 2)
+    counts = shift_down(gathered, 2) if counts is None else counts
     divisor = jnp.maximum(jnp.sum(counts, axis=0), 1.0)
     mean = jnp.sum(sums, axis=0) / divisor
     apart = sums / jnp.maximum(counts, 1.0) - mean[None]
@@ -199,16 +214,16 @@
 
 def layout_body(n, dims, x, pick, spread, ids_px, ids_lane, ids_all, mean_c, inv_c, div, cnt,
                 col_l, col_r, row_u, row_d, buf, idbuf, halo, tmp_a, tmp_b, send, recv, isend, irecv,
-                hsend, hrecv, pump=no_pump):
+                hsend, hrecv, pump=no_pump, cnt_all=None):
     canvases, rows, width = dims
     cells = canvases * rows * width // UNIT
-    me = lax.axis_index("height")
+    me = lax.axis_index(HEIGHT)
     id_copies = []
     idbuf[0] = ids_lane[...]
     for d in range(1, n):
         cp = pltpu.make_async_remote_copy(
             src_ref=idbuf.at[0], dst_ref=idbuf.at[d], send_sem=isend.at[d], recv_sem=irecv.at[d],
-            device_id={"height": lax.rem(me + d, n)}, device_id_type=MESH)
+            device_id={HEIGHT: lax.rem(me + d, n)}, device_id_type=MESH)
         cp.start()
         id_copies.append(cp)
     up, down = halo_copies(n, ids_px.at[:, 0], ids_px.at[:, rows - 1], halo, hsend, hrecv)
@@ -244,6 +259,8 @@
     for cp in copies:
         cp.wait_recv()
     mean, inv, divisor = combine_stats(buf[0])
+    if cnt_all is not None:
+        cnt_all[...] = shift_down(buf[0], 2)
     mean_c[...] = split_dot(spread[...], unpack(mean))
     inv_c[...] = split_dot(spread[...], unpack(inv))
     div[...] = unpack(divisor)[:, :LANES]
@@ -257,18 +274,18 @@
 
 
 def halo_copies(n, first_row, last_row, halo, hsend, hrecv):
-    me = lax.axis_index("height")
+    me = lax.axis_index(HEIGHT)
     up = pltpu.make_async_remote_copy(
         src_ref=first_row, dst_ref=halo.at[1], send_sem=hsend.at[0], recv_sem=hrecv.at[1],
-        device_id={"height": lax.rem(me + n - 1, n)}, device_id_type=MESH)
+        device_id={HEIGHT: lax.rem(me + n - 1, n)}, device_id_type=MESH)
     down = pltpu.make_async_remote_copy(
         src_ref=last_row, dst_ref=halo.at[0], send_sem=hsend.at[1], recv_sem=hrecv.at[0],
-        device_id={"height": lax.rem(me + 1, n)}, device_id_type=MESH)
+        device_id={HEIGHT: lax.rem(me + 1, n)}, device_id_type=MESH)
     return up, down
 
 
 def start_halo(n, up, down):
-    me = lax.axis_index("height")
+    me = lax.axis_index(HEIGHT)
 
     @pl.when(me > 0)
     def _():
@@ -280,7 +297,7 @@
 
 
 def wait_halo(n, up, down, halo, edge):
-    me = lax.axis_index("height")
+    me = lax.axis_index(HEIGHT)
 
     @pl.when(me > 0)
     def _():
@@ -354,8 +371,8 @@
 
 class Convolver:
     def __init__(self, n, dims, x, pick, spread, cnt, col_l, col_r, row_u, row_d, halo, buf, tmp_a, tmp_b, send,
-                 recv, hsend, hrecv):
-        self.n, self.dims = n, dims
+                 recv, hsend, hrecv, cnt_all=None):
+        self.n, self.dims, self.cnt_all = n, dims, cnt_all
         self.x, self.pick, self.spread, self.cnt = x, pick, spread, cnt
         self.col_l, self.col_r, self.row_u, self.row_d = col_l, col_r, row_u, row_d
         self.halo, self.buf, self.tmp_a, self.tmp_b = halo, buf, tmp_a, tmp_b
@@ -427,14 +444,17 @@
         def load(i):
             return source[pl.ds(i * 16 * UNIT, 16 * UNIT), :]
 
-        self.buf[rnd, 0] = stats_payload(load, self.pick, self.spread, self.cnt, self.cells, self.tmp_a, self.tmp_b)
+        counted = self.cnt_all is None
+        self.buf[rnd, 0] = stats_payload(
+            load, self.pick, self.spread, self.cnt, self.cells, self.tmp_a, self.tmp_b, counted)
         copies = spread_copies(self.n, self.buf, self.send, self.recv, rnd)
         for cp in copies:
             cp.start()
         pump()
         for cp in copies:
             cp.wait_recv()
-        m, s, _ = combine_stats(self.buf[rnd])
+        m, s, _ = (
+            combine_stats(self.buf[rnd]) if counted else combine_stats(unfold(self.buf[rnd]), self.cnt_all[...]))
         mean[...] = split_dot(self.spread[...], unpack(m))
         inv[...] = split_dot(self.spread[...], unpack(s))
         self.sent = self.sent + copies
@@ -690,7 +710,7 @@
 
 
 def gather_kernel(n, u, ua, lsem, send, recv):
-    me = lax.axis_index("height")
+    me = lax.axis_index(HEIGHT)
     half = n // 2
     mine = me // half
     base = mine * half
@@ -706,7 +726,7 @@
     barrier = pltpu.get_barrier_semaphore()
     peers = [partner, sibling] + [mate(j) for j in range(1, mates)]
     for p in peers:
-        pl.semaphore_signal(barrier, inc=1, device_id={"height": p}, device_id_type=MESH)
+        pl.semaphore_signal(barrier, inc=1, device_id={HEIGHT: p}, device_id_type=MESH)
     pl.semaphore_wait(barrier, len(peers))
     count = [0]
     started = []
@@ -714,7 +734,7 @@
     def push(src, slot, to):
         cp = pltpu.make_async_remote_copy(
             src_ref=src, dst_ref=ua.at[slot], send_sem=send.at[count[0]], recv_sem=recv.at[slot],
-            device_id={"height": to}, device_id_type=MESH)
+            device_id={HEIGHT: to}, device_id_type=MESH)
         count[0] += 1
         cp.start()
         started.append(cp)
@@ -722,7 +742,7 @@
     def arrived(slot):
         pltpu.make_async_remote_copy(
             src_ref=u.at[0], dst_ref=ua.at[slot], send_sem=send.at[0], recv_sem=recv.at[slot],
-            device_id={"height": partner}, device_id_type=MESH).wait_recv()
+            device_id={HEIGHT: partner}, device_id_type=MESH).wait_recv()
 
     own = pltpu.make_async_copy(u.at[mine], ua.at[me], lsem.at[0])
     own.start()
@@ -771,7 +791,7 @@
 
 
 def scatter_kernel(n, dup, out, from_sib, from_mate, mine_sum, from_partner, lsem, send, recv):
-    me = lax.axis_index("height")
+    me = lax.axis_index(HEIGHT)
     half = n // 2
     mine = me // half
     base = mine * half
@@ -787,7 +807,7 @@
 
     peers = [partner, sibling] + [mate(j) for j in range(1, mates)]
     for p in peers:
-        pl.semaphore_signal(barrier, inc=1, device_id={"height": p}, device_id_type=MESH)
+        pl.semaphore_signal(barrier, inc=1, device_id={HEIGHT: p}, device_id_type=MESH)
     pl.semaphore_wait(barrier, len(peers))
     order = [(j, far) for j in range(1, mates) for far in (1, 0)] + [(0, 1), (0, 0)]
 
@@ -800,7 +820,7 @@
         cp = pltpu.make_async_remote_copy(
             src_ref=dup.at[rows_of(j, far, 1 - core)], dst_ref=from_sib.at[t],
             send_sem=send.at[t], recv_sem=recv.at[t],
-            device_id={"height": sibling}, device_id_type=MESH)
+            device_id={HEIGHT: sibling}, device_id_type=MESH)
         cp.start()
         sib.append(cp)
     base_sem = len(order)
@@ -814,7 +834,7 @@
             cp = pltpu.make_async_remote_copy(
                 src_ref=mine_sum.at[t], dst_ref=from_mate.at[at],
                 send_sem=send.at[base_sem + at], recv_sem=recv.at[base_sem + at],
-                device_id={"height": mate(j)}, device_id_type=MESH)
+                device_id={HEIGHT: mate(j)}, device_id_type=MESH)
             cp.start()
             out_copies.append(cp)
     t_far, t_own = len(order) - 2, len(order) - 1
@@ -823,21 +843,21 @@
         at = (j - 1) * 2 + 1
         pltpu.make_async_remote_copy(
             src_ref=mine_sum.at[0], dst_ref=from_mate.at[at], send_sem=send.at[0],
-            recv_sem=recv.at[base_sem + at], device_id={"height": sibling},
+            recv_sem=recv.at[base_sem + at], device_id={HEIGHT: sibling},
             device_id_type=MESH).wait_recv()
         total = total + from_mate[at].astype(F32)
     mine_sum[t_far] = total.astype(B16)
     last = base_sem + 2 * (mates - 1)
     home = pltpu.make_async_remote_copy(
         src_ref=mine_sum.at[t_far], dst_ref=from_partner, send_sem=send.at[last],
-        recv_sem=recv.at[last], device_id={"height": partner}, device_id_type=MESH)
+        recv_sem=recv.at[last], device_id={HEIGHT: partner}, device_id_type=MESH)
     home.start()
     total = dup[me].astype(F32) + from_sib[t_own].astype(F32)
     for j in range(1, mates):
         at = (j - 1) * 2
         pltpu.make_async_remote_copy(
             src_ref=mine_sum.at[0], dst_ref=from_mate.at[at], send_sem=send.at[0],
-            recv_sem=recv.at[base_sem + at], device_id={"height": sibling},
+            recv_sem=recv.at[base_sem + at], device_id={HEIGHT: sibling},
             device_id_type=MESH).wait_recv()
         total = total + from_mate[at].astype(F32)
     out[mine] = total
@@ -1110,8 +1130,8 @@
     def __init__(self, columns, n):
         self.columns, self.n, self.seats = columns, n, n // 2
         self.phases = columns.bit_length() - 1
-        self.c = lax.axis_index("canvas")
-        self.h = lax.axis_index("height")
+        self.c = lax.axis_index(CANVAS)
+        self.h = lax.axis_index(HEIGHT)
         self.seat, self.core = self.h // 2, lax.rem(self.h, 2)
         flips = [
             (1 - 2 * lax.rem(self.c // 2**t, 2)) * 2**t for t in range(self.phases)
@@ -1133,19 +1153,19 @@
         return col
 
     def mate(self, k):
-        return {"canvas": self.c + self.flips[k], "height": self.h}
+        return {CANVAS: self.c + self.flips[k], HEIGHT: self.h}
 
     def sibling(self):
-        return {"canvas": self.c, "height": 2 * self.seat + 1 - self.core}
+        return {CANVAS: self.c, HEIGHT: 2 * self.seat + 1 - self.core}
 
     def beside(self, step):
-        return {"canvas": self.c, "height": self.h + 2 * step}
+        return {CANVAS: self.c, HEIGHT: self.h + 2 * step}
 
     def greet(self):
         barrier = pltpu.get_barrier_semaphore()
         for d in range(1, self.n):
             pl.semaphore_signal(
-                barrier, inc=1, device_id={"canvas": self.c, "height": lax.rem(self.h + d, self.n)},
+                barrier, inc=1, device_id={CANVAS: self.c, HEIGHT: lax.rem(self.h + d, self.n)},
                 device_id_type=MESH)
         for k in range(self.phases):
             pl.semaphore_signal(barrier, inc=1, device_id=self.mate(k), device_id_type=MESH)
@@ -1321,12 +1341,12 @@
     def vector_copy(d):
         src = lax.rem(g.h + d, n)
         return remote(vbuf.at[g.h], vbuf.at[g.h], vsend.at[d], vrecv.at[g.h],
-                      {"canvas": g.c, "height": src})
+                      {CANVAS: g.c, HEIGHT: src})
 
     def vector_arrival(d):
         src = lax.rem(g.h + d, n)
         return remote(vbuf.at[src], vbuf.at[src], vsend.at[d], vrecv.at[src],
-                      {"canvas": g.c, "height": src})
+                      {CANVAS: g.c, HEIGHT: src})
 
     for d in range(1, n):
         vector_copy(d).start()
@@ -1513,7 +1533,7 @@
         return pl.ds(self.row(q, seat, core), self.size)
 
     def at_column(self, col):
-        return {"canvas": col, "height": self.g.h}
+        return {CANVAS: col, HEIGHT: self.g.h}
 
     def halves(self):
         first = 2 * lax.rem(self.g.c, 2)
@@ -1569,22 +1589,14 @@
                     remote(piece, self.part(block, half), send.at[0], recv.at[half], self.at_column(col)).wait_recv()
 
 
-def gate(only, q, seat, core, do):
-    if only is None:
-        do()
-    else:
-        pl.when(only(q, seat, core))(do)
-
-
-def gather_pieces(group, piece, dest, own, zsend, msend, ssend, recv, srecv, only=None):
+def gather_pieces(group, piece, dest, own, zsend, msend, ssend, recv, srecv):
     g = group.g
     seats, phases = g.seats, g.phases
     local = pltpu.make_async_copy(piece, dest.at[group.rows(g.c, g.seat, g.core)], own.at[0])
 
-    def gated(e, seat, do):
-        gate(only, g.column(e), seat, g.core, do)
-
-    gated(0, g.seat, local.start)
+    local.start()
+    top = 1 << (phases - 1)
+    lines = [0, top]
 
     def slot(e, seat):
         return dest.at[group.rows(g.column(e), seat, g.core)]
@@ -1593,31 +1605,32 @@
         k_top = phases if e == 0 else lowest_bit(e)
         for k in range(k_top - 1, -1, -1):
             cp = remote(src, slot(e, seat), msend.at[k, e, seat], recv.at[e | (1 << k), seat], g.mate(k))
-            cp.start() if start else cp.wait_send()
+            do = cp.start if start else cp.wait_send
+            if e == 0 and k == phases - 1:
+                pl.when(seat == g.seat)(do)
+            else:
+                do()
         cp = remote(src, slot(e, seat), ssend.at[e, seat], srecv.at[e, seat], g.sibling())
         cp.start() if start else cp.wait_send()
 
-    def along(seat, step, src, start):
-        cp = remote(src, slot(0, seat), zsend.at[(step + 1) // 2, seat], recv.at[0, seat], g.beside(step))
+    def along(e, seat, step, src, start):
+        cp = remote(src, slot(e, seat), zsend.at[(step + 1) // 2, min(e, 1), seat], recv.at[e, seat], g.beside(step))
         cp.start() if start else cp.wait_send()
 
-    def line(seat, src, start):
+    def line(e, seat, src, start):
         @pl.when((seat <= g.seat) & (g.seat < seats - 1))
         def _():
-            along(seat, 1, src, start)
+            along(e, seat, 1, src, start)
 
         @pl.when((seat >= g.seat) & (g.seat > 0))
         def _():
-            along(seat, -1, src, start)
+            along(e, seat, -1, src, start)
 
     def handle(e, seat):
-        def do():
-            remote(piece, slot(e, seat), ssend.at[0, 0], recv.at[e, seat], g.sibling()).wait_recv()
-            if e == 0:
-                line(seat, slot(0, seat), True)
-            forward(e, seat, slot(e, seat), True)
-
-        gated(e, seat, do)
+        remote(piece, slot(e, seat), ssend.at[0, 0], recv.at[e, seat], g.sibling()).wait_recv()
+        if e in lines:
+            line(e, seat, slot(e, seat), True)
+        forward(e, seat, slot(e, seat), True)
 
     early = sorted((e for e in range(1, 2**phases) if lowest_bit(e) > 0), key=lambda e: -lowest_bit(e))
     late = [e for e in range(1, 2**phases) if lowest_bit(e) == 0]
@@ -1631,11 +1644,8 @@
                 for e in todo:
                     handle(e, seat)
 
-    def first():
-        line(g.seat, piece, True)
-        forward(0, g.seat, piece, True)
-
-    gated(0, g.seat, first)
+    forward(0, g.seat, piece, True)
+    line(0, g.seat, piece, True)
     yield
     for e in early:
         handle(e, g.seat)
@@ -1652,24 +1662,19 @@
 
     def siblings(seat, _):
         for e in range(2**phases):
-            q = g.column(e, g.other_flips)
-            cp = remote(piece, dest.at[group.rows(q, seat, 1 - g.core)], ssend.at[0, 0], srecv.at[e, seat],
-                        g.sibling())
-            gate(only, q, seat, 1 - g.core, cp.wait_recv)
+            remote(piece, dest.at[group.rows(g.column(e, g.other_flips), seat, 1 - g.core)], ssend.at[0, 0],
+                   srecv.at[e, seat], g.sibling()).wait_recv()
         return 0
 
     lax.fori_loop(0, seats, siblings, 0)
-    gated(0, g.seat, local.wait)
+    local.wait()
     yield True
 
     def drain(seat, _):
-        def sent(e):
+        for e in range(2**phases):
             forward(e, seat, slot(e, seat), False)
-            if e == 0:
-                line(seat, slot(0, seat), False)
-
-        for e in range(2**phases):
-            gated(e, seat, functools.partial(sent, e))
+            if e in lines:
+                line(e, seat, slot(e, seat), False)
         return 0
 
     lax.fori_loop(0, seats, drain, 0)
@@ -1680,7 +1685,7 @@
     dma = pltpu.SemaphoreType.DMA
     return [
         dma((1,)),
-        dma((2, seats)),
+        dma((2, 2, seats)),
         dma((phases, columns, seats)),
         dma((columns, seats)),
         dma((columns, seats)),
@@ -1688,7 +1693,7 @@
     ]
 
 
-def reduce_pieces(group, src, piece, sib, got, box, gsend, grecv, psend, precv, usend, urecv, only=None):
+def reduce_pieces(group, src, piece, sib, got, box, gsend, grecv, psend, precv, usend, urecv):
     g = group.g
     seats, phases = g.seats, g.phases
     slots = 2**phases
@@ -1708,11 +1713,11 @@
 
     def line_copy(seat):
         return remote(src.at[mine(0, seat), :], box.at[g.seat], usend.at[seat], urecv.at[g.seat],
-                      {"canvas": g.c, "height": 2 * seat + g.core})
+                      {CANVAS: g.c, HEIGHT: 2 * seat + g.core})
 
     def line_arrival(seat):
         return remote(src.at[mine(0, seat), :], box.at[seat], usend.at[seat], urecv.at[seat],
-                      {"canvas": g.c, "height": 2 * seat + g.core})
+                      {CANVAS: g.c, HEIGHT: 2 * seat + g.core})
 
     def local(e, seat, below):
         total = src[mine(e, seat), :].astype(F32) + sib[e, seat].astype(F32)
@@ -1720,15 +1725,9 @@
             total = total + got[k, e >> (k + 1), seat].astype(F32)
         return total
 
-    def gated(e, seat, do):
-        gate(only, g.column(e), seat, g.core, do)
-
-    def gated_sibling(e, seat, do):
-        gate(only, g.column(e, g.other_flips), seat, 1 - g.core, do)
-
     for e in order:
         for seat in turns:
-            gated_sibling(e, seat, sibling_copy(e, seat).start)
+            sibling_copy(e, seat).start()
     yield
 
     def pass_on(e, k, seat):
@@ -1742,7 +1741,7 @@
         if e == 0:
             break
         for seat in turns:
-            gated(e, seat, functools.partial(pass_on, e, lowest_bit(e), seat))
+            pass_on(e, lowest_bit(e), seat)
             yield
 
     def own_column(seat):
@@ -1756,34 +1755,28 @@
             line_copy(seat).start()
 
     for seat in turns:
-        gated(0, seat, functools.partial(own_column, seat))
+        own_column(seat)
         yield
-
-    def last():
-        total = local(0, g.seat, phases)
-        for seat in turns:
-            @pl.when(seat != g.seat)
-            def _():
-                line_arrival(seat).wait_recv()
-
-            total = total + jnp.where(seat == g.seat, 0.0, box[seat].astype(F32))
-        piece[...] = total.astype(B16)
-
-    gated(0, g.seat, last)
+    total = local(0, g.seat, phases)
+    for seat in turns:
+        @pl.when(seat != g.seat)
+        def _():
+            line_arrival(seat).wait_recv()
+
+        total = total + jnp.where(seat == g.seat, 0.0, box[seat].astype(F32))
+    piece[...] = total.astype(B16)
     yield True
 
     def drain(seat, _):
-        def sent(e):
+        for e in range(slots):
+            sibling_copy(e, seat).wait_send()
             if e > 0:
                 phase_copy(lowest_bit(e), e, seat).wait_send()
-            else:
-                @pl.when(seat != g.seat)
-                def _():
-                    line_copy(seat).wait_send()
-
-        for e in range(slots):
-            gated_sibling(e, seat, sibling_copy(e, seat).wait_send)
-            gated(e, seat, functools.partial(sent, e))
+
+        @pl.when(seat != g.seat)
+        def _():
+            line_copy(seat).wait_send()
+
         return 0
 
     lax.fori_loop(0, seats, drain, 0)
@@ -1818,16 +1811,60 @@
 
 
 def named_call(kernel, name, cid, inputs, outputs, scratch):
+    loads = [k for k, (_, spec) in inputs.items() if spec == LOAD]
+    stores = [k for k, (_, _, spec) in outputs.items() if spec == STORE]
+    parts = 12
     shapes = {**inputs, **outputs, **scratch}
     flat = []
     for value in scratch.values():
         flat += value if isinstance(value, list) else [value]
+    held = [pltpu.VMEM(inputs[k][0].shape, inputs[k][0].dtype) for k in loads]
+    held += [pltpu.VMEM(*outputs[k][:2]) for k in stores]
+    sems = [pltpu.SemaphoreType.DMA((max(len(loads), 1),)), pltpu.SemaphoreType.DMA((max(len(stores), 1), parts))]
+
+    def wrapped(*refs):
+        own = len(held) + len(sems)
+        R = Named(shapes, refs[:-own])
+        kept, (load_sem, store_sem) = refs[-own:-2], refs[-2:]
+        waiting, begun, ends = {}, {k: 0 for k in stores}, []
+        for i, k in enumerate(loads):
+            waiting[k] = pltpu.make_async_copy(getattr(R, k), kept[i], load_sem.at[i])
+            waiting[k].start()
+            setattr(R, k, kept[i])
+        targets = {}
+        for i, k in enumerate(stores):
+            targets[k] = getattr(R, k)
+            setattr(R, k, kept[len(loads) + i])
+
+        def need(*names):
+            for k in names:
+                if k in waiting:
+                    waiting.pop(k).wait()
+
+        def store(k, first=None, count=None):
+            src, dst = getattr(R, k), targets[k]
+            if first is not None:
+                src, dst = src.at[pl.ds(first, count)], dst.at[pl.ds(first, count)]
+            cp = pltpu.make_async_copy(src, dst, store_sem.at[stores.index(k), begun[k]])
+            cp.start()
+            begun[k] += 1
+            ends.append(cp)
+
+        R.need, R.store = need, store
+        kernel(R)
+        need(*list(waiting))
+        for k in stores:
+            if not begun[k]:
+                store(k)
+        for cp in ends:
+            cp.wait()
+
     results = pl.pallas_call(
-        lambda *refs: kernel(Named(shapes, refs)),
+        wrapped,
         out_shape=[sds(shape, kind) for shape, kind, _ in outputs.values()],
-        in_specs=[spec for _, spec in inputs.values()],
-        out_specs=[spec for _, _, spec in outputs.values()],
-        scratch_shapes=flat,
+        in_specs=[anyw if spec == LOAD else spec for _, spec in inputs.values()],
+        out_specs=[anyw if spec == STORE else spec for _, _, spec in outputs.values()],
+        scratch_shapes=flat + held + sems,
         compiler_params=params_of(cid),
         name=name,
     )(*[array for array, _ in inputs.values()])
@@ -1838,10 +1875,10 @@
     barrier = pltpu.get_barrier_semaphore()
     for d in range(1, grid.n):
         pl.semaphore_signal(
-            barrier, inc=1, device_id={"canvas": grid.c, "height": lax.rem(grid.h + d, grid.n)}, device_id_type=MESH)
+            barrier, inc=1, device_id={CANVAS: grid.c, HEIGHT: lax.rem(grid.h + d, grid.n)}, device_id_type=MESH)
     for d in range(1, grid.columns):
         pl.semaphore_signal(
-            barrier, inc=1, device_id={"canvas": lax.rem(grid.c + d, grid.columns), "height": grid.h},
+            barrier, inc=1, device_id={CANVAS: lax.rem(grid.c + d, grid.columns), HEIGHT: grid.h},
             device_id_type=MESH)
     pl.semaphore_wait(barrier, grid.n - 1 + grid.columns - 1)
 
@@ -1896,11 +1933,14 @@
             engines[1].pump()
         turn[0] += 1
 
+    R.need("x")
     layout_body(n, dims, R.x, R.pick, R.spread, R.ids_px, R.ids_lane, R.ids_all, R.mean1, R.inv1, R.div, R.cnt,
-                R.col_l, R.col_r, R.row_u, R.row_d, *R.layout, pump=pump)
+                R.col_l, R.col_r, R.row_u, R.row_d, *R.layout, pump=pump, cnt_all=R.cnt_all)
+    for k in ("col_l", "col_r", "row_u", "row_d"):
+        R.store(k)
     pump()
     conv = Convolver(n, dims, R.x, R.pick, R.spread, R.cnt, R.col_l, R.col_r, R.row_u, R.row_d, R.halo, R.buf,
-                     R.tmp_a, R.tmp_b, R.send, R.recv, R.hsend, R.hrecv)
+                     R.tmp_a, R.tmp_b, R.send, R.recv, R.hsend, R.hrecv, R.cnt_all)
     vec = R.vec
     conv.activate(R.x, R.mean1, R.inv1, vec[0:1, :], vec[1:2, :], R.s1, 0, pump)
     out_s1 = pltpu.make_async_copy(R.s1, R.s1_out, R.osem.at[0])
@@ -1933,6 +1973,7 @@
         R.hid[at, :] = total + vec[5:6, :] + R.x[at, :].astype(F32)
 
     conv.convolve(R.s2, across(R.w_top, R.w_low), emit_second)
+    R.store("hid")
     conv.statistics(R.hid, R.mean3, R.inv3, 1)
     conv.normalise(R.hid, R.mean3, R.inv3, vec[6:7, :], vec[7:8, :], R.u)
     for cp in conv.sent:
@@ -1953,13 +1994,13 @@
     tall = (canvases, rows + 2, width)
     half = block.shape[0] // 2
     dma = pltpu.SemaphoreType.DMA
-    inputs = dict(x=(x, vmem), ids_lane=(ids_lane, vmem), vectors=(vectors, vmem), block=(block, vmem))
+    inputs = dict(x=(x, LOAD), ids_lane=(ids_lane, vmem), vectors=(vectors, vmem), block=(block, vmem))
     cell = ((cells, C), F32, vmem)
     outputs = dict(
         vec=((16, C), F32, vmem), pick=((stats, cells), B16, vmem), spread=((cells, stats), B16, vmem),
         ids_all=((n,) + ids_lane.shape, F32, vmem), mean1=cell, inv1=cell, div=((stats, LANES), F32, vmem),
-        cnt=((stats, LANES), F32, vmem), col_l=(tall + (LANES,), F32, vmem), col_r=(tall + (LANES,), F32, vmem),
-        row_u=((px, LANES), F32, vmem), row_d=((px, LANES), F32, vmem), hid=((px, C), F32, vmem),
+        cnt=((stats, LANES), F32, vmem), cnt_all=((n, stats, LANES), F32, vmem), col_l=(tall + (LANES,), F32, STORE), col_r=(tall + (LANES,), F32, STORE),
+        row_u=((px, LANES), F32, STORE), row_d=((px, LANES), F32, STORE), hid=((px, C), F32, STORE),
         u=((px, C), B16, vmem), mean2=cell, inv2=cell, mean3=cell, inv3=cell, y1_out=((px, C), F32, anyw),
         s1_out=(tall + (3 * C,), B16, anyw), s2_out=(tall + (3 * C,), B16, anyw),
         top=((11 * C, C), B16, anyw), bottom=((11 * C, C), B16, anyw))
@@ -1970,7 +2011,7 @@
         pieces=pltpu.VMEM((2, half, C), B16), tsend=dma((2, 2)), trecv=dma((2, 1)),
         gather0=gather_pieces_scratch(columns, n), gather1=gather_pieces_scratch(columns, n),
         layout=layout_scratch(n, dims, ids_lane), halo=pltpu.VMEM((2, 2, canvases, width, C), B16),
-        buf=pltpu.VMEM((2, n, stats, LANES), F32), tmp_a=pltpu.VMEM((cells, C), F32),
+        buf=pltpu.VMEM((2, n, stats // 2, LANES), F32), tmp_a=pltpu.VMEM((cells, C), F32),
         tmp_b=pltpu.VMEM((cells, C), F32), send=dma((2, n)), recv=dma((2, n)), hsend=dma((2, 2)),
         hrecv=dma((2, 2)), osem=dma((5,)))
     return named_call(functools.partial(first_kernel, columns, n, dims), "first_forward", 1, inputs, outputs, scratch)
@@ -2006,7 +2047,7 @@
 
         zero = jnp.zeros((1, C), F32)
         dg, db = lax.fori_loop(0, self.cells // 16, body, (zero, zero))
-        R.buf[rnd, 0] = pack([group_totals(R.pick, R.tmp_a[...]), group_totals(R.pick, R.tmp_b[...])])
+        R.buf[rnd, 0] = fold(pack([group_totals(R.pick, R.tmp_a[...]), group_totals(R.pick, R.tmp_b[...])]))
         copies = spread_copies(self.n, R.buf, R.send, R.recv, rnd)
         for cp in copies:
             cp.start()
@@ -2017,7 +2058,7 @@
         R = self.R
         for cp in copies:
             cp.wait_recv()
-        gathered = jnp.sum(R.buf[rnd], axis=0) / R.div[...]
+        gathered = unfold(jnp.sum(R.buf[rnd], axis=0)) / R.div[...]
         R.tmp_a[...] = split_dot(R.spread[...], unpack(gathered))
         R.tmp_b[...] = split_dot(R.spread[...], unpack(shift_down(gathered, 1)))
 
@@ -2130,6 +2171,7 @@
     greet_all(g)
     vec = R.vec
     back = Backer(n, dims, R)
+    R.need("du", "hid")
     copies, dg3, db3 = back.norm_sums(lambda i, unit: R.du[back.pixels(i), :], R.hid, R.mean3, R.inv3, vec[6:7, :], 0)
 
     def emit_hidden(i, value):
@@ -2138,11 +2180,13 @@
         R.dh[at, :] = total
         R.grad[at, :] = total.astype(B16)
 
+    R.need("cot", "col_l", "col_r", "row_u", "row_d")
     back.norm_finish(copies, 0, R.inv3, emit_hidden)
+    R.store("dh")
     up, down = back.send_rows(R.grad, 0)
     plane = dims[1] * dims[2]
     o_back = remote(R.o.at[pl.ds(plane, plane)], R.o_back, R.lsem.at[2], R.lsem.at[3],
-                    {"canvas": g.c, "height": lax.rem(g.h + n // 2, n)})
+                    {CANVAS: g.c, HEIGHT: lax.rem(g.h + n // 2, n)})
     o_back.start()
     back.mask_rows(R.grad)
     load_s.wait()
@@ -2152,6 +2196,7 @@
 
     back.weight_grad(R.s, R.grad, dest_two)
     load_att.wait()
+    R.store("g_top", 9 * C, 2 * C)
     load_s = pltpu.make_async_copy(R.s1, R.s, R.lsem.at[0])
     load_s.start()
     engine = Engine(reduce_pieces(group, R.g_low, R.sum_low, *R.reduce))
@@ -2166,6 +2211,7 @@
     def grad_two(i, unit):
         return R.part[back.pixels(i), :] * silu_slope(unit * gain2 + bias2)
 
+    R.need("y1")
     copies, dg2, db2 = back.norm_sums(grad_two, R.y1, R.mean2, R.inv2, gain2, 1)
     engine.pump(2)
 
@@ -2173,11 +2219,19 @@
         R.grad[back.pixels(i), :] = value.astype(B16)
 
     back.norm_finish(copies, 1, R.inv2, emit_grad)
+    R.store("grad")
     engine.pump(2)
     back.mask_rows(R.grad)
     dc1 = jnp.sum(R.grad[...].astype(F32), axis=0, keepdims=True)
     load_s.wait()
-    back.weight_grad(R.s, R.grad, lambda tap: (R.g_top, tap * C), engine.pump)
+    taps = []
+
+    def after_tap():
+        R.store("g_top", len(taps) * C, C)
+        taps.append(None)
+        engine.pump()
+
+    back.weight_grad(R.s, R.grad, lambda tap: (R.g_top, tap * C), after_tap)
     R.dvec[...] = jnp.concatenate([dc1, dg2, db2, dc2, dg3, db3, jnp.zeros((2, C), F32)], axis=0)
     engine.ready()
     engine.finish()
@@ -2194,19 +2248,19 @@
     stats = canvases * CROPS
     dma = pltpu.SemaphoreType.DMA
     names = ("mean2", "inv2", "mean3", "inv3")
-    inputs = dict(cot=(cot, vmem), du=(du, vmem), hid=(hid, vmem), y1=(y1, vmem), s1=(s1, anyw), s2=(s2, anyw),
+    inputs = dict(du=(du, LOAD), hid=(hid, LOAD), cot=(cot, LOAD),
+                  **{k: (v, LOAD) for k, v in zip(("col_l", "col_r", "row_u", "row_d"), masks)}, y1=(y1, LOAD), s1=(s1, anyw), s2=(s2, anyw),
                   pick=(pick, vmem), spread=(spread, vmem), div=(div, vmem), vec=(vec, vmem), top=(top, anyw),
                   bottom=(bottom, anyw), datt=(datt, anyw), o=(o, anyw),
-                  **{k: (v, vmem) for k, v in zip(names, norms)},
-                  **{k: (v, vmem) for k, v in zip(("col_l", "col_r", "row_u", "row_d"), masks)})
-    outputs = dict(dh=((px, C), F32, vmem), grad=((px, C), B16, vmem), g_top=((11 * C, C), B16, vmem),
+                  **{k: (v, vmem) for k, v in zip(names, norms)})
+    outputs = dict(dh=((px, C), F32, STORE), grad=((px, C), B16, STORE), g_top=((11 * C, C), B16, STORE),
                    dvec=((8, C), F32, vmem), sum_low=((block_rows // 2, C), B16, vmem),
                    o_back=((px // canvases, C), B16, anyw))
     scratch = dict(
         g_low=pltpu.VMEM((11 * C, C), B16), s=pltpu.VMEM(s1.shape, B16), k=pltpu.VMEM((9 * C, C), B16),
         d3=pltpu.VMEM(s1.shape, B16), low_u=pltpu.VMEM((px, C), B16), low_d=pltpu.VMEM((px, C), B16),
         part=pltpu.VMEM((px, C), F32), norm=pltpu.VMEM((px, C), F32),
-        halo=pltpu.VMEM((1, 2, canvases, width, C), B16), buf=pltpu.VMEM((2, n, stats, LANES), F32),
+        halo=pltpu.VMEM((1, 2, canvases, width, C), B16), buf=pltpu.VMEM((2, n, stats // 2, LANES), F32),
         tmp_a=pltpu.VMEM((cells, C), F32), tmp_b=pltpu.VMEM((cells, C), F32),
         reduce=reduce_pieces_scratch(columns, n, block_rows // 2),
         lsem=dma((5,)), ksem=dma((3,)),
@@ -2242,8 +2296,10 @@
     reducer = Engine(reduce_pieces(upper, R.g_top, R.sum_top, *R.reduce))
     reducer.pump()
     back = Backer(n, dims, R)
+    R.need("grad", "col_l", "col_r", "row_u", "row_d")
     up, down = back.send_rows(R.grad, 0)
     reducer.pump(2)
+    R.need("x")
     for cp in loads:
         cp.wait()
 
@@ -2273,7 +2329,7 @@
     R.vbuf[g.h] = jnp.concatenate([dg1, db1, R.dvec[0:6, :], R.dvec_att[...]], axis=0)
     vector_sends = [
         remote(R.vbuf.at[g.h], R.vbuf.at[g.h], R.vsend.at[d], R.vrecv.at[g.h],
-               {"canvas": g.c, "height": lax.rem(g.h + d, n)})
+               {CANVAS: g.c, HEIGHT: lax.rem(g.h + d, n)})
         for d in range(1, n)
     ]
     for cp in vector_sends:
@@ -2296,11 +2352,12 @@
         R.igrad[at, :] = R.igrad[at, :] + value
 
     back.norm_finish(copies, 0, R.inv1, emit_input)
+    R.store("igrad")
     gather_top.pump()
     for d in range(1, n):
         src = lax.rem(g.h + d, n)
         remote(R.vbuf.at[src], R.vbuf.at[src], R.vsend.at[d], R.vrecv.at[src],
-               {"canvas": g.c, "height": src}).wait_recv()
+               {CANVAS: g.c, HEIGHT: src}).wait_recv()
     R.vtrade[0, 0] = jnp.sum(R.vbuf[...], axis=0)
 
     def trade(k):
@@ -2321,7 +2378,7 @@
     R.new_vec[0:count, :] = R.new_vw[...].astype(B16).astype(F32)
     new_vec, s1, y1 = R.new_vec, R.d3, R.part
     conv = Convolver(n, dims, R.x, R.pick, R.spread, R.cnt, R.col_l, R.col_r, R.row_u, R.row_d, R.chalo, R.cbuf,
-                     R.tmp_a, R.tmp_b, R.csend, R.crecv, R.chsend, R.chrecv)
+                     R.tmp_a, R.tmp_b, R.csend, R.crecv, R.chsend, R.chrecv, R.cnt_all)
     conv.activate(R.x, R.mean1, R.inv1, new_vec[0:1, :], new_vec[1:2, :], s1, 0, gather_top.pump)
     gather_top.ready()
     pump = gather_low.pump
@@ -2341,9 +2398,12 @@
         R.hid[at, :] = total + new_vec[5:6, :] + R.x[at, :].astype(F32)
 
     conv.convolve(R.s2, across(R.new_top, R.new_low), emit_second)
-    conv.statistics(R.hid, R.mean2, R.inv2, 1)
+    R.store("hid")
     upper.block_arrived(R.sum_top, R.totals.at[0], R.asend.at[0], R.arecv.at[0])
     adam(upper, R.totals.at[0])
+    for k in ("new_w", "new_m", "new_s"):
+        R.store(k)
+    conv.statistics(R.hid, R.mean2, R.inv2, 1)
     conv.normalise(R.hid, R.mean2, R.inv2, new_vec[6:7, :], new_vec[7:8, :], R.u)
     for engine in (gather_low, gather_top, reducer):
         engine.finish()
@@ -2357,7 +2417,7 @@
     out_att.wait()
 
 
-def renew_call(columns, n, dims, grad, dh, x, mean1, inv1, pick, spread, div, cnt, masks, vec, top, g_top, sum_low,
+def renew_call(columns, n, dims, grad, dh, x, mean1, inv1, pick, spread, div, cnt, cnt_all, masks, vec, top, g_top, sum_low,
                dvec, dvec_att, w, m, v, shares, vw, vm, vs):
     canvases, rows, width = dims
     px = canvases * rows * width
@@ -2368,14 +2428,15 @@
     seats, phases = n // 2, columns.bit_length() - 1
     dma = pltpu.SemaphoreType.DMA
     tall = (canvases, rows + 2, width, 3 * C)
-    arrays = dict(grad=grad, x=x, mean1=mean1, inv1=inv1, pick=pick, spread=spread, div=div, cnt=cnt, vec=vec,
+    arrays = dict(mean1=mean1, inv1=inv1, pick=pick, spread=spread, div=div, cnt=cnt, cnt_all=cnt_all, vec=vec,
                   sum_low=sum_low, dvec=dvec, dvec_att=dvec_att, vw=vw, vm=vm, vs=vs)
-    inputs = dict(top=(top, anyw), g_in=(g_top, anyw), w=(w, anyw), m=(m, anyw), v=(v, anyw), shares=(shares, anyw), dh=(dh, anyw),
-                  **{k: (a, vmem) for k, a in arrays.items()},
-                  **{k: (a, vmem) for k, a in zip(("col_l", "col_r", "row_u", "row_d"), masks)})
-    outputs = dict(igrad=((px, C), F32, vmem), new_w=(block, F32, vmem), new_m=(block, F32, vmem),
-                   new_s=(block, F32, vmem), new_vw=(vw.shape, F32, vmem), new_vm=(vw.shape, F32, vmem),
-                   new_vs=(vw.shape, F32, vmem), new_vec=((16, C), F32, vmem), hid=((px, C), F32, vmem),
+    inputs = dict(grad=(grad, LOAD),
+                  **{k: (a, LOAD) for k, a in zip(("col_l", "col_r", "row_u", "row_d"), masks)}, x=(x, LOAD),
+                  top=(top, anyw), g_in=(g_top, anyw), w=(w, anyw), m=(m, anyw), v=(v, anyw), shares=(shares, anyw), dh=(dh, anyw),
+                  **{k: (a, vmem) for k, a in arrays.items()})
+    outputs = dict(igrad=((px, C), F32, STORE), new_w=(block, F32, STORE), new_m=(block, F32, STORE),
+                   new_s=(block, F32, STORE), new_vw=(vw.shape, F32, vmem), new_vm=(vw.shape, F32, vmem),
+                   new_vs=(vw.shape, F32, vmem), new_vec=((16, C), F32, vmem), hid=((px, C), F32, STORE),
                    u=((px, C), B16, vmem), new_att=((4 * C, C), B16, anyw))
     scratch = dict(
         g_top=pltpu.VMEM((11 * C, C), B16), sum_top=pltpu.VMEM((half, C), B16), totals=pltpu.VMEM((2,) + block, B16),
@@ -2384,7 +2445,7 @@
         d3=pltpu.VMEM(tall, B16), s2=pltpu.VMEM(tall, B16), part=pltpu.VMEM((px, C), F32),
         norm=pltpu.VMEM((px, C), F32), mean2=pltpu.VMEM((cells, C), F32), inv2=pltpu.VMEM((cells, C), F32),
         halo=pltpu.VMEM((1, 2, canvases, width, C), B16), chalo=pltpu.VMEM((2, 2, canvases, width, C), B16),
-        buf=pltpu.VMEM((1, n, stats, LANES), F32), cbuf=pltpu.VMEM((2, n, stats, LANES), F32),
+        buf=pltpu.VMEM((1, n, stats // 2, LANES), F32), cbuf=pltpu.VMEM((2, n, stats // 2, LANES), F32),
         tmp_a=pltpu.VMEM((cells, C), F32), tmp_b=pltpu.VMEM((cells, C), F32),
         vbuf=pltpu.VMEM((n, 16, C), F32), vtrade=pltpu.VMEM((phases + 1, 2, 16, C), F32),
         reduce=reduce_pieces_scratch(columns, n, half), gather0=gather_pieces_scratch(columns, n),
@@ -2397,7 +2458,7 @@
 
 
 def attend_kernel(n, keep, R):
-    me = lax.axis_index("height")
+    me = lax.axis_index(HEIGHT)
     half = n // 2
     mine = me // half
     base = mine * half
@@ -2420,7 +2481,7 @@
         return lax.rem(b + half, n)
 
     def to(h):
-        return {"canvas": lax.axis_index("canvas"), "height": h}
+        return {CANVAS: lax.axis_index(CANVAS), HEIGHT: h}
 
     loads = [pltpu.make_async_copy(R.low.at[pl.ds(R.low.shape[0] - 4 * C, 4 * C)], R.w, R.lsem.at[0])]
     if keep:
@@ -2431,9 +2492,9 @@
     own.start()
     barrier = pltpu.get_barrier_semaphore()
     peers = [to(p) for p in [partner, sibling] + [mate(j) for j in range(1, mates)]]
-    column = lax.axis_index("canvas")
+    column = lax.axis_index(CANVAS)
     if keep:
-        peers += [{"canvas": lax.rem(column + d, 4), "height": me} for d in range(1, 4)]
+        peers += [{CANVAS: lax.rem(column + d, 4), HEIGHT: me} for d in range(1, 4)]
     for p in peers:
         pl.semaphore_signal(barrier, inc=1, device_id=p, device_id_type=MESH)
     pl.semaphore_wait(barrier, len(peers))
@@ -2443,7 +2504,7 @@
         rows = R.shares.shape[1]
         for i, src in enumerate((R.params, R.first, R.second)):
             cp = remote(src.at[pl.ds(half_number * rows, rows)], R.shares.at[i], R.wsend.at[half_number, i],
-                        R.wrecv.at[i], {"canvas": to_column, "height": me})
+                        R.wrecv.at[i], {CANVAS: to_column, HEIGHT: me})
             if begin:
                 pl.when(column == from_column)(cp.start)
             else:
@@ -2660,6 +2721,7 @@
     dwq = lax.dot_general(R.u[partner], R.dq[far_rows, :], tn, preferred_element_type=F32)
     dwq = dwq + lax.dot_general(R.u[me], R.dq[own_rows, :], tn, preferred_element_type=F32)
     R.dw[0:C, :] = dwq.astype(B16)
+    R.store("dw")
     R.dvec[...] = jnp.concatenate(
         [
             jnp.sum(R.dq[...].astype(F32), axis=0, keepdims=True),
@@ -2710,7 +2772,7 @@
         lsem=dma((4,)), gsend=dma((4 * mates,)), grecv=dma((n,)))
     if keep:
         inputs.update(cot=(cot, anyw), **{k: (a, anyw) for k, a in zip(("params", "first", "second"), state)})
-        outputs = dict(o_home=((2 * seg, C), B16, anyw), dw=((4 * C, C), B16, vmem), dvec=((8, C), F32, vmem),
+        outputs = dict(o_home=((2 * seg, C), B16, anyw), dw=((4 * C, C), B16, STORE), dvec=((8, C), F32, vmem),
                        du=(home, F32, vmem), shares=((3, state[0].shape[0] // 2, C), F32, anyw))
         scratch.update(
             csend=dma((seg // rows,)), crecv=dma((seg // rows,)), dz=pltpu.VMEM((2 * seg, C), B16), dout=pltpu.VMEM((2 * seg, C), B16), q=pltpu.VMEM((2 * seg, C), B16),
@@ -2732,45 +2794,53 @@
 
 
 def outputs_kernel(n, R):
-    mine = lax.axis_index("height") // (n // 2)
+    mine = lax.axis_index(HEIGHT) // (n // 2)
     seg = R.o_back.shape[0]
     own, other = (pl.ds(pl.multiple_of(i * seg, seg), seg) for i in (mine, 1 - mine))
     loads = [
         pltpu.make_async_copy(R.low.at[pl.ds(R.low.shape[0] - C, C)], R.w.at[0], R.sem.at[0]),
-        pltpu.make_async_copy(R.new_low.at[pl.ds(R.new_low.shape[0] - C, C)], R.w.at[1], R.sem.at[1]),
-        pltpu.make_async_copy(R.hid, R.hid_in, R.sem.at[2]),
-        pltpu.make_async_copy(R.hid2, R.hid2_in, R.sem.at[3]),
-        pltpu.make_async_copy(R.o.at[pl.ds(0, seg)], R.o_in.at[0, own], R.sem.at[4]),
-        pltpu.make_async_copy(R.o_back, R.o_in.at[0, other], R.sem.at[5]),
-        pltpu.make_async_copy(R.o2, R.o_in.at[1], R.sem.at[6]),
-        pltpu.make_async_copy(R.igrad, R.igrad_in, R.sem.at[7]),
+        pltpu.make_async_copy(R.o.at[pl.ds(0, seg)], R.o_in.at[0, own], R.sem.at[1]),
+        pltpu.make_async_copy(R.o_back, R.o_in.at[0, other], R.sem.at[2]),
+        pltpu.make_async_copy(R.new_low.at[pl.ds(R.new_low.shape[0] - C, C)], R.w.at[1], R.sem.at[3]),
+        pltpu.make_async_copy(R.o2, R.o_in.at[1], R.sem.at[4]),
     ]
     for cp in loads:
         cp.start()
-    for cp in loads:
+    count = R.part.shape[2]
+    parts = R.hid.shape[0] // count
+    bases = {}
+    for which, src in enumerate((R.hid, R.hid2, R.igrad)):
+        for i in range(parts):
+            at = pl.ds(i * count, count)
+            bases[which, i] = pltpu.make_async_copy(src.at[at], R.held.at[which, at], R.hsem.at[which, i])
+            bases[which, i].start()
+    ends = []
+
+    def out(src, dst, sem):
+        cp = pltpu.make_async_copy(src, dst, sem)
+        cp.start()
+        ends.append(cp)
+
+    for cp in loads[:3]:
         cp.wait()
-    backs = [
-        pltpu.make_async_copy(R.hid_in, R.hid_out, R.sem.at[2]),
-        pltpu.make_async_copy(R.igrad_in, R.igrad_out, R.sem.at[7]),
-    ]
-    for cp in backs:
-        cp.start()
-    count = R.part.shape[1]
-    parts = R.hid.shape[0] // count
-    last = {}
-    for i in range(2 * parts):
-        which, at = i // parts, pl.ds((i % parts) * count, count)
-        base = (R.hid_in, R.hid2_in)[which]
-        vec = (R.vec, R.new_vec)[which]
-        slot = i % 2
-        if slot in last:
-            last[slot].wait()
-        R.part[slot] = (
-            base[at, :] + jnp.dot(R.o_in[which, at, :], R.w[which], preferred_element_type=F32) + vec[10:11, :])
-        cp = pltpu.make_async_copy(R.part.at[slot], (R.first, R.second)[which].at[at], R.sem.at[8 + slot])
-        cp.start()
-        last[slot] = cp
-    for cp in backs + list(last.values()):
+    for which, (vec, dst) in enumerate(((R.vec, R.first), (R.new_vec, R.second))):
+        if which == 1:
+            for cp in loads[3:]:
+                cp.wait()
+        for i in range(parts):
+            at = pl.ds(i * count, count)
+            bases[which, i].wait()
+            if which == 0:
+                out(R.held.at[0, at], R.hid_out.at[at], R.osem.at[0, i])
+            R.part[which, i] = (
+                R.held[which, at, :]
+                + jnp.dot(R.o_in[which, at, :], R.w[which], preferred_element_type=F32) + vec[10:11, :])
+            out(R.part.at[which, i], dst.at[at], R.osem.at[1 + which, i])
+    for i in range(parts):
+        at = pl.ds(i * count, count)
+        bases[2, i].wait()
+        out(R.held.at[2, at], R.igrad_out.at[at], R.osem.at[3, i])
+    for cp in ends:
         cp.wait()
 
 
@@ -2781,10 +2851,12 @@
                   vec=(vec, vmem), new_vec=(new_vec, vmem), low=(low, anyw), new_low=(new_low, anyw))
     whole = ((px, C), F32, anyw)
     outputs = dict(hid_out=whole, first=whole, second=whole, igrad_out=whole)
+    count = min(256, px)
+    parts = px // count
+    dma = pltpu.SemaphoreType.DMA
     scratch = dict(
-        w=pltpu.VMEM((2, C, C), B16), hid_in=pltpu.VMEM((px, C), F32), hid2_in=pltpu.VMEM((px, C), F32),
-        igrad_in=pltpu.VMEM((px, C), F32), o_in=pltpu.VMEM((2, px, C), B16), part=pltpu.VMEM((2, min(256, px), C), F32),
-        sem=pltpu.SemaphoreType.DMA((10,)))
+        w=pltpu.VMEM((2, C, C), B16), held=pltpu.VMEM((3, px, C), F32), o_in=pltpu.VMEM((2, px, C), B16),
+        part=pltpu.VMEM((2, parts, count, C), F32), sem=dma((5,)), hsem=dma((3, parts)), osem=dma((4, parts)))
     return named_call(functools.partial(outputs_kernel, n), "outputs", None, inputs, outputs, scratch)
 
 
@@ -2799,7 +2871,7 @@
     px = canvases * rows * width
     plane = rows * width
     half = n // 2
-    me = lax.axis_index("height")
+    me = lax.axis_index(HEIGHT)
     mine = me // half
     partner = lax.rem(me + half, n)
     swap = [(i, (i + half) % n) for i in range(n)]
@@ -2825,8 +2897,8 @@
         du = att["du"].reshape(px, channels)
         back = back_call(columns, n, dims, cot, du, hid, y1, norms, s1, s2, pick, spread, div, masks, vec, top, low,
                          att["dw"], att["o_home"], params.shape[0])
-        new = renew_call(columns, n, dims, back["grad"], back["dh"], x, mean1, inv1, pick, spread, div, cnt, masks, vec,
-                         top, back["g_top"], back["sum_low"], back["dvec"], att["dvec"], params, first_moment,
+        new = renew_call(columns, n, dims, back["grad"], back["dh"], x, mean1, inv1, pick, spread, div, cnt, first["cnt_all"],
+                         masks, vec, top, back["g_top"], back["sum_low"], back["dvec"], att["dvec"], params, first_moment,
                          second_moment, att["shares"], vectors, vector_first, vector_second)
         new_vec, new_att = new["new_vec"], new["new_att"]
         o2 = attend_call(n, False, 5, new["u"].reshape(canvases, plane, channels), ids_all, new_vec, new_att)["o_home"]
@@ -2855,7 +2927,7 @@
         n, dims, True, x, pick, spread, cnt, mean1, inv1, masks, vec, top, low)
     own_cot = lax.dynamic_index_in_dim(cot3, mine, axis=0, keepdims=False)
     far_cot = lax.ppermute(
-        lax.dynamic_index_in_dim(cot3, 1 - mine, axis=0, keepdims=False), "height", swap)
+        lax.dynamic_index_in_dim(cot3, 1 - mine, axis=0, keepdims=False), HEIGHT, swap)
     dz = jnp.concatenate([own_cot, far_cot], axis=0)
     canvas_ids = lax.dynamic_index_in_dim(ids_all, mine, axis=1, keepdims=False)
     key_ids = canvas_ids.reshape(1, n * plane)
@@ -2864,7 +2936,7 @@
     offsets = jnp.stack([me, partner]) * plane
 
     def attention_output(o, hid, low, bias):
-        back = lax.ppermute(o[plane:], "height", swap)
+        back = lax.ppermute(o[plane:], HEIGHT, swap)
         ordered = jnp.where(mine == 0, jnp.stack([o[:plane], back]), jnp.stack([back, o[:plane]]))
         product = jnp.dot(ordered.reshape(px, channels), low[10 * C :], preferred_element_type=F32)
         return hid + product + bias
@@ -2898,12 +2970,12 @@
 
 
 def solution(mesh):
-    spatial = P("canvas", "height", None, None)
-    owned = P(("canvas", "height"), None)
+    spatial = P(CANVAS, HEIGHT, None, None)
+    owned = P((CANVAS, HEIGHT), None)
     return jax.shard_map(
-        functools.partial(body, mesh.shape["canvas"], mesh.shape["height"]),
+        functools.partial(body, mesh.shape[CANVAS], mesh.shape[HEIGHT]),
         mesh=mesh,
-        in_specs=(spatial, P("canvas", "height", None), owned, P(), owned, owned, P(), P(), spatial),
+        in_specs=(spatial, P(CANVAS, HEIGHT, None), owned, P(), owned, owned, P(), P(), spatial),
         out_specs=(spatial, spatial, spatial, spatial, owned, owned, owned, P(), P(), P()),
         check_vma=False,
     )

time: 537 us -> 505 us (0.940)
  Pallas kernels: 524 us -> 492 us
    pallas_call x6, Pallas kernels: 524 us -> 492 us  [named_call(): pl.pallas_call(wrapped, out_shape=[sds(shape, kind) for shape, kind, _ in...]
where the time goes in v4:
time: 505 us; the launch traced here: 499 us
  Pallas kernels  492 us (97%)
  local copies, waits for them, and re-layouts  5.14 us (1%)
    pallas_call x6, Pallas kernels, named_call(): pl.pallas_call(wrapped, out_shape=[sds(shape, kind) for shape, kind, _ in...  492 us

profile of v4, /device:TPU:0, one launch (start us, length us, event | category | flops | bytes accessed | tf_op | source)
XLA Modules:
  0.0 498.9 jit_solution(8705089078152882126)
XLA Ops:
  0.6 0.7 convert_element_type.5
  1.3 0.1 reshape.57
  1.4 0.6 pad.4.refs_1_
  2.0 98.5 %first_forward.1 = (f32[16,512]{1,0:T(8,128)}, bf16[32,128]{1,0:T(8,128)(2,1)}, bf16[128,32]{1,0:T(8,128)(2,1)}, f32[8,8,512]{2,1,0:T(8,128)}, f32[128,512]{1,0:...) custom-call(bf16[1024,512]{1,0:T(8,128)(2,1)} %bitcast.13, ...), custom_call_target="tpu_custom_call" | custom-call | tf_op jit(solution)/shard_map/first_forward/pallas_call | solution.py:1862
  100.6 115.6 %attend.1 = (bf16[1024,512]{1,0:T(8,128)(2,1)}, bf16[2048,512]{1,0:T(8,128)(2,1)}, f32[8,512]{1,0:T(8,128)}, f32[2,512,512]{2,1,0:T(8,128)}, f32[3,176,512]{2,1,0:T(8,128)}) custom-call(bf16[2,512,512]{2,1,0:T(8,128)(2,1)} %bitcast.17, f32[8,8,512]{2,1,0:T(8,128)} %get-tuple-element.62.refs_1_, ...), custom_call_target="tpu_custom_call" | custom-call | tf_op jit(solution)/shard_map/attend/pallas_call | solution.py:1862
  216.2 66.5 %back.1 = (f32[1024,512]{1,0:T(8,128)}, bf16[1024,512]{1,0:T(8,128)(2,1)}, bf16[5632,512]{1,0:T(8,128)(2,1)}, f32[8,512]{1,0:T(8,128)}, bf16[176,512]{1,0:T(8,128)(2,1)}, /*index=5*/bf16[512,512]{1,0:T(8,128)(2,1)}) custom-call(f32[1024,512]{1,0:T(8,128)} %bitcast.16, f32[1024,512]{1,0:T(8,128)} %get-tuple-element.60.refs_1_.refs_0_, ...), custom_call_target="tpu_custom_call" | custom-call | tf_op jit(solution)/shard_map/back/pallas_call | solution.py:1862
  282.7 133.4 %renew.1 = (f32[1024,512]{1,0:T(8,128)}, f32[352,512]{1,0:T(8,128)}, f32[352,512]{1,0:T(8,128)}, f32[352,512]{1,0:T(8,128)}, f32[11,512]{1,0:T(8,128)}, /*index=...) custom-call(bf16[1024,512]{1,0:T(8,128)(2,1)} %get-tuple-element.83., ...), custom_call_target="tpu_custom_call" | custom-call | tf_op jit(solution)/shard_map/renew/pallas_call | solution.py:1862
  416.1 69.8 %attend_again.1 = bf16[2,512,512]{2,1,0:T(8,128)(2,1)} custom-call(bf16[2,512,512]{2,1,0:T(8,128)(2,1)} %bitcast.18, f32[8,8,512]{2,1,0:T(8,128)} %get-tuple-element.62.refs_1_, f32[16,512]{1,0:T(8,128)} %get-tuple-element.97.refs_2_.refs_7_, bf16[2048,512]{1,0:T(8,128)(2,1)} %get-tuple-element.98.refs_3_.refs_9_), custom_call_target="tpu_custom_call" | custom-call | tf_op jit(solution)/shard_map/attend_again/pallas_call | solution.py:1862
  486.0 0.0 copy-start.2
  486.0 0.0 copy-start.1
  486.0 8.2 %outputs.1 = (f32[1024,512]{1,0:T(8,128)}, f32[1024,512]{1,0:T(8,128)}, f32[1024,512]{1,0:T(8,128)}, f32[1024,512]{1,0:T(8,128)}) custom-call(f32[1024,512]{1,0:T(8,128)} %get-tuple-element.60.refs_1_.refs_0_, f32[1024,512]{1,0:T(8,128)} %get-tuple-element.94.refs_1_, bf16[1024,512]{1,0:T(8,128)(2,1)} %get-tuple-element.78.refs_17_.refs_2_, ...), custom_call_target="tpu_custom_call" | custom-call | tf_op jit(solution)/shard_map/outputs/pallas_call | solution.py:1862
  494.2 0.0 copy-start
  494.3 0.0 copy-done.2
  494.3 0.0 copy-start.5
  494.3 0.0 copy-start.4
  494.3 0.0 copy-start.3
  494.3 0.9 copy.25
  495.2 0.0 copy-done.1
  495.2 0.9 copy.26
  496.0 0.0 copy-done
  496.0 0.9 copy.27
  496.9 0.0 copy-done.5
  496.9 0.6 copy.28
  497.5 0.0 copy-done.4
  497.5 0.6 copy.29
  498.1 0.0 copy-done.3
  498.1 0.6 copy.30
Async XLA Ops:
  486.0 8.3 %copy-start.2 = (f32[352,512]{1,0:T(8,128)S(1)}, f32[352,512]{1,0:T(8,128)}, u32[]{:S(2)}) copy-start(f32[352,512]{1,0:T(8,128)} %get-tuple-element.124) | copy-start | bytes 2162692
  486.0 9.2 %copy-start.1 = (f32[352,512]{1,0:T(8,128)S(1)}, f32[352,512]{1,0:T(8,128)}, u32[]{:S(2)}) copy-start(f32[352,512]{1,0:T(8,128)} %get-tuple-element.125) | copy-start | bytes 2162692
  494.2 1.8 copy-start
  494.3 2.6 copy-start.5
  494.3 3.2 copy-start.4
  494.3 3.8 copy-start.3

commit v5 on v4

--- a/solution.py
+++ b/solution.py
@@ -1693,6 +1693,99 @@
     ]
 
 
+def fold_columns(group, src, column, sib, got, gsend, grecv, psend, precv):
+    g = group.g
+    seats, phases = g.seats, g.phases
+    slots = 2**phases
+    turns = [i // 2 if i % 2 == 0 else seats - 1 - i // 2 for i in range(seats)]
+    order = sorted(range(slots), key=lambda e: (lowest_bit(e) if e else phases, e == (e & -e)))
+
+    def mine(e, seat):
+        return group.rows(g.column(e), seat, g.core)
+
+    def sibling_copy(e, seat):
+        return remote(src.at[group.rows(g.column(e, g.other_flips), seat, 1 - g.core)], sib.at[e, seat],
+                      gsend.at[e, seat], grecv.at[e, seat], g.sibling())
+
+    def phase_copy(k, e, seat):
+        at = (k, e >> (k + 1), seat)
+        return remote(src.at[mine(e, seat), :], got.at[at], psend.at[at], precv.at[at], g.mate(k))
+
+    for e in order:
+        for seat in turns:
+            sibling_copy(e, seat).start()
+    yield
+    for e in order:
+        k = lowest_bit(e) if e else phases
+        for seat in turns:
+            sibling_copy(e, seat).wait_recv()
+            total = src[mine(e, seat), :].astype(F32) + sib[e, seat].astype(F32)
+            for q in range(k):
+                phase_copy(q, e | (1 << q), seat).wait_recv()
+                total = total + got[q, e >> (q + 1), seat].astype(F32)
+            if e:
+                src[mine(e, seat), :] = total.astype(B16)
+                phase_copy(k, e, seat).start()
+            else:
+                column[seat] = total.astype(B16)
+            yield
+    yield True
+
+    def drain(seat, _):
+        for e in range(slots):
+            sibling_copy(e, seat).wait_send()
+            if e:
+                phase_copy(lowest_bit(e), e, seat).wait_send()
+        return 0
+
+    lax.fori_loop(0, seats, drain, 0)
+
+
+def fold_columns_scratch(columns, n, half_rows):
+    seats, phases = n // 2, columns.bit_length() - 1
+    dma = pltpu.SemaphoreType.DMA
+    block = (half_rows, C)
+    return [
+        pltpu.VMEM((columns, seats) + block, B16),
+        pltpu.VMEM((phases, columns // 2, seats) + block, B16),
+        dma((columns, seats)),
+        dma((columns, seats)),
+        dma((phases, columns // 2, seats)),
+        dma((phases, columns // 2, seats)),
+    ]
+
+
+def fold_seats(group, column, piece, box, usend, urecv):
+    g = group.g
+    seats = g.seats
+
+    def line_copy(seat):
+        return remote(column.at[seat], box.at[g.seat], usend.at[seat], urecv.at[g.seat],
+                      {CANVAS: g.c, HEIGHT: 2 * seat + g.core})
+
+    def line_arrival(seat):
+        return remote(column.at[seat], box.at[seat], usend.at[seat], urecv.at[seat],
+                      {CANVAS: g.c, HEIGHT: 2 * seat + g.core})
+
+    for seat in range(seats):
+        pl.when(seat != g.seat)(line_copy(seat).start)
+    yield
+    total = column[g.seat].astype(F32)
+    for seat in range(seats):
+        pl.when(seat != g.seat)(line_arrival(seat).wait_recv)
+        total = total + jnp.where(seat == g.seat, 0.0, box[seat].astype(F32))
+    piece[...] = total.astype(B16)
+    yield True
+    for seat in range(seats):
+        pl.when(seat != g.seat)(line_copy(seat).wait_send)
+
+
+def fold_seats_scratch(n, half_rows):
+    seats = n // 2
+    dma = pltpu.SemaphoreType.DMA
+    return [pltpu.VMEM((seats, half_rows, C), B16), dma((seats,)), dma((seats,))]
+
+
 def reduce_pieces(group, src, piece, sib, got, box, gsend, grecv, psend, precv, usend, urecv):
     g = group.g
     seats, phases = g.seats, g.phases
@@ -2160,8 +2253,7 @@
 
 def back_kernel(columns, n, dims, R):
     g = Grid(columns, n)
-    half = R.sum_low.shape[0]
-    group = Group(g, 1, half)
+    group = Group(g, 1, R.halves.shape[1])
     load_s = pltpu.make_async_copy(R.s2, R.s, R.lsem.at[0])
     load_s.start()
     load_k = second_matrix(R.top, R.bottom, R.k, R.ksem)
@@ -2199,7 +2291,7 @@
     R.store("g_top", 9 * C, 2 * C)
     load_s = pltpu.make_async_copy(R.s1, R.s, R.lsem.at[0])
     load_s.start()
-    engine = Engine(reduce_pieces(group, R.g_low, R.sum_low, *R.reduce))
+    engine = Engine(fold_columns(group, R.g_low, R.halves, *R.reduce))
     engine.pump()
     dc2 = jnp.sum(R.grad[...].astype(F32), axis=0, keepdims=True)
     back.finish_rows(up, down, 0)
@@ -2254,7 +2346,7 @@
                   bottom=(bottom, anyw), datt=(datt, anyw), o=(o, anyw),
                   **{k: (v, vmem) for k, v in zip(names, norms)})
     outputs = dict(dh=((px, C), F32, STORE), grad=((px, C), B16, STORE), g_top=((11 * C, C), B16, STORE),
-                   dvec=((8, C), F32, vmem), sum_low=((block_rows // 2, C), B16, vmem),
+                   dvec=((8, C), F32, vmem), halves=((n // 2, block_rows // 2, C), B16, STORE),
                    o_back=((px // canvases, C), B16, anyw))
     scratch = dict(
         g_low=pltpu.VMEM((11 * C, C), B16), s=pltpu.VMEM(s1.shape, B16), k=pltpu.VMEM((9 * C, C), B16),
@@ -2262,7 +2354,7 @@
         part=pltpu.VMEM((px, C), F32), norm=pltpu.VMEM((px, C), F32),
         halo=pltpu.VMEM((1, 2, canvases, width, C), B16), buf=pltpu.VMEM((2, n, stats // 2, LANES), F32),
         tmp_a=pltpu.VMEM((cells, C), F32), tmp_b=pltpu.VMEM((cells, C), F32),
-        reduce=reduce_pieces_scratch(columns, n, block_rows // 2),
+        reduce=fold_columns_scratch(columns, n, block_rows // 2),
         lsem=dma((5,)), ksem=dma((3,)),
         send=dma((2, n)), recv=dma((2, n)), hsend=dma((1, 2)), hrecv=dma((1, 2)))
     return named_call(functools.partial(back_kernel, columns, n, dims), "back", 7, inputs, outputs, scratch)
@@ -2291,13 +2383,15 @@
         piece_loads.append(there)
     greet_all(g)
     vec = R.vec
-    lower.to_owner(R.sum_low, R.totals.at[1], R.asend.at[1], R.arecv.at[1], True)
+    R.need("halves")
+    folder = Engine(fold_seats(lower, R.halves, R.sum_low, *R.fold))
     load_g.wait()
     reducer = Engine(reduce_pieces(upper, R.g_top, R.sum_top, *R.reduce))
     reducer.pump()
     back = Backer(n, dims, R)
     R.need("grad", "col_l", "col_r", "row_u", "row_d")
     up, down = back.send_rows(R.grad, 0)
+    folder.pump()
     reducer.pump(2)
     R.need("x")
     for cp in loads:
@@ -2312,13 +2406,19 @@
             R.new_w[...] = next_w
             R.fresh[...] = next_w.astype(B16)
 
-    lower.block_arrived(R.sum_low, R.totals.at[1], R.asend.at[1], R.arecv.at[1])
-    adam(lower, R.totals.at[1])
-    lower.to_pieces(R.fresh, R.pieces.at[1], R.tsend.at[1], R.trecv.at[1], True)
     reducer.pump(2)
     back.finish_rows(up, down, 0)
     load_k.wait()
-    back.convolve_back(lambda tap: (R.k, tap * C), reducer.pump)
+    turn = []
+
+    def pump_both():
+        reducer.pump()
+        turn.append(None)
+        if len(turn) == 4:
+            folder.ready()
+            lower.to_owner(R.sum_low, R.totals, R.asend.at[1], R.arecv.at[1], True)
+
+    back.convolve_back(lambda tap: (R.k, tap * C), pump_both)
     gain1, bias1 = vec[0:1, :], vec[1:2, :]
 
     def grad_one(i, unit):
@@ -2326,6 +2426,9 @@
 
     copies, dg1, db1 = back.norm_sums(grad_one, R.x, R.mean1, R.inv1, gain1, 0)
     reducer.pump(2)
+    lower.block_arrived(R.sum_low, R.totals, R.asend.at[1], R.arecv.at[1])
+    adam(lower, R.totals)
+    lower.to_pieces(R.fresh, R.pieces.at[1], R.tsend.at[1], R.trecv.at[1], True)
     R.vbuf[g.h] = jnp.concatenate([dg1, db1, R.dvec[0:6, :], R.dvec_att[...]], axis=0)
     vector_sends = [
         remote(R.vbuf.at[g.h], R.vbuf.at[g.h], R.vsend.at[d], R.vrecv.at[g.h],
@@ -2334,9 +2437,6 @@
     ]
     for cp in vector_sends:
         cp.start()
-    lower.piece_arrived(R.fresh, R.pieces.at[1], R.tsend.at[1], R.trecv.at[1])
-    gather_low = Engine(gather_pieces(lower, R.pieces.at[1], R.new_low, *R.gather1))
-    gather_low.pump()
     reducer.ready()
     for cp in piece_loads:
         cp.wait()
@@ -2345,7 +2445,10 @@
     R.pieces[0] = next_piece.astype(B16)
     gather_top = Engine(gather_pieces(upper, R.pieces.at[0], R.new_top, *R.gather0))
     gather_top.pump()
-    upper.to_owner(R.sum_top, R.totals.at[0], R.asend.at[0], R.arecv.at[0], True)
+    lower.piece_arrived(R.fresh, R.pieces.at[1], R.tsend.at[1], R.trecv.at[1])
+    gather_low = Engine(gather_pieces(lower, R.pieces.at[1], R.new_low, *R.gather1))
+    gather_low.pump()
+    upper.to_owner(R.sum_top, R.totals, R.asend.at[0], R.arecv.at[0], True)
 
     def emit_input(i, value):
         at = back.pixels(i)
@@ -2376,7 +2479,7 @@
         R.vw[...], R.vtrade[g.phases, 0][0:count, :], R.vm[...], R.vs[...], vector_rate)
     R.new_vec[...] = jnp.zeros(R.new_vec.shape, F32)
     R.new_vec[0:count, :] = R.new_vw[...].astype(B16).astype(F32)
-    new_vec, s1, y1 = R.new_vec, R.d3, R.part
+    new_vec, s1, y1, hid = R.new_vec, R.d3, R.part, R.norm
     conv = Convolver(n, dims, R.x, R.pick, R.spread, R.cnt, R.col_l, R.col_r, R.row_u, R.row_d, R.chalo, R.cbuf,
                      R.tmp_a, R.tmp_b, R.csend, R.crecv, R.chsend, R.chrecv, R.cnt_all)
     conv.activate(R.x, R.mean1, R.inv1, new_vec[0:1, :], new_vec[1:2, :], s1, 0, gather_top.pump)
@@ -2395,29 +2498,34 @@
     out_att.start()
 
     def emit_second(at, total):
-        R.hid[at, :] = total + new_vec[5:6, :] + R.x[at, :].astype(F32)
+        hid[at, :] = total + new_vec[5:6, :] + R.x[at, :].astype(F32)
 
     conv.convolve(R.s2, across(R.new_top, R.new_low), emit_second)
-    R.store("hid")
-    upper.block_arrived(R.sum_top, R.totals.at[0], R.asend.at[0], R.arecv.at[0])
-    adam(upper, R.totals.at[0])
-    for k in ("new_w", "new_m", "new_s"):
-        R.store(k)
-    conv.statistics(R.hid, R.mean2, R.inv2, 1)
-    conv.normalise(R.hid, R.mean2, R.inv2, new_vec[6:7, :], new_vec[7:8, :], R.u)
-    for engine in (gather_low, gather_top, reducer):
+    out_hid = pltpu.make_async_copy(hid, R.hid, R.ksem.at[1])
+    out_hid.start()
+
+    def update_owned():
+        upper.block_arrived(R.sum_top, R.totals, R.asend.at[0], R.arecv.at[0])
+        adam(upper, R.totals)
+        for k in ("new_w", "new_m", "new_s"):
+            R.store(k)
+
+    conv.statistics(hid, R.mean2, R.inv2, 1, update_owned)
+    conv.normalise(hid, R.mean2, R.inv2, new_vec[6:7, :], new_vec[7:8, :], R.u)
+    for engine in (gather_low, gather_top, reducer, folder):
         engine.finish()
     for cp in back.sent + conv.sent + vector_sends:
         cp.wait_send()
     for k in range(g.phases):
         trade(k).wait_send()
     for i, group in enumerate((upper, lower)):
-        group.to_owner((R.sum_top, R.sum_low)[i], R.totals.at[i], R.asend.at[i], R.arecv.at[i], False)
+        group.to_owner((R.sum_top, R.sum_low)[i], R.totals, R.asend.at[i], R.arecv.at[i], False)
     lower.to_pieces(R.fresh, R.pieces.at[1], R.tsend.at[1], R.trecv.at[1], False)
     out_att.wait()
-
-
-def renew_call(columns, n, dims, grad, dh, x, mean1, inv1, pick, spread, div, cnt, cnt_all, masks, vec, top, g_top, sum_low,
+    out_hid.wait()
+
+
+def renew_call(columns, n, dims, grad, dh, x, mean1, inv1, pick, spread, div, cnt, cnt_all, masks, vec, top, g_top, halves,
                dvec, dvec_att, w, m, v, shares, vw, vm, vs):
     canvases, rows, width = dims
     px = canvases * rows * width
@@ -2429,17 +2537,18 @@
     dma = pltpu.SemaphoreType.DMA
     tall = (canvases, rows + 2, width, 3 * C)
     arrays = dict(mean1=mean1, inv1=inv1, pick=pick, spread=spread, div=div, cnt=cnt, cnt_all=cnt_all, vec=vec,
-                  sum_low=sum_low, dvec=dvec, dvec_att=dvec_att, vw=vw, vm=vm, vs=vs)
-    inputs = dict(grad=(grad, LOAD),
+                  dvec=dvec, dvec_att=dvec_att, vw=vw, vm=vm, vs=vs)
+    inputs = dict(halves=(halves, LOAD), grad=(grad, LOAD),
                   **{k: (a, LOAD) for k, a in zip(("col_l", "col_r", "row_u", "row_d"), masks)}, x=(x, LOAD),
                   top=(top, anyw), g_in=(g_top, anyw), w=(w, anyw), m=(m, anyw), v=(v, anyw), shares=(shares, anyw), dh=(dh, anyw),
                   **{k: (a, vmem) for k, a in arrays.items()})
     outputs = dict(igrad=((px, C), F32, STORE), new_w=(block, F32, STORE), new_m=(block, F32, STORE),
                    new_s=(block, F32, STORE), new_vw=(vw.shape, F32, vmem), new_vm=(vw.shape, F32, vmem),
-                   new_vs=(vw.shape, F32, vmem), new_vec=((16, C), F32, vmem), hid=((px, C), F32, STORE),
+                   new_vs=(vw.shape, F32, vmem), new_vec=((16, C), F32, vmem), hid=((px, C), F32, anyw),
                    u=((px, C), B16, vmem), new_att=((4 * C, C), B16, anyw))
     scratch = dict(
-        g_top=pltpu.VMEM((11 * C, C), B16), sum_top=pltpu.VMEM((half, C), B16), totals=pltpu.VMEM((2,) + block, B16),
+        g_top=pltpu.VMEM((11 * C, C), B16), sum_top=pltpu.VMEM((half, C), B16),
+        sum_low=pltpu.VMEM((half, C), B16), fold=fold_seats_scratch(n, half), totals=pltpu.VMEM(block, B16),
         new_top=pltpu.VMEM((11 * C, C), B16), new_low=pltpu.VMEM((11 * C, C), B16),
         fresh=pltpu.VMEM(block, B16), pieces=pltpu.VMEM((2, half, C), B16), k=pltpu.VMEM((9 * C, C), B16),
         d3=pltpu.VMEM(tall, B16), s2=pltpu.VMEM(tall, B16), part=pltpu.VMEM((px, C), F32),
@@ -2761,7 +2870,7 @@
     mates = half // 2
     pairs = 2 * mates
     total = n * seg
-    rows = min(256, seg)
+    rows = min(256 if keep else 128, seg)
     dma = pltpu.SemaphoreType.DMA
     inputs = dict(u_in=(u, anyw), ids_all=(ids_all, vmem), vec=(vec, vmem), low=(low, anyw))
     piece = (seg, C)
@@ -2898,7 +3007,7 @@
         back = back_call(columns, n, dims, cot, du, hid, y1, norms, s1, s2, pick, spread, div, masks, vec, top, low,
                          att["dw"], att["o_home"], params.shape[0])
         new = renew_call(columns, n, dims, back["grad"], back["dh"], x, mean1, inv1, pick, spread, div, cnt, first["cnt_all"],
-                         masks, vec, top, back["g_top"], back["sum_low"], back["dvec"], att["dvec"], params, first_moment,
+                         masks, vec, top, back["g_top"], back["halves"], back["dvec"], att["dvec"], params, first_moment,
                          second_moment, att["shares"], vectors, vector_first, vector_second)
         new_vec, new_att = new["new_vec"], new["new_att"]
         o2 = attend_call(n, False, 5, new["u"].reshape(canvases, plane, channels), ids_all, new_vec, new_att)["o_home"]

time: 505 us -> 502 us (level)
  no operation moved by 1% of the time
where the time goes in v5:
time: 502 us; the launch traced here: 496 us
  Pallas kernels  489 us (97%)
  local copies, waits for them, and re-layouts  5.14 us (1%)
    pallas_call x6, Pallas kernels, named_call(): pl.pallas_call(wrapped, out_shape=[sds(shape, kind) for shape, kind, _ in...  489 us

profile of v5, /device:TPU:0, one launch (start us, length us, event | category | flops | bytes accessed | tf_op | source)
XLA Modules:
  0.0 495.7 jit_solution(14456102259069630440)
XLA Ops:
  0.6 0.7 convert_element_type.5
  1.3 0.1 reshape.57
  1.4 0.6 pad.4.refs_1_
  2.0 98.5 %first_forward.1 = (f32[16,512]{1,0:T(8,128)}, bf16[32,128]{1,0:T(8,128)(2,1)}, bf16[128,32]{1,0:T(8,128)(2,1)}, f32[8,8,512]{2,1,0:T(8,128)}, f32[128,512]{1,0:...) custom-call(bf16[1024,512]{1,0:T(8,128)(2,1)} %bitcast.14, ...), custom_call_target="tpu_custom_call" | custom-call | tf_op jit(solution)/shard_map/first_forward/pallas_call | solution.py:1955
  100.5 115.6 %attend.1 = (bf16[1024,512]{1,0:T(8,128)(2,1)}, bf16[2048,512]{1,0:T(8,128)(2,1)}, f32[8,512]{1,0:T(8,128)}, f32[2,512,512]{2,1,0:T(8,128)}, f32[3,176,512]{2,1,0:T(8,128)}) custom-call(bf16[2,512,512]{2,1,0:T(8,128)(2,1)} %bitcast.17, f32[8,8,512]{2,1,0:T(8,128)} %get-tuple-element.62.refs_1_, ...), custom_call_target="tpu_custom_call" | custom-call | tf_op jit(solution)/shard_map/attend/pallas_call | solution.py:1955
  216.1 59.2 %back.1 = (f32[1024,512]{1,0:T(8,128)}, bf16[1024,512]{1,0:T(8,128)(2,1)}, bf16[5632,512]{1,0:T(8,128)(2,1)}, f32[8,512]{1,0:T(8,128)}, bf16[4,176,512]{2,1,0:T(8,128)(2,1)}, /*index=5*/bf16[512,512]{1,0:T(8,128)(2,1)}) custom-call(f32[1024,512]{1,0:T(8,128)} %bitcast.16, f32[1024,512]{1,0:T(8,128)} %get-tuple-element.60.refs_1_.refs_0_, ...), custom_call_target="tpu_custom_call" | custom-call | tf_op jit(solution)/shard_map/back/pallas_call | solution.py:1955
  275.3 138.6 %renew.1 = (f32[1024,512]{1,0:T(8,128)}, f32[352,512]{1,0:T(8,128)}, f32[352,512]{1,0:T(8,128)}, f32[352,512]{1,0:T(8,128)}, f32[11,512]{1,0:T(8,128)}, /*index=...) custom-call(bf16[4,176,512]{2,1,0:T(8,128)(2,1)} %get-tuple-element., ...), custom_call_target="tpu_custom_call" | custom-call | tf_op jit(solution)/shard_map/renew/pallas_call | solution.py:1955
  413.9 68.7 %attend_again.1 = bf16[2,512,512]{2,1,0:T(8,128)(2,1)} custom-call(bf16[2,512,512]{2,1,0:T(8,128)(2,1)} %bitcast.18, f32[8,8,512]{2,1,0:T(8,128)} %get-tuple-element.62.refs_1_, f32[16,512]{1,0:T(8,128)} %get-tuple-element.97.refs_2_.refs_7_, bf16[2048,512]{1,0:T(8,128)(2,1)} %get-tuple-element.98.refs_3_.refs_9_), custom_call_target="tpu_custom_call" | custom-call | tf_op jit(solution)/shard_map/attend_again/pallas_call | solution.py:1955
  482.5 0.0 copy-start.2
  482.5 0.0 copy-start.1
  482.5 8.2 %outputs.1 = (f32[1024,512]{1,0:T(8,128)}, f32[1024,512]{1,0:T(8,128)}, f32[1024,512]{1,0:T(8,128)}, f32[1024,512]{1,0:T(8,128)}) custom-call(f32[1024,512]{1,0:T(8,128)} %get-tuple-element.60.refs_1_.refs_0_, f32[1024,512]{1,0:T(8,128)} %get-tuple-element.94.refs_1_, bf16[1024,512]{1,0:T(8,128)(2,1)} %get-tuple-element.78.refs_17_.refs_2_, ...), custom_call_target="tpu_custom_call" | custom-call | tf_op jit(solution)/shard_map/outputs/pallas_call | solution.py:1955
  490.8 0.0 copy-start
  490.8 0.0 copy-done.2
  490.8 0.0 copy-start.5
  490.8 0.0 copy-start.4
  490.8 0.0 copy-start.3
  490.8 0.9 copy.25
  491.7 0.0 copy-done.1
  491.7 0.9 copy.26
  492.6 0.0 copy-done
  492.6 0.9 copy.27
  493.4 0.0 copy-done.5
  493.4 0.6 copy.28
  494.0 0.0 copy-done.4
  494.0 0.6 copy.29
  494.7 0.0 copy-done.3
  494.7 0.6 copy.30
Async XLA Ops:
  482.5 8.3 %copy-start.2 = (f32[352,512]{1,0:T(8,128)S(1)}, f32[352,512]{1,0:T(8,128)}, u32[]{:S(2)}) copy-start(f32[352,512]{1,0:T(8,128)} %get-tuple-element.124) | copy-start | bytes 2162692
  482.5 9.2 %copy-start.1 = (f32[352,512]{1,0:T(8,128)S(1)}, f32[352,512]{1,0:T(8,128)}, u32[]{:S(2)}) copy-start(f32[352,512]{1,0:T(8,128)} %get-tuple-element.125) | copy-start | bytes 2162692
  490.8 1.8 copy-start
  490.8 2.6 copy-start.5
  490.8 3.2 copy-start.4
  490.8 3.8 copy-start.3

commit v6 on v5

--- a/solution.py
+++ b/solution.py
@@ -2029,7 +2029,7 @@
     R.need("x")
     layout_body(n, dims, R.x, R.pick, R.spread, R.ids_px, R.ids_lane, R.ids_all, R.mean1, R.inv1, R.div, R.cnt,
                 R.col_l, R.col_r, R.row_u, R.row_d, *R.layout, pump=pump, cnt_all=R.cnt_all)
-    for k in ("col_l", "col_r", "row_u", "row_d"):
+    for k in ("col_l", "col_r", "row_u", "row_d", "mean1", "inv1"):
         R.store(k)
     pump()
     conv = Convolver(n, dims, R.x, R.pick, R.spread, R.cnt, R.col_l, R.col_r, R.row_u, R.row_d, R.halo, R.buf,
@@ -2055,6 +2055,8 @@
     out_y1 = pltpu.make_async_copy(R.y1, R.y1_out, R.osem.at[2])
     out_y1.start()
     conv.statistics(R.y1, R.mean2, R.inv2, 0, pump_low)
+    R.store("mean2")
+    R.store("inv2")
     conv.activate(R.y1, R.mean2, R.inv2, vec[3:4, :], vec[4:5, :], R.s2, 1, pump_low)
     out_s2 = pltpu.make_async_copy(R.s2, R.s2_out, R.osem.at[3])
     out_s2.start()
@@ -2068,6 +2070,8 @@
     conv.convolve(R.s2, across(R.w_top, R.w_low), emit_second)
     R.store("hid")
     conv.statistics(R.hid, R.mean3, R.inv3, 1)
+    R.store("mean3")
+    R.store("inv3")
     conv.normalise(R.hid, R.mean3, R.inv3, vec[6:7, :], vec[7:8, :], R.u)
     for cp in conv.sent:
         cp.wait_send()
@@ -2088,7 +2092,7 @@
     half = block.shape[0] // 2
     dma = pltpu.SemaphoreType.DMA
     inputs = dict(x=(x, LOAD), ids_lane=(ids_lane, vmem), vectors=(vectors, vmem), block=(block, vmem))
-    cell = ((cells, C), F32, vmem)
+    cell = ((cells, C), F32, STORE)
     outputs = dict(
         vec=((16, C), F32, vmem), pick=((stats, cells), B16, vmem), spread=((cells, stats), B16, vmem),
         ids_all=((n,) + ids_lane.shape, F32, vmem), mean1=cell, inv1=cell, div=((stats, LANES), F32, vmem),
@@ -2263,7 +2267,7 @@
     greet_all(g)
     vec = R.vec
     back = Backer(n, dims, R)
-    R.need("du", "hid")
+    R.need("mean3", "inv3", "du", "hid")
     copies, dg3, db3 = back.norm_sums(lambda i, unit: R.du[back.pixels(i), :], R.hid, R.mean3, R.inv3, vec[6:7, :], 0)
 
     def emit_hidden(i, value):
@@ -2303,7 +2307,7 @@
     def grad_two(i, unit):
         return R.part[back.pixels(i), :] * silu_slope(unit * gain2 + bias2)
 
-    R.need("y1")
+    R.need("y1", "mean2", "inv2")
     copies, dg2, db2 = back.norm_sums(grad_two, R.y1, R.mean2, R.inv2, gain2, 1)
     engine.pump(2)
 
@@ -2344,7 +2348,7 @@
                   **{k: (v, LOAD) for k, v in zip(("col_l", "col_r", "row_u", "row_d"), masks)}, y1=(y1, LOAD), s1=(s1, anyw), s2=(s2, anyw),
                   pick=(pick, vmem), spread=(spread, vmem), div=(div, vmem), vec=(vec, vmem), top=(top, anyw),
                   bottom=(bottom, anyw), datt=(datt, anyw), o=(o, anyw),
-                  **{k: (v, vmem) for k, v in zip(names, norms)})
+                  **{k: (v, LOAD) for k, v in zip(names, norms)})
     outputs = dict(dh=((px, C), F32, STORE), grad=((px, C), B16, STORE), g_top=((11 * C, C), B16, STORE),
                    dvec=((8, C), F32, vmem), halves=((n // 2, block_rows // 2, C), B16, STORE),
                    o_back=((px // canvases, C), B16, anyw))
@@ -2393,7 +2397,7 @@
     up, down = back.send_rows(R.grad, 0)
     folder.pump()
     reducer.pump(2)
-    R.need("x")
+    R.need("x", "mean1", "inv1")
     for cp in loads:
         cp.wait()
 
@@ -2536,10 +2540,10 @@
     seats, phases = n // 2, columns.bit_length() - 1
     dma = pltpu.SemaphoreType.DMA
     tall = (canvases, rows + 2, width, 3 * C)
-    arrays = dict(mean1=mean1, inv1=inv1, pick=pick, spread=spread, div=div, cnt=cnt, cnt_all=cnt_all, vec=vec,
+    arrays = dict(pick=pick, spread=spread, div=div, cnt=cnt, cnt_all=cnt_all, vec=vec,
                   dvec=dvec, dvec_att=dvec_att, vw=vw, vm=vm, vs=vs)
     inputs = dict(halves=(halves, LOAD), grad=(grad, LOAD),
-                  **{k: (a, LOAD) for k, a in zip(("col_l", "col_r", "row_u", "row_d"), masks)}, x=(x, LOAD),
+                  **{k: (a, LOAD) for k, a in zip(("col_l", "col_r", "row_u", "row_d"), masks)}, x=(x, LOAD), mean1=(mean1, LOAD), inv1=(inv1, LOAD),
                   top=(top, anyw), g_in=(g_top, anyw), w=(w, anyw), m=(m, anyw), v=(v, anyw), shares=(shares, anyw), dh=(dh, anyw),
                   **{k: (a, vmem) for k, a in arrays.items()})
     outputs = dict(igrad=((px, C), F32, STORE), new_w=(block, F32, STORE), new_m=(block, F32, STORE),
@@ -2752,18 +2756,22 @@
     zero = jnp.zeros((C, C), F32)
     pairs = 2 * mates
 
-    def du_of(b, carry):
-        dwk, dwv, dbv = carry
+    def du_of(b):
         at = block(b)
         dk = (lax.dot_general(R.sbuf[:, at], R.q[...], tn, preferred_element_type=F32) * scale).astype(B16)
         dvf = lax.dot_general(R.pbuf[:, at], R.dout[...], tn, preferred_element_type=F32)
         dv = dvf.astype(B16)
         du = lax.dot_general(dk, R.w[C : 2 * C, :], nt, preferred_element_type=F32)
         du = du + lax.dot_general(dv, R.w[2 * C : 3 * C, :], nt, preferred_element_type=F32)
+        return du, (b, dk, dv, jnp.sum(dvf, axis=0, keepdims=True))
+
+    def weigh(found, carry):
+        b, dk, dv, total = found
+        dwk, dwv, dbv = carry
         piece = R.u[b]
         dwk = dwk + lax.dot_general(piece, dk, tn, preferred_element_type=F32)
         dwv = dwv + lax.dot_general(piece, dv, tn, preferred_element_type=F32)
-        return du, (dwk, dwv, dbv + jnp.sum(dvf, axis=0, keepdims=True))
+        return dwk, dwv, dbv + total
 
     def place(t):
         far = 1 - t // mates
@@ -2801,10 +2809,11 @@
     def back(t, carry):
         j, far = place(t)
         theirs, ours = mate(j, 1 - core), mate(j)
-        du, carry = du_of(lax.rem(theirs + far * half, n), carry)
+        du, found = du_of(lax.rem(theirs + far * half, n))
         R.for_sib[t] = du.astype(B16)
         sib_copy(t).start()
-        du, carry = du_of(lax.rem(ours + far * half, n), carry)
+        carry = weigh(found, carry)
+        du, found = du_of(lax.rem(ours + far * half, n))
         sib_copy(t).wait_recv()
         R.sums[t] = (du + R.from_sib[t].astype(F32)).astype(B16)
 
@@ -2817,12 +2826,13 @@
         def _():
             send_home(0)
 
-        return carry
+        return weigh(found, carry)
 
     dwk, dwv, dbv = lax.fori_loop(0, pairs, back, (zero, zero, jnp.zeros((1, C), F32)))
     send_home(1)
     for part in range(2):
         R.du[mine, pl.ds(part * (seg // 2), seg // 2), :] = gathered(0, part)
+    R.store("du", mine, 1)
     R.dw[C : 2 * C, :] = dwk.astype(B16)
     R.dw[2 * C : 3 * C, :] = dwv.astype(B16)
     R.dw[3 * C : 4 * C, :] = lax.dot_general(
@@ -2843,6 +2853,7 @@
     for part in range(2):
         home_copy(part).wait()
     R.du[1 - mine] = R.from_partner[...].astype(F32)
+    R.store("du", 1 - mine, 1)
     for move in moves:
         share(*move, False)
     all_out.wait()
@@ -2882,7 +2893,7 @@
     if keep:
         inputs.update(cot=(cot, anyw), **{k: (a, anyw) for k, a in zip(("params", "first", "second"), state)})
         outputs = dict(o_home=((2 * seg, C), B16, anyw), dw=((4 * C, C), B16, STORE), dvec=((8, C), F32, vmem),
-                       du=(home, F32, vmem), shares=((3, state[0].shape[0] // 2, C), F32, anyw))
+                       du=(home, F32, STORE), shares=((3, state[0].shape[0] // 2, C), F32, anyw))
         scratch.update(
             csend=dma((seg // rows,)), crecv=dma((seg // rows,)), dz=pltpu.VMEM((2 * seg, C), B16), dout=pltpu.VMEM((2 * seg, C), B16), q=pltpu.VMEM((2 * seg, C), B16),
             dq=pltpu.VMEM((2 * seg, C), B16), pbuf=pltpu.VMEM((2 * seg, total), B16),

time: 502 us -> 503 us (level)
  no operation moved by 1% of the time
where the time goes in v6:
time: 503 us; the launch traced here: 497 us
  Pallas kernels  490 us (97%)
  local copies, waits for them, and re-layouts  5.14 us (1%)
    pallas_call x6, Pallas kernels, named_call(): pl.pallas_call(wrapped, out_shape=[sds(shape, kind) for shape, kind, _ in...  490 us

profile of v6, /device:TPU:0, one launch (start us, length us, event | category | flops | bytes accessed | tf_op | source)
XLA Modules:
  0.0 496.9 jit_solution(13334645257753649565)
XLA Ops:
  0.6 0.7 convert_element_type.5
  1.3 0.1 reshape.57
  1.4 0.6 pad.4.refs_1_
  2.0 98.6 %first_forward.1 = (f32[16,512]{1,0:T(8,128)}, bf16[32,128]{1,0:T(8,128)(2,1)}, bf16[128,32]{1,0:T(8,128)(2,1)}, f32[8,8,512]{2,1,0:T(8,128)}, f32[128,512]{1,0:...) custom-call(bf16[1024,512]{1,0:T(8,128)(2,1)} %bitcast.14, ...), custom_call_target="tpu_custom_call" | custom-call | tf_op jit(solution)/shard_map/first_forward/pallas_call | solution.py:1955
  100.6 115.2 %attend.1 = (bf16[1024,512]{1,0:T(8,128)(2,1)}, bf16[2048,512]{1,0:T(8,128)(2,1)}, f32[8,512]{1,0:T(8,128)}, f32[2,512,512]{2,1,0:T(8,128)}, f32[3,176,512]{2,1,0:T(8,128)}) custom-call(bf16[2,512,512]{2,1,0:T(8,128)(2,1)} %bitcast.17, f32[8,8,512]{2,1,0:T(8,128)} %get-tuple-element.62.refs_1_, ...), custom_call_target="tpu_custom_call" | custom-call | tf_op jit(solution)/shard_map/attend/pallas_call | solution.py:1955
  215.8 60.8 %back.1 = (f32[1024,512]{1,0:T(8,128)}, bf16[1024,512]{1,0:T(8,128)(2,1)}, bf16[5632,512]{1,0:T(8,128)(2,1)}, f32[8,512]{1,0:T(8,128)}, bf16[4,176,512]{2,1,0:T(8,128)(2,1)}, /*index=5*/bf16[512,512]{1,0:T(8,128)(2,1)}) custom-call(f32[1024,512]{1,0:T(8,128)} %bitcast.16, f32[1024,512]{1,0:T(8,128)} %get-tuple-element.60.refs_1_.refs_0_, ...), custom_call_target="tpu_custom_call" | custom-call | tf_op jit(solution)/shard_map/back/pallas_call | solution.py:1955
  276.6 138.4 %renew.1 = (f32[1024,512]{1,0:T(8,128)}, f32[352,512]{1,0:T(8,128)}, f32[352,512]{1,0:T(8,128)}, f32[352,512]{1,0:T(8,128)}, f32[11,512]{1,0:T(8,128)}, /*index=...) custom-call(bf16[4,176,512]{2,1,0:T(8,128)(2,1)} %get-tuple-element., ...), custom_call_target="tpu_custom_call" | custom-call | tf_op jit(solution)/shard_map/renew/pallas_call | solution.py:1955
  415.0 68.7 %attend_again.1 = bf16[2,512,512]{2,1,0:T(8,128)(2,1)} custom-call(bf16[2,512,512]{2,1,0:T(8,128)(2,1)} %bitcast.18, f32[8,8,512]{2,1,0:T(8,128)} %get-tuple-element.62.refs_1_, f32[16,512]{1,0:T(8,128)} %get-tuple-element.97.refs_2_.refs_7_, bf16[2048,512]{1,0:T(8,128)(2,1)} %get-tuple-element.98.refs_3_.refs_9_), custom_call_target="tpu_custom_call" | custom-call | tf_op jit(solution)/shard_map/attend_again/pallas_call | solution.py:1955
  483.7 0.0 copy-start.2
  483.7 0.0 copy-start.1
  483.7 8.2 %outputs.1 = (f32[1024,512]{1,0:T(8,128)}, f32[1024,512]{1,0:T(8,128)}, f32[1024,512]{1,0:T(8,128)}, f32[1024,512]{1,0:T(8,128)}) custom-call(f32[1024,512]{1,0:T(8,128)} %get-tuple-element.60.refs_1_.refs_0_, f32[1024,512]{1,0:T(8,128)} %get-tuple-element.94.refs_1_, bf16[1024,512]{1,0:T(8,128)(2,1)} %get-tuple-element.78.refs_17_.refs_2_, ...), custom_call_target="tpu_custom_call" | custom-call | tf_op jit(solution)/shard_map/outputs/pallas_call | solution.py:1955
  492.0 0.0 copy-start
  492.0 0.0 copy-done.2
  492.0 0.0 copy-start.5
  492.0 0.0 copy-start.4
  492.0 0.0 copy-start.3
  492.0 0.9 copy.25
  492.9 0.0 copy-done.1
  492.9 0.9 copy.26
  493.7 0.0 copy-done
  493.7 0.9 copy.27
  494.6 0.0 copy-done.5
  494.6 0.6 copy.28
  495.2 0.0 copy-done.4
  495.2 0.6 copy.29
  495.8 0.0 copy-done.3
  495.8 0.6 copy.30
Async XLA Ops:
  483.7 8.3 %copy-start.2 = (f32[352,512]{1,0:T(8,128)S(1)}, f32[352,512]{1,0:T(8,128)}, u32[]{:S(2)}) copy-start(f32[352,512]{1,0:T(8,128)} %get-tuple-element.124) | copy-start | bytes 2162692
  483.7 9.2 %copy-start.1 = (f32[352,512]{1,0:T(8,128)S(1)}, f32[352,512]{1,0:T(8,128)}, u32[]{:S(2)}) copy-start(f32[352,512]{1,0:T(8,128)} %get-tuple-element.125) | copy-start | bytes 2162692
  492.0 1.8 copy-start
  492.0 2.6 copy-start.5
  492.0 3.2 copy-start.4
  492.0 3.8 copy-start.3
